TPU v7x, 32 devices: a whole 2x2x4 slice. The times are simulated.
32 devices in a mesh: group: 2 (over x), dp: 16 (over z, y, core).
Axes of the slice: x: 2, y: 2, z: 4, core: 2. Of those that a mesh axis runs over, the one named last changes fastest.
Arguments:
- features: bfloat16 [4096, 24576], P(('group', 'dp')), parts along dimension 0, may hold values from -120 to 120, as said below
- joining_gains: float32 [3, 8192], replicated, may hold values from 0.5 to 1.5
- destination: int32 [4096, 1], P(('group', 'dp')), parts along dimension 0, may hold values from 0 to 15; in each aligned block of 128 rows (0 to 127, 128 to 255, ...) at most 12 rows name the same one
- target_logits: bfloat16 [4096, 128], P(('group', 'dp')), parts along dimension 0, may hold values from -20 to 260, as said below
- joined_cotangent: bfloat16 [6144, 8192], P(('group', 'dp')), parts along dimension 0, may hold values from -0.4375 to 0.4375
Outputs:
- joined_input: bfloat16 [6144, 8192], P(('group', 'dp')), parts along dimension 0
- soft_labels: bfloat16 [6144, 128], P(('group', 'dp')), parts along dimension 0
- log_partition: float32 [6144], P(('group', 'dp')), parts along dimension 0
- gain_grad: float32 [6, 8192], P('group', 'dp'), parts along dimension 0
There are 2 independent parts, one for each index of `group`. A program takes and returns all parts, laid end to end along the dimension named above; an argument that names none is the same for every part. Nothing has to cross between parts.
Inputs may be any that keep to these rules, and one draw needn't show every extreme that they name: `destination`: at most 12 tokens of one feature device name the same trainer; in every draw some feature device sends exactly 12 tokens to one trainer. `features`: Real-valued hidden states; rows and channels have unlike scales. `target_logits`: Real-valued logits.
All inputs are finite; a program needn't handle non-finite values.
Results may differ from a plain program's by a relative error of at most 0.001.
Values may be sent and summed in bfloat16 or wider, within the bound.
No kernel may reach another device: no remote copies, remote signals or barrier semaphores. Data moves between devices by JAX's collectives and lax.ppermute only.
A program may use at most 256 MiB of HBM per device.

v0:
```python
import jax
import jax.numpy as jnp
from jax import lax
from jax.sharding import PartitionSpec as P

eps = 1e-06


def normalize(row_block, joining_gains):
    layers, feature_width = joining_gains.shape
    widened = row_block.astype(jnp.float32).reshape(row_block.shape[0], layers, feature_width)
    scaled = widened * lax.rsqrt(jnp.mean(widened * widened, axis=2, keepdims=True) + eps)
    joined_vals = jnp.sum(scaled * joining_gains[None], axis=1)
    return (scaled, joined_vals)


def per_device(features, joining_gains, destination, target_logits, joined_cotangent):
    groups = lax.axis_size("dp")
    capacity = joined_cotangent.shape[0] // groups
    slot_total = groups * capacity
    feature_width = joining_gains.shape[1]
    target = destination[:, 0]
    onehot = (target[:, None] == jnp.arange(groups, dtype=jnp.int32)[None, :]).astype(jnp.int32)
    before = jnp.cumsum(onehot, axis=0) - onehot
    position = target * capacity + jnp.sum(before * onehot, axis=1)
    logit_send = (
        jnp.zeros((slot_total, target_logits.shape[1]), jnp.bfloat16)
        .at[position]
        .set(target_logits)
    )
    scaled, joined_vals = normalize(features, joining_gains)
    joined_send = (
        jnp.zeros((slot_total, feature_width), jnp.bfloat16)
        .at[position]
        .set(joined_vals.astype(jnp.bfloat16))
    )
    joined_input, logit_slots = (
        lax.all_to_all(joined_send, "dp", split_axis=0, concat_axis=0, tiled=True),
        lax.all_to_all(logit_send, "dp", split_axis=0, concat_axis=0, tiled=True),
    )
    returned = lax.all_to_all(joined_cotangent, "dp", split_axis=0, concat_axis=0, tiled=True)
    row_cot = returned[position].astype(jnp.float32)
    partial_value = jnp.sum(scaled * row_cot[:, None, :], axis=0)
    gain_grad = lax.psum_scatter(partial_value, "dp", scatter_dimension=1, tiled=True)
    logit_values = logit_slots.astype(jnp.float32)
    row_max = jnp.max(logit_values, axis=1, keepdims=True)
    log_partition = row_max[:, 0] + jnp.log(jnp.sum(jnp.exp(logit_values - row_max), axis=1))
    soft_labels = jnp.exp(logit_values - log_partition[:, None]).astype(jnp.bfloat16)
    return (joined_input, soft_labels, log_partition, gain_grad)


def solution(mesh):
    placed = (
        P(("group", "dp"), None),
        P(),
        P(("group", "dp"), None),
        P(("group", "dp"), None),
        P(("group", "dp"), None),
    )
    return jax.shard_map(
        per_device,
        mesh=mesh,
        in_specs=placed,
        out_specs=(
            P(("group", "dp"), None),
            P(("group", "dp"), None),
            P(("group", "dp")),
            P("group", "dp"),
        ),
        check_vma=False,
    )
```

profile of v0, /device:TPU:13, one launch (start us, length us, event | category | flops | bytes accessed | tf_op | source)
XLA Modules:
  0.0 257.5 jit_solution(8420930831890253040)
XLA Ops:
  7.2 0.7 fusion.3
  7.9 0.2 reduce_window_sum.11
  8.1 0.8 select_reduce_fusion
  8.9 0.7 fusion.6
  9.6 1.1 scatter_custom_fusion.1
  10.7 0.6 all_to_all.25
  11.3 6.6 %all-to-all-start.1 = ((bf16[16,12,128]{2,1,0:T(8,128)(2,1)}), bf16[16,12,128]{2,1,0:T(8,128)(2,1)S(1)}, u32[]{:S(2)}, u32[]{:S(2)}) async-start(bf16[16,12,128]{2,1,0:T(8,128)(2,1)} %all_to_all.25), calls=%async_computation.1 | async-start | bytes 131072 | tf_op jit(solution)/shard_map/all_to_all | solution.py:39
  17.9 4.7 %all_to_all.27 = bf16[16,12,8192]{2,1,0:T(8,128)(2,1)} reshape(bf16[192,8192]{1,0:T(8,128)(2,1)} %param.9) | data formatting | bytes 6291456 | tf_op jit(solution)/shard_map/all_to_all | solution.py:41
  22.6 0.0 all-to-all-done.1
  22.6 6.6 %all-to-all-start.2 = ((bf16[16,12,8192]{2,1,0:T(8,128)(2,1)}), bf16[16,12,8192]{2,1,0:T(8,128)(2,1)}, u32[]{:S(2)}, u32[]{:S(2)}) async-start(bf16[16,12,8192]{2,1,0:T(8,128)(2,1)} %all_to_all.27), calls=%async_computation.2 | async-start | bytes 8388608 | tf_op jit(solution)/shard_map/all_to_all | solution.py:41
  29.2 8.7 %copy.13 = bf16[128,24576]{0,1:T(8,128)(2,1)} copy(bf16[128,24576]{1,0:T(8,128)(2,1)} %param.5) | data formatting | bytes 12582912 | tf_op args[0]
  37.9 0.0 copy-start
  37.9 4.0 %multiply_reduce_fusion.1 = (f32[128,3]{0,1:T(4,128)S(1)}, f32[128,3,8192]{0,2,1:T(8,128)S(1)}) fusion(bf16[128,3,8192]{0,2,1:T(8,128)(2,1)} %bitcast.19), kind=kLoop, calls=%fused_computation.7 | loop fusion | flops 9436800 | bytes 18875904 | tf_op jit(solution)/shard_map/reduce_sum | solution.py:12
  41.9 0.0 copy-done
  41.9 4.4 %multiply_reduce_fusion = bf16[128,8192]{0,1:T(8,128)(2,1)S(1)} fusion(f32[128,3,8192]{0,2,1:T(8,128)S(1)} %get-tuple-element.5, f32[3,8192]{1,0:T(4,128)S(1)} %copy-done, f32[128,3]{0,1:T(4,128)S(1)} %add_rsqrt_fusion), kind=kLoop, calls=%fused_computation.6 | loop fusion | flops 8388608 | bytes 14779904 | tf_op jit(solution)/shard_map/reduce_sum | solution.py:13
  46.4 2.9 %copy.14 = bf16[128,8192]{1,0:T(8,128)(2,1)} copy(bf16[128,8192]{0,1:T(8,128)(2,1)S(1)} %multiply_reduce_fusion) | data formatting | bytes 4194304 | tf_op jit(solution)/shard_map/convert_element_type | solution.py:35
  49.2 5.4 %scatter_custom_fusion = bf16[192,8192]{1,0:T(8,128)(2,1)S(1)} fusion(s32[128]{0:T(128)S(1)} %fusion.6, bf16[128,8192]{1,0:T(8,128)(2,1)} %copy.14, bf16[]{:T(256)} %constant.8.clone.1), kind=kCustom, calls=%fused_computation.8 | custom fusion | bytes 3146240 | tf_op jit(solution)/shard_map/scatter | solution.py:35
  54.7 2.8 %all_to_all.22 = bf16[16,12,8192]{2,1,0:T(8,128)(2,1)} reshape(bf16[192,8192]{1,0:T(8,128)(2,1)S(1)} %scatter_custom_fusion) | data formatting | bytes 6291456 | tf_op jit(solution)/shard_map/all_to_all | solution.py:38
  57.5 64.2 %all-to-all-done.2 = bf16[16,12,8192]{2,1,0:T(8,128)(2,1)} async-done(((bf16[16,12,8192]{2,1,0:T(8,128)(2,1)}), bf16[16,12,8192]{2,1,0:T(8,128)(2,1)}, u32[]{:S(2)}, u32[]{:S(2)}) %all-to-all-start.2) | async-done | bytes 3145760 | tf_op jit(solution)/shard_map/all_to_all | solution.py:41
  121.7 4.9 %all-to-all-start = ((bf16[16,12,8192]{2,1,0:T(8,128)(2,1)}), bf16[16,12,8192]{2,1,0:T(8,128)(2,1)}, u32[]{:S(2)}, u32[]{:S(2)}) async-start(bf16[16,12,8192]{2,1,0:T(8,128)(2,1)} %all_to_all.22), calls=%async_computation | async-start | bytes 8388608 | tf_op jit(solution)/shard_map/all_to_all | solution.py:38
  126.6 0.2 reduce-scatter.4.cloned.1.call-start
  126.8 0.1 reduce_max.14
  126.9 0.2 exponential_reduce_fusion
  127.2 0.1 add.38
  127.2 0.0 copy-start.1
  127.3 3.2 %all_to_all.29 = bf16[192,8192]{1,0:T(8,128)(2,1)S(1)} reshape(bf16[16,12,8192]{2,1,0:T(8,128)(2,1)} %all-to-all-done.2) | data formatting | bytes 6291456 | tf_op jit(solution)/shard_map/all_to_all | solution.py:41
  130.5 3.2 %gather_fusion = bf16[128,8192]{1,0:T(8,128)(2,1)} fusion(bf16[192,8192]{1,0:T(8,128)(2,1)S(1)} %all_to_all.29, s32[1024]{0:T(1024)S(1)} %pad_clamp_fusion), kind=kCustom, calls=%fused_computation | custom fusion | bytes 4194816 | tf_op jit(solution)/shard_map/gather | solution.py:42
  133.7 4.3 %copy.15 = f32[128,8192]{0,1:T(8,128)} copy(bf16[128,8192]{1,0:T(8,128)(2,1)} %gather_fusion) | data formatting | bytes 6291456 | tf_op jit(solution)/shard_map/convert_element_type | solution.py:42
  138.1 6.8 %fusion = f32[24576]{0:T(1024)S(1)} fusion(f32[128,8192]{0,1:T(8,128)} %copy.15, f32[128,3]{0,1:T(4,128)S(1)} %add_rsqrt_fusion, bf16[128,24576]{0,1:T(8,128)(2,1)} %copy.13), kind=kLoop, calls=%fused_computation.4 | loop fusion | flops 12558336 | bytes 10585600 | tf_op jit(solution)/shard_map/reduce_sum | solution.py:43
  144.9 2.6 %copy.16 = f32[3,8192]{0,1:T(8,128)} copy(f32[3,8192]{1,0:T(4,128)S(1)} %reduce_sum.55) | data formatting | bytes 196608
  147.5 0.0 reduce-scatter.4.cloned.1.call-update
  147.5 0.0 copy-done.1
  147.5 0.7 exponential_convert_fusion
  148.3 96.1 %all-to-all-done = bf16[16,12,8192]{2,1,0:T(8,128)(2,1)} async-done(((bf16[16,12,8192]{2,1,0:T(8,128)(2,1)}), bf16[16,12,8192]{2,1,0:T(8,128)(2,1)}, u32[]{:S(2)}, u32[]{:S(2)}) %all-to-all-start) | async-done | bytes 3145760 | tf_op jit(solution)/shard_map/all_to_all | solution.py:38
  244.3 4.7 %all_to_all.24 = bf16[192,8192]{1,0:T(8,128)(2,1)} reshape(bf16[16,12,8192]{2,1,0:T(8,128)(2,1)} %all-to-all-done) | data formatting | bytes 6291456 | tf_op jit(solution)/shard_map/all_to_all | solution.py:38
  249.0 0.0 reduce-scatter.4.cloned.1.call-done
  249.0 1.7 copy.17
  (6 shorter events, 0.1 us)
Async XLA Ops:
  11.3 11.2 %all-to-all-start.1 = ((bf16[16,12,128]{2,1,0:T(8,128)(2,1)}), bf16[16,12,128]{2,1,0:T(8,128)(2,1)S(1)}, u32[]{:S(2)}, u32[]{:S(2)}) async-start(bf16[16,12,128]{2,1,0:T(8,128)(2,1)} %all_to_all.25), calls=%async_computation.1 | async-start | bytes 131072 | tf_op jit(solution)/shard_map/all_to_all | solution.py:39
  22.6 99.1 %all-to-all-start.2 = ((bf16[16,12,8192]{2,1,0:T(8,128)(2,1)}), bf16[16,12,8192]{2,1,0:T(8,128)(2,1)}, u32[]{:S(2)}, u32[]{:S(2)}) async-start(bf16[16,12,8192]{2,1,0:T(8,128)(2,1)} %all_to_all.27), calls=%async_computation.2 | async-start | bytes 8388608 | tf_op jit(solution)/shard_map/all_to_all | solution.py:41
  37.9 4.1 %copy-start = (f32[3,8192]{1,0:T(4,128)S(1)}, f32[3,8192]{1,0:T(4,128)}, u32[]{:S(2)}) copy-start(f32[3,8192]{1,0:T(4,128)} %param.6) | copy-start | bytes 294916
  121.7 122.7 %all-to-all-start = ((bf16[16,12,8192]{2,1,0:T(8,128)(2,1)}), bf16[16,12,8192]{2,1,0:T(8,128)(2,1)}, u32[]{:S(2)}, u32[]{:S(2)}) async-start(bf16[16,12,8192]{2,1,0:T(8,128)(2,1)} %all_to_all.22), calls=%async_computation | async-start | bytes 8388608 | tf_op jit(solution)/shard_map/all_to_all | solution.py:38
  126.6 122.5 %reduce-scatter.4.cloned.1.call-start = ((), (), s32[]{:S(2)}) async-start(), calls=%async_computation.4 | async-start | bytes 4456448
  127.2 20.3 %copy-start.1 = (f32[192]{0:T(256)}, f32[192]{0:T(256)S(1)}, u32[]{:S(2)}) copy-start(f32[192]{0:T(256)S(1)} %add.38) | copy-start | bytes 2308
Sparse Core Ops, SparseCore 0:
  147.6 94.7 reduce-scatter.3
where the time goes:
time: 259 us; the launch traced here: 258 us
  waiting for transfers between devices  160 us (62%)
  local copies, waits for them, and re-layouts  46.1 us (18%)
  other arithmetic  18.7 us (7%)
  starting transfers between devices  18.3 us (7%)
  between operations  14.2 us (5%)
    all_to_all x1, waiting for transfers between devices, per_device(): lax.all_to_all(joined_send, 'dp', split_axis=0, concat_axis=0, tiled=True)  96.1 us
    all_to_all x1, waiting for transfers between devices, per_device(): lax.all_to_all(joined_cotangent, 'dp', split_axis=0, concat_axis=0, tiled...  64.2 us
    unnamed x7, local copies, waits for them, and re-layouts  13 us
    all_to_all x2, local copies, waits for them, and re-layouts, per_device(): lax.all_to_all(joined_cotangent, 'dp', split_axis=0, concat_axis=0, tiled...  7.91 us
    all_to_all x2, local copies, waits for them, and re-layouts, per_device(): lax.all_to_all(joined_send, 'dp', split_axis=0, concat_axis=0, tiled=True)  7.48 us
    reduce_sum x1, other arithmetic, per_device(): partial_value = jnp.sum(scaled * row_cot[:, None, :], axis=0)  6.75 us
    all_to_all x1, starting transfers between devices, per_device(): lax.all_to_all(joined_cotangent, 'dp', split_axis=0, concat_axis=0, tiled...  6.64 us
    all_to_all x1, starting transfers between devices, per_device(): lax.all_to_all(logit_send, 'dp', split_axis=0, concat_axis=0, tiled=True)  6.55 us
  transfers between devices with their start and end apart: 4, of which 2 were waited for; matrix products, arithmetic and copies ran while one was open for 17% of the time, Pallas kernels for 0%

commit v1 on v0

v1 whole, which is shorter than its diff:
```python
import functools

import jax
import jax.numpy as jnp
from jax import lax
from jax.experimental import pallas as pl
from jax.experimental.pallas import tpu as pltpu
from jax.sharding import PartitionSpec as P

eps = 1e-06
SUB = 8
GROUP = 1024
LANES = 128
VMEM_LIMIT = 40 * 1024 * 1024


def pieces_of(capacity):
    found, first = [], 0
    for size in (8, 4, 2, 1):
        while capacity - first >= size:
            found.append((first, size, SUB // size))
            first += size
    return found


def iota(shape, dim):
    return lax.broadcasted_iota(jnp.int32, shape, dim)


def ranks_of(dest_row):
    tokens = dest_row.shape[1]
    across = jnp.broadcast_to(dest_row.astype(jnp.float32), (tokens, tokens))
    down = across.T
    same = across == down
    row, col = iota((tokens, tokens), 0), iota((tokens, tokens), 1)
    rank_row = jnp.sum(jnp.where(same & (row < col), 1.0, 0.0), axis=0, keepdims=True).astype(jnp.int32)
    rank_col = jnp.sum(jnp.where(same & (col < row), 1.0, 0.0), axis=1, keepdims=True).astype(jnp.int32)
    return dest_row, rank_row, down[:, :1].astype(jnp.int32), rank_col


def spread(target, rank, first, size, h):
    inside = (rank >= first) & (rank < first + size)
    return jnp.where(inside, target * SUB + h * size + rank - first, -1)


def hot(cond):
    return jnp.where(cond, 1.0, 0.0).astype(jnp.bfloat16)


def select(matrix, values):
    return jnp.dot(matrix, values, preferred_element_type=jnp.float32).astype(jnp.bfloat16)


def pack_matrices(target, rank, groups, capacity):
    shape = (groups * SUB, target.shape[1])
    out = []
    for first, size, splits in pieces_of(capacity):
        parts = [hot(iota(shape, 0) == spread(target, rank, first, size, h)) for h in range(splits)]
        out.append(parts[0] if splits == 1 else jnp.concatenate(parts, axis=1))
    return out


def pack_group(values, matrices, capacity):
    out = []
    for (_, _, splits), matrix in zip(pieces_of(capacity), matrices):
        wide = values.shape[1] // splits
        stacked = values if splits == 1 else jnp.concatenate([values[:, h * wide : (h + 1) * wide] for h in range(splits)], axis=0)
        out.append(select(matrix, stacked))
    return out


def unpack_matrices(target, rank, groups, capacity):
    shape = (target.shape[0], groups * SUB)
    runs = pieces_of(capacity)
    finest = max(splits for _, _, splits in runs)
    out = []
    for b in range(finest):
        parts = [hot(iota(shape, 1) == spread(target, rank, first, size, b * splits // finest)) for first, size, splits in runs]
        out.append(jnp.concatenate(parts, axis=1))
    return out


def unpack_group(packed, matrices, capacity, group):
    runs = pieces_of(capacity)
    finest = max(splits for _, _, splits in runs)
    wide = group // finest
    out = []
    for b in range(finest):
        parts, base = [], 0
        for _, _, splits in runs:
            own = group // splits
            at = base + b * wide - (b * splits // finest) * own
            parts.append(packed[:, at : at + wide])
            base += own
        out.append(jnp.dot(matrices[b], jnp.concatenate(parts, axis=0), preferred_element_type=jnp.float32))
    return out


def cols(ref, g, wide):
    return ref.at[:, g * wide : (g + 1) * wide]


def cot_kernel(groups, capacity, dest_ref, logit_ref, cot_hbm, out_hbm, cot_v, out_v, log_v, in_sem, out_sem, log_sem):
    count, slots, group = cot_v.shape
    packed = out_v.shape[2]
    loads = [pltpu.make_async_copy(cols(cot_hbm, g, group), cot_v.at[g], in_sem.at[g]) for g in range(count)]
    stores = [pltpu.make_async_copy(out_v.at[g], cols(out_hbm, g, packed), out_sem.at[g]) for g in range(count)]
    for load in loads:
        load.start()
    target, rank, _, _ = ranks_of(dest_ref[...])
    shape = (groups * SUB, target.shape[1])
    for m in range(log_v.shape[1] // LANES):
        place = hot(iota(shape, 0) == spread(target, rank, m * SUB, SUB, 0))
        log_v[:, m * LANES : (m + 1) * LANES] = select(place, logit_ref[...])
    log_store = pltpu.make_async_copy(log_v, out_hbm.at[:, count * packed : count * packed + log_v.shape[1]], log_sem)
    log_store.start()
    slot = iota((1, slots), 1)
    matrices = pack_matrices(slot // capacity, slot % capacity, groups, capacity)
    for g in range(count):
        loads[g].wait()
        base = 0
        for block in pack_group(cot_v[g], matrices, capacity):
            out_v[g, :, base : base + block.shape[1]] = block
            base += block.shape[1]
        stores[g].start()
    for store in stores:
        store.wait()
    log_store.wait()


def join_kernel(groups, capacity, dest_ref, gain_ref, feat_hbm, out_hbm, inv_ref, feat_v, out_v, in_sem, out_sem):
    layers, count, tokens, group = feat_v.shape
    width = count * group
    packed = out_v.shape[2]
    loads = [
        [pltpu.make_async_copy(cols(feat_hbm, l * count + g, group), feat_v.at[l, g], in_sem.at[l, g]) for g in range(count)]
        for l in range(layers)
    ]
    stores = [pltpu.make_async_copy(out_v.at[g], cols(out_hbm, g, packed), out_sem.at[g]) for g in range(count)]
    for row in loads:
        for load in row:
            load.start()
    target, rank, _, _ = ranks_of(dest_ref[...])
    matrices = pack_matrices(target, rank, groups, capacity)
    lane = iota((tokens, LANES), 1)
    inv_all = jnp.zeros((tokens, LANES), jnp.float32)
    inverse = []
    for l in range(layers):
        total = jnp.zeros((tokens, LANES), jnp.float32)
        for g in range(count):
            loads[l][g].wait()
            for k in range(group // LANES):
                x = feat_v[l, g, :, k * LANES : (k + 1) * LANES].astype(jnp.float32)
                total = total + x * x
        mean = jnp.sum(total, axis=1, keepdims=True) / width
        inv = lax.rsqrt(mean + eps)
        inverse.append(inv)
        inv_all = jnp.where(lane == l, inv, inv_all)
    inv_ref[...] = inv_all
    for g in range(count):
        joined = None
        for l in range(layers):
            term = feat_v[l, g].astype(jnp.float32) * inverse[l] * gain_ref[l : l + 1, g * group : (g + 1) * group]
            joined = term if joined is None else joined + term
        base = 0
        for block in pack_group(joined.astype(jnp.bfloat16), matrices, capacity):
            out_v[g, :, base : base + block.shape[1]] = block
            base += block.shape[1]
        stores[g].start()
    for store in stores:
        store.wait()


def grad_kernel(
    groups, capacity, dest_ref, inv_ref, feat_hbm, got_hbm, grad_ref, soft_ref, part_ref, feat_v, got_v, log_v, in_sem, got_sem, log_sem
):
    layers, count, tokens, group = feat_v.shape
    packed = got_v.shape[2]
    own = grad_ref.shape[1] // layers
    log_load = pltpu.make_async_copy(got_hbm.at[:, count * packed : count * packed + log_v.shape[1]], log_v, log_sem)
    log_load.start()
    gots = [pltpu.make_async_copy(cols(got_hbm, g, packed), got_v.at[g], got_sem.at[g]) for g in range(count)]
    loads = [
        [pltpu.make_async_copy(cols(feat_hbm, l * count + g, group), feat_v.at[l, g], in_sem.at[l, g]) for g in range(count)]
        for l in range(layers)
    ]
    for g in range(count):
        gots[g].start()
        for l in range(layers):
            loads[l][g].start()
    _, _, target, rank = ranks_of(dest_ref[...])
    matrices = unpack_matrices(target, rank, groups, capacity)
    for g in range(count):
        gots[g].wait()
        for l in range(layers):
            loads[l][g].wait()
        blocks = unpack_group(got_v[g], matrices, capacity, group)
        wide = group // len(blocks)
        for b, cot in enumerate(blocks):
            step = min(own, wide)
            for l in range(layers):
                x = feat_v[l, g, :, b * wide : (b + 1) * wide].astype(jnp.float32)
                part = jnp.sum(x * inv_ref[:, l : l + 1] * cot, axis=0, keepdims=True)
                for u in range(wide // step):
                    at = g * group + b * wide + u * step
                    lo = l * own + at % own
                    grad_ref[at // own : at // own + 1, lo : lo + step] = part[:, u * step : (u + 1) * step]
    log_load.wait()
    slots = soft_ref.shape[0]
    slot = iota((slots, 1), 0)
    target, rank = slot // capacity, slot % capacity
    shape = (slots, groups * SUB)
    logits = jnp.zeros((slots, LANES), jnp.float32)
    for m in range(log_v.shape[1] // LANES):
        place = hot(iota(shape, 1) == spread(target, rank, m * SUB, SUB, 0))
        logits = logits + jnp.dot(place, log_v[:, m * LANES : (m + 1) * LANES], preferred_element_type=jnp.float32)
    top = jnp.max(logits, axis=1, keepdims=True)
    partition = top + jnp.log(jnp.sum(jnp.exp(logits - top), axis=1, keepdims=True))
    part_ref[...] = partition
    soft_ref[...] = jnp.exp(logits - partition).astype(jnp.bfloat16)


def place_kernel(groups, capacity, got_hbm, out_hbm, got_v, out_v, in_sem, out_sem):
    count, slots, group = out_v.shape
    packed = got_v.shape[2]
    loads = [pltpu.make_async_copy(cols(got_hbm, g, packed), got_v.at[g], in_sem.at[g]) for g in range(count)]
    stores = [pltpu.make_async_copy(out_v.at[g], cols(out_hbm, g, group), out_sem.at[g]) for g in range(count)]
    for load in loads:
        load.start()
    slot = iota((slots, 1), 0)
    matrices = unpack_matrices(slot // capacity, slot % capacity, groups, capacity)
    for g in range(count):
        loads[g].wait()
        blocks = unpack_group(got_v[g], matrices, capacity, group)
        wide = group // len(blocks)
        for b, block in enumerate(blocks):
            out_v[g, :, b * wide : (b + 1) * wide] = block.astype(jnp.bfloat16)
        stores[g].start()
    for store in stores:
        store.wait()


vmem = pl.BlockSpec(memory_space=pltpu.VMEM)
hbm = pl.BlockSpec(memory_space=pl.ANY)


def call(kernel, name, ins, out_shape, outs, scratch, moved, flops):
    return pl.pallas_call(
        kernel,
        out_shape=out_shape,
        in_specs=ins,
        out_specs=outs,
        scratch_shapes=scratch,
        compiler_params=pltpu.CompilerParams(vmem_limit_bytes=VMEM_LIMIT),
        cost_estimate=pl.CostEstimate(flops=flops, bytes_accessed=moved, transcendentals=0),
        name=name,
    )


def reduce_rows(rows, axis):
    size = lax.axis_size(axis)
    me = lax.axis_index(axis)
    half = size // 2
    while half >= 1:
        upper = (me // half) % 2 == 1
        low, high = rows[:half], rows[half:]
        sent = jnp.where(upper, low, high)
        kept = jnp.where(upper, high, low)
        rows = kept + lax.ppermute(sent, axis, [(i, i ^ half) for i in range(size)])
        half //= 2
    return rows


def per_device(features, joining_gains, destination, target_logits, joined_cotangent):
    groups = lax.axis_size("dp")
    slots, width = joined_cotangent.shape
    capacity = slots // groups
    layers = joining_gains.shape[0]
    tokens, kept = target_logits.shape
    count = width // GROUP
    packed = GROUP * capacity // SUB
    rows = groups * SUB
    log_wide = -(-capacity // SUB) * kept
    bf16, f32, dma = jnp.bfloat16, jnp.float32, pltpu.SemaphoreType.DMA
    shape = jax.ShapeDtypeStruct
    dest_row = destination.reshape(1, tokens)

    cot_send = call(
        functools.partial(cot_kernel, groups, capacity),
        "pack_cotangent",
        [vmem, vmem, hbm],
        shape((rows, count * packed + log_wide), bf16),
        hbm,
        [
            pltpu.VMEM((count, slots, GROUP), bf16),
            pltpu.VMEM((count, rows, packed), bf16),
            pltpu.VMEM((rows, log_wide), bf16),
            dma((count,)),
            dma((count,)),
            dma,
        ],
        4 * slots * width,
        2 * rows * slots * width * 2,
    )(dest_row, target_logits, joined_cotangent)
    cot_got = lax.all_to_all(cot_send, "dp", split_axis=0, concat_axis=0, tiled=True)

    join_send, inverse = call(
        functools.partial(join_kernel, groups, capacity),
        "join_layers",
        [vmem, vmem, hbm],
        (shape((rows, count * packed), bf16), shape((tokens, LANES), f32)),
        (hbm, vmem),
        [
            pltpu.VMEM((layers, count, tokens, GROUP), bf16),
            pltpu.VMEM((count, rows, packed), bf16),
            dma((layers, count)),
            dma((count,)),
        ],
        2 * layers * tokens * width + 2 * slots * width,
        2 * rows * tokens * width * 2,
    )(dest_row, joining_gains, features)
    join_got = lax.all_to_all(join_send, "dp", split_axis=0, concat_axis=0, tiled=True)

    partial_rows, soft_labels, log_partition = call(
        functools.partial(grad_kernel, groups, capacity),
        "gain_partials",
        [vmem, vmem, hbm, hbm],
        (shape((groups, layers * width // groups), f32), shape((slots, kept), bf16), shape((slots, 1), f32)),
        (vmem, vmem, vmem),
        [
            pltpu.VMEM((layers, count, tokens, GROUP), bf16),
            pltpu.VMEM((count, rows, packed), bf16),
            pltpu.VMEM((rows, log_wide), bf16),
            dma((layers, count)),
            dma((count,)),
            dma,
        ],
        2 * layers * tokens * width + 2 * slots * width,
        2 * rows * tokens * width * 2,
    )(dest_row, inverse, features, cot_got)
    gain_grad = reduce_rows(partial_rows, "dp").reshape(layers, width // groups)

    joined_input = call(
        functools.partial(place_kernel, groups, capacity),
        "place_joined",
        [hbm],
        shape((slots, width), bf16),
        hbm,
        [pltpu.VMEM((count, rows, packed), bf16), pltpu.VMEM((count, slots, GROUP), bf16), dma((count,)), dma((count,))],
        4 * slots * width,
        2 * rows * slots * width * 2,
    )(join_got)
    return (joined_input, soft_labels, log_partition[:, 0], gain_grad)


def solution(mesh):
    placed = (
        P(("group", "dp"), None),
        P(),
        P(("group", "dp"), None),
        P(("group", "dp"), None),
        P(("group", "dp"), None),
    )
    return jax.shard_map(
        per_device,
        mesh=mesh,
        in_specs=placed,
        out_specs=(
            P(("group", "dp"), None),
            P(("group", "dp"), None),
            P(("group", "dp")),
            P("group", "dp"),
        ),
        check_vma=False,
    )
```

time: 259 us -> 179 us (0.69)
  waiting for transfers between devices: 160 us -> 124 us
  local copies, waits for them, and re-layouts: 46.1 us -> 11.1 us
  Pallas kernels: 0 us -> 19.1 us
  other arithmetic: 18.7 us -> 0.78 us
  between operations: 14.2 us -> 0.78 us
    all_to_all x3 -> x2, waiting for transfers between devices: 160 us -> 60.8 us  [the longest x1 60.8 us: per_device(): lax.all_to_all(cot_send, 'dp', split_axis=0, concat_axis=0, tiled=True)]
    ppermute x0 -> x4, waiting for transfers between devices: none -> 63.1 us  [reduce_rows(): rows = kept + lax.ppermute(sent, axis, [(i, i ^ half) for i in range(size)])]
    pallas_call x0 -> x4, Pallas kernels: none -> 19.1 us  [the longest x1 5.98 us: per_device(): call(functools.partial(join_kernel, groups, capacity), 'join_layers', [vm...]
    reduce_sum x5 -> x0, other arithmetic: 16.2 us -> none  [the longest x1 6.75 us: per_device(): partial_value = jnp.sum(scaled * row_cot[:, None, :], axis=0)]
    all_to_all x5 -> x0, local copies, waits for them, and re-layouts: 16 us -> none  [the longest x2 7.91 us: per_device(): lax.all_to_all(joined_cotangent, 'dp', split_axis=0, concat_axis=0, tiled...]
    ppermute x0 -> x4, starting transfers between devices: none -> 8.72 us  [reduce_rows(): rows = kept + lax.ppermute(sent, axis, [(i, i ^ half) for i in range(size)])]
    convert_element_type x3 -> x0, local copies, waits for them, and re-layouts: 7.25 us -> none  [the longest x1 4.34 us: per_device(): row_cot = returned[position].astype(jnp.float32)]
    scatter x2 -> x0, local copies, waits for them, and re-layouts: 6.52 us -> none  [the longest x1 5.42 us: per_device(): joined_send = jnp.zeros((slot_total, feature_width), jnp.bfloat16).at[pos...]
  transfers between devices with their start and end apart: 4 -> 6, of which waited for: 2 -> 4; matrix products, arithmetic and copies ran while one was open for 17% -> 0% of each run, Pallas kernels for 0% -> 9%
where the time goes in v1:
time: 179 us; the launch traced here: 176 us
  waiting for transfers between devices  124 us (69%)
  starting transfers between devices  20.3 us (11%)
  Pallas kernels  19.1 us (11%)
  local copies, waits for them, and re-layouts  11.1 us (6%)
    ppermute x4, waiting for transfers between devices, reduce_rows(): rows = kept + lax.ppermute(sent, axis, [(i, i ^ half) for i in range(size)])  63.1 us
    all_to_all x1, waiting for transfers between devices, per_device(): lax.all_to_all(cot_send, 'dp', split_axis=0, concat_axis=0, tiled=True)  60.8 us
    unnamed x16, local copies, waits for them, and re-layouts  10.5 us
    ppermute x4, starting transfers between devices, reduce_rows(): rows = kept + lax.ppermute(sent, axis, [(i, i ^ half) for i in range(size)])  8.72 us
    all_to_all x1, starting transfers between devices, per_device(): lax.all_to_all(cot_send, 'dp', split_axis=0, concat_axis=0, tiled=True)  6.68 us
    pallas_call x1, Pallas kernels, per_device(): call(functools.partial(join_kernel, groups, capacity), 'join_layers', [vm...  5.98 us
    pallas_call x1, Pallas kernels, per_device(): call(functools.partial(grad_kernel, groups, capacity), 'gain_partials', [...  5.21 us
    all_to_all x1, starting transfers between devices, per_device(): lax.all_to_all(join_send, 'dp', split_axis=0, concat_axis=0, tiled=True)  4.91 us
  transfers between devices with their start and end apart: 6, of which 4 were waited for; matrix products, arithmetic and copies ran while one was open for 0% of the time, Pallas kernels for 9%

profile of v1, /device:TPU:13, one launch (start us, length us, event | category | flops | bytes accessed | tf_op | source)
XLA Modules:
  0.0 176.1 jit_solution(11594380532051008532)
XLA Ops:
  0.6 0.0 copy-start.2
  0.6 1.9 %copy-done.2 = bf16[192,8192]{1,0:T(8,128)(2,1)S(1)} copy-done((bf16[192,8192]{1,0:T(8,128)(2,1)S(1)}, bf16[192,8192]{1,0:T(8,128)(2,1)}, u32[]{:S(2)}) %copy-start.2) | copy-done | bytes 3145752
  2.5 0.0 copy-start.5
  2.5 0.8 copy-done.5
  3.3 0.0 copy-start.6
  3.3 0.7 copy-done.6
  3.9 3.9 %pack_cotangent.1 = bf16[128,12544]{1,0:T(8,128)(2,1)} custom-call(s32[1,128]{1,0:T(1,128)S(1)} %bitcast.7, bf16[128,128]{1,0:T(8,128)(2,1)S(1)} %copy-done.5, bf16[192,8192]{1,0:T(8,128)(2,1)S(1)} %copy-done.2), custom_call_target="tpu_custom_call" | custom-call | flops 805306368 | bytes 6291456 | tf_op jit(solution)/shard_map/pack_cotangent/pallas_call | solution.py:288
  7.9 0.0 copy-start.4
  7.9 0.0 copy-start.7
  7.9 6.7 %all-to-all-start.1 = ((bf16[16,8,12544]{2,1,0:T(8,128)(2,1)}), bf16[16,8,12544]{2,1,0:T(8,128)(2,1)S(1)}, u32[]{:S(2)}, u32[]{:S(2)}) async-start(bf16[16,8,12544]{2,1,0:T(8,128)(2,1)} %bitcast.3), calls=%async_computation.1 | async-start | bytes 6422528 | tf_op jit(solution)/shard_map/all_to_all | solution.py:305
  14.6 0.0 copy-done.4
  14.6 0.0 copy-done.7
  14.6 0.0 copy-start
  14.6 2.8 %copy-done = bf16[128,24576]{1,0:T(8,128)(2,1)S(1)} copy-done((bf16[128,24576]{1,0:T(8,128)(2,1)S(1)}, bf16[128,24576]{1,0:T(8,128)(2,1)}, u32[]{:S(2)}) %copy-start) | copy-done | bytes 6291480
  17.4 6.0 %join_layers.1 = (bf16[128,12288]{1,0:T(8,128)(2,1)S(1)}, f32[128,128]{1,0:T(8,128)S(1)}) custom-call(s32[1,128]{1,0:T(1,128)S(1)} %bitcast.8, f32[3,8192]{1,0:T(4,128)S(1)} %copy-done.4, bf16[128,24576]{1,0:T(8,128)(2,1)S(1)} %copy-done), custom_call_target="tpu_custom_call" | custom-call | flops 536870912 | bytes 9437184 | tf_op jit(solution)/shard_map/join_layers/pallas_call | solution.py:307
  23.4 0.0 copy-start.3
  23.4 1.7 copy-done.3
  25.0 60.8 %all-to-all-done.1 = bf16[16,8,12544]{2,1,0:T(8,128)(2,1)S(1)} async-done(((bf16[16,8,12544]{2,1,0:T(8,128)(2,1)}), bf16[16,8,12544]{2,1,0:T(8,128)(2,1)S(1)}, u32[]{:S(2)}, u32[]{:S(2)}) %all-to-all-start.1) | async-done | bytes 3211296 | tf_op jit(solution)/shard_map/all_to_all | solution.py:305
  85.9 4.9 %all-to-all-start = ((bf16[16,8,12288]{2,1,0:T(8,128)(2,1)}), bf16[16,8,12288]{2,1,0:T(8,128)(2,1)}, u32[]{:S(2)}, u32[]{:S(2)}) async-start(bf16[16,8,12288]{2,1,0:T(8,128)(2,1)} %bitcast.6), calls=%async_computation | async-start | bytes 6291456 | tf_op jit(solution)/shard_map/all_to_all | solution.py:322
  90.8 0.0 copy-start.1
  90.8 2.8 %copy-done.1 = bf16[128,24576]{1,0:T(8,128)(2,1)S(1)} copy-done((bf16[128,24576]{1,0:T(8,128)(2,1)S(1)}, bf16[128,24576]{1,0:T(8,128)(2,1)}, u32[]{:S(2)}) %copy-start.1) | copy-done | bytes 6291480
  93.6 5.2 %gain_partials.1 = (f32[16,1536]{1,0:T(8,128)S(1)}, bf16[192,128]{1,0:T(8,128)(2,1)}, f32[192,1]{1,0:T(8,128)S(1)}) custom-call(s32[1,128]{1,0:T(1,128)S(1)} %bitcast.9, f32[128,128]{1,0:T(8,128)S(1)} %get-tuple-element.10.inv_ref, bf16[128,24576]{1,0:T(8,128)(2,1)S(1)} %copy-done.1, bf16[128,12544]{1,0:T(8,128)(2,1)S(1)} %bitcast.5), custom_call_target="tpu_custom_call" | custom-call | flops 536870912 | bytes 9437184 | tf_op jit(solution)/shard_map/gain_partials/pallas_call | solution.py:324
  98.8 2.1 %collective-permute-start = (f32[8,1536]{1,0:T(8,128)S(1)}, f32[8,1536]{1,0:T(8,128)S(1)}, u32[]{:S(2)}, u32[]{:S(2)}) collective-permute-start(f32[8,1536]{1,0:T(8,128)S(1)} %slice_select_fusion), channel_id=1, source_target_pairs={{0,8},{1,9},{2,10},{3,11},{4,12},{5,13},{6,14},{7,15},{8,0},{9,1},... | collective-permute-start | bytes 147464 | tf_op jit(solution)/shard_map/ppermute | solution.py:269
  100.9 59.6 %collective-permute-done = f32[8,1536]{1,0:T(8,128)S(1)} collective-permute-done((f32[8,1536]{1,0:T(8,128)S(1)}, f32[8,1536]{1,0:T(8,128)S(1)}, u32[]{:S(2)}, u32[]{:S(2)}) %collective-permute-start) | collective-permute-done | bytes 49184 | tf_op jit(solution)/shard_map/ppermute | solution.py:269
  160.6 3.3 %collective-permute-start.1 = (f32[4,1536]{1,0:T(4,128)S(1)}, f32[4,1536]{1,0:T(4,128)S(1)}, u32[]{:S(2)}, u32[]{:S(2)}) collective-permute-start(f32[4,1536]{1,0:T(4,128)S(1)} %slice_select_fusion.1), channel_id=1, source_target_pairs={{0,4},{1,5},{2,6},{3,7},{4,0},{5,1},{6,2},{7,3},{8,12},{9,13},{10,... | collective-permute-start | bytes 73736 | tf_op jit(solution)/shard_map/ppermute | solution.py:269
  163.9 1.2 collective-permute-done.1
  165.1 0.3 collective-permute-start.2
  165.5 2.3 %collective-permute-done.2 = f32[2,1536]{1,0:T(2,128)S(1)} collective-permute-done((f32[2,1536]{1,0:T(2,128)S(1)}, f32[2,1536]{1,0:T(2,128)S(1)}, u32[]{:S(2)}, u32[]{:S(2)}) %collective-permute-start.2) | collective-permute-done | bytes 12320 | tf_op jit(solution)/shard_map/ppermute | solution.py:269
  167.8 3.0 %collective-permute-start.3 = (f32[1,1536]{1,0:T(1,128)S(1)}, f32[1,1536]{1,0:T(1,128)S(1)}, u32[]{:S(2)}, u32[]{:S(2)}) collective-permute-start(f32[1,1536]{1,0:T(1,128)S(1)} %broadcast_select_fusion.1), channel_id=1, source_target_pairs={{0,1},{1,0},{2,3},{3,2},{4,5},{5,4},{6,7},{7,6},{8,9},{9,8},{10,11... | collective-permute-start | bytes 18440 | tf_op jit(solution)/shard_map/ppermute | solution.py:269
  170.7 0.0 all-to-all-done
  170.7 4.0 %place_joined.1 = bf16[192,8192]{1,0:T(8,128)(2,1)} custom-call(bf16[128,12288]{1,0:T(8,128)(2,1)} %bitcast.2.got_hbm), custom_call_target="tpu_custom_call" | custom-call | flops 805306368 | bytes 6291456 | tf_op jit(solution)/shard_map/place_joined/pallas_call | solution.py:343
  174.8 0.7 reduce
  175.4 0.0 collective-permute-done.3
  175.5 0.6 reshape.19
  (8 shorter events, 0.1 us)
Async XLA Ops:
  0.6 1.9 %copy-start.2 = (bf16[192,8192]{1,0:T(8,128)(2,1)S(1)}, bf16[192,8192]{1,0:T(8,128)(2,1)}, u32[]{:S(2)}) copy-start(bf16[192,8192]{1,0:T(8,128)(2,1)} %cot_hbm.1) | copy-start | bytes 9437188
  2.5 0.8 copy-start.5
  3.3 0.7 copy-start.6
  7.9 6.7 %copy-start.4 = (f32[3,8192]{1,0:T(4,128)S(1)}, f32[3,8192]{1,0:T(4,128)}, u32[]{:S(2)}) copy-start(f32[3,8192]{1,0:T(4,128)} %gain_ref.1) | copy-start | bytes 294916
  7.9 6.7 %copy-start.7 = (s32[128,1]{0,1:T(1,128)S(1)}, s32[128,1]{0,1:T(1,128)}, u32[]{:S(2)}) copy-start(s32[128,1]{0,1:T(1,128)} %param.7) | copy-start | bytes 1540
  7.9 78.0 %all-to-all-start.1 = ((bf16[16,8,12544]{2,1,0:T(8,128)(2,1)}), bf16[16,8,12544]{2,1,0:T(8,128)(2,1)S(1)}, u32[]{:S(2)}, u32[]{:S(2)}) async-start(bf16[16,8,12544]{2,1,0:T(8,128)(2,1)} %bitcast.3), calls=%async_computation.1 | async-start | bytes 6422528 | tf_op jit(solution)/shard_map/all_to_all | solution.py:305
  14.6 2.8 %copy-start = (bf16[128,24576]{1,0:T(8,128)(2,1)S(1)}, bf16[128,24576]{1,0:T(8,128)(2,1)}, u32[]{:S(2)}) copy-start(bf16[128,24576]{1,0:T(8,128)(2,1)} %feat_hbm.3) | copy-start | bytes 18874372
  23.4 1.7 copy-start.3
  85.9 84.9 %all-to-all-start = ((bf16[16,8,12288]{2,1,0:T(8,128)(2,1)}), bf16[16,8,12288]{2,1,0:T(8,128)(2,1)}, u32[]{:S(2)}, u32[]{:S(2)}) async-start(bf16[16,8,12288]{2,1,0:T(8,128)(2,1)} %bitcast.6), calls=%async_computation | async-start | bytes 6291456 | tf_op jit(solution)/shard_map/all_to_all | solution.py:322
  90.8 2.8 %copy-start.1 = (bf16[128,24576]{1,0:T(8,128)(2,1)S(1)}, bf16[128,24576]{1,0:T(8,128)(2,1)}, u32[]{:S(2)}) copy-start(bf16[128,24576]{1,0:T(8,128)(2,1)} %feat_hbm.3) | copy-start | bytes 18874372
  98.8 61.8 %collective-permute-start = (f32[8,1536]{1,0:T(8,128)S(1)}, f32[8,1536]{1,0:T(8,128)S(1)}, u32[]{:S(2)}, u32[]{:S(2)}) collective-permute-start(f32[8,1536]{1,0:T(8,128)S(1)} %slice_select_fusion), channel_id=1, source_target_pairs={{0,8},{1,9},{2,10},{3,11},{4,12},{5,13},{6,14},{7,15},{8,0},{9,1},... | collective-permute-start | bytes 147464 | tf_op jit(solution)/shard_map/ppermute | solution.py:269
  160.6 4.5 %collective-permute-start.1 = (f32[4,1536]{1,0:T(4,128)S(1)}, f32[4,1536]{1,0:T(4,128)S(1)}, u32[]{:S(2)}, u32[]{:S(2)}) collective-permute-start(f32[4,1536]{1,0:T(4,128)S(1)} %slice_select_fusion.1), channel_id=1, source_target_pairs={{0,4},{1,5},{2,6},{3,7},{4,0},{5,1},{6,2},{7,3},{8,12},{9,13},{10,... | collective-permute-start | bytes 73736 | tf_op jit(solution)/shard_map/ppermute | solution.py:269
  165.1 2.6 %collective-permute-start.2 = (f32[2,1536]{1,0:T(2,128)S(1)}, f32[2,1536]{1,0:T(2,128)S(1)}, u32[]{:S(2)}, u32[]{:S(2)}) collective-permute-start(f32[2,1536]{1,0:T(2,128)S(1)} %broadcast_select_fusion), channel_id=1, source_target_pairs={{0,2},{1,3},{2,0},{3,1},{4,6},{5,7},{6,4},{7,5},{8,10},{9,11},{10,... | collective-permute-start | bytes 36872 | tf_op jit(solution)/shard_map/ppermute | solution.py:269
  167.8 7.7 %collective-permute-start.3 = (f32[1,1536]{1,0:T(1,128)S(1)}, f32[1,1536]{1,0:T(1,128)S(1)}, u32[]{:S(2)}, u32[]{:S(2)}) collective-permute-start(f32[1,1536]{1,0:T(1,128)S(1)} %broadcast_select_fusion.1), channel_id=1, source_target_pairs={{0,1},{1,0},{2,3},{3,2},{4,5},{5,4},{6,7},{7,6},{8,9},{9,8},{10,11... | collective-permute-start | bytes 18440 | tf_op jit(solution)/shard_map/ppermute | solution.py:269

commit v2 on v1

--- a/solution.py
+++ b/solution.py
@@ -9,9 +9,10 @@
 
 eps = 1e-06
 SUB = 8
-GROUP = 1024
+GROUP = 2048
 LANES = 128
-VMEM_LIMIT = 40 * 1024 * 1024
+VMEM_LIMIT = 20 * 1024 * 1024
+VMEM_WHOLE = 56 * 1024 * 1024
 
 
 def pieces_of(capacity):
@@ -21,6 +22,24 @@
             found.append((first, size, SUB // size))
             first += size
     return found
+
+
+def radices(size):
+    found = []
+    while size > 1:
+        found.append(4 if size % 4 == 0 else 2)
+        size //= found[-1]
+    return found
+
+
+def exchange_order(size):
+    order = []
+    for device in range(size):
+        row, rest = 0, device
+        for radix in radices(size):
+            row, rest = row * radix + rest % radix, rest // radix
+        order.append(row)
+    return order
 
 
 def iota(shape, dim):
@@ -100,18 +119,26 @@
     return ref.at[:, g * wide : (g + 1) * wide]
 
 
-def cot_kernel(groups, capacity, dest_ref, logit_ref, cot_hbm, out_hbm, cot_v, out_v, log_v, in_sem, out_sem, log_sem):
+def cot_kernel(
+    groups, capacity, dest_hbm, logit_hbm, cot_hbm, out_hbm, dest_v, logit_v, cot_v, out_v, log_v, dest_sem, logit_sem, in_sem, out_sem, log_sem
+):
     count, slots, group = cot_v.shape
     packed = out_v.shape[2]
     loads = [pltpu.make_async_copy(cols(cot_hbm, g, group), cot_v.at[g], in_sem.at[g]) for g in range(count)]
     stores = [pltpu.make_async_copy(out_v.at[g], cols(out_hbm, g, packed), out_sem.at[g]) for g in range(count)]
+    dest_load = pltpu.make_async_copy(dest_hbm, dest_v, dest_sem)
+    logit_load = pltpu.make_async_copy(logit_hbm, logit_v, logit_sem)
+    dest_load.start()
+    logit_load.start()
     for load in loads:
         load.start()
-    target, rank, _, _ = ranks_of(dest_ref[...])
+    dest_load.wait()
+    target, rank, _, _ = ranks_of(dest_v[...])
     shape = (groups * SUB, target.shape[1])
+    logit_load.wait()
     for m in range(log_v.shape[1] // LANES):
         place = hot(iota(shape, 0) == spread(target, rank, m * SUB, SUB, 0))
-        log_v[:, m * LANES : (m + 1) * LANES] = select(place, logit_ref[...])
+        log_v[:, m * LANES : (m + 1) * LANES] = select(place, logit_v[...])
     log_store = pltpu.make_async_copy(log_v, out_hbm.at[:, count * packed : count * packed + log_v.shape[1]], log_sem)
     log_store.start()
     slot = iota((1, slots), 1)
@@ -177,6 +204,7 @@
     layers, count, tokens, group = feat_v.shape
     packed = got_v.shape[2]
     own = grad_ref.shape[1] // layers
+    order = exchange_order(groups)
     log_load = pltpu.make_async_copy(got_hbm.at[:, count * packed : count * packed + log_v.shape[1]], log_v, log_sem)
     log_load.start()
     gots = [pltpu.make_async_copy(cols(got_hbm, g, packed), got_v.at[g], got_sem.at[g]) for g in range(count)]
@@ -204,7 +232,8 @@
                 for u in range(wide // step):
                     at = g * group + b * wide + u * step
                     lo = l * own + at % own
-                    grad_ref[at // own : at // own + 1, lo : lo + step] = part[:, u * step : (u + 1) * step]
+                    row = order[at // own]
+                    grad_ref[row : row + 1, lo : lo + step] = part[:, u * step : (u + 1) * step]
     log_load.wait()
     slots = soft_ref.shape[0]
     slot = iota((slots, 1), 0)
@@ -241,17 +270,18 @@
 
 
 vmem = pl.BlockSpec(memory_space=pltpu.VMEM)
-hbm = pl.BlockSpec(memory_space=pl.ANY)
-
-
-def call(kernel, name, ins, out_shape, outs, scratch, moved, flops):
+hbm = pl.BlockSpec(memory_space=pltpu.HBM)
+anywhere = pl.BlockSpec(memory_space=pl.ANY)
+
+
+def call(kernel, name, ins, out_shape, outs, scratch, moved, flops, limit=VMEM_LIMIT):
     return pl.pallas_call(
         kernel,
         out_shape=out_shape,
         in_specs=ins,
         out_specs=outs,
         scratch_shapes=scratch,
-        compiler_params=pltpu.CompilerParams(vmem_limit_bytes=VMEM_LIMIT),
+        compiler_params=pltpu.CompilerParams(vmem_limit_bytes=limit),
         cost_estimate=pl.CostEstimate(flops=flops, bytes_accessed=moved, transcendentals=0),
         name=name,
     )
@@ -260,14 +290,19 @@
 def reduce_rows(rows, axis):
     size = lax.axis_size(axis)
     me = lax.axis_index(axis)
-    half = size // 2
-    while half >= 1:
-        upper = (me // half) % 2 == 1
-        low, high = rows[:half], rows[half:]
-        sent = jnp.where(upper, low, high)
-        kept = jnp.where(upper, high, low)
-        rows = kept + lax.ppermute(sent, axis, [(i, i ^ half) for i in range(size)])
-        half //= 2
+    stride = 1
+    for radix in radices(size):
+        part = rows.shape[0] // radix
+        digit = lax.rem(lax.div(me, stride), radix)
+        total = lax.dynamic_slice_in_dim(rows, digit * part, part, 0)
+        got = []
+        for m in range(1, radix):
+            sent = lax.dynamic_slice_in_dim(rows, (digit ^ m) * part, part, 0)
+            got.append(lax.ppermute(sent, axis, [(i, i ^ (m * stride)) for i in range(size)]))
+        for value in got:
+            total = total + value
+        rows = total
+        stride *= radix
     return rows
 
 
@@ -288,19 +323,24 @@
     cot_send = call(
         functools.partial(cot_kernel, groups, capacity),
         "pack_cotangent",
-        [vmem, vmem, hbm],
+        [hbm, hbm, hbm],
         shape((rows, count * packed + log_wide), bf16),
         hbm,
         [
+            pltpu.VMEM((1, tokens), jnp.int32),
+            pltpu.VMEM((tokens, kept), bf16),
             pltpu.VMEM((count, slots, GROUP), bf16),
             pltpu.VMEM((count, rows, packed), bf16),
             pltpu.VMEM((rows, log_wide), bf16),
+            dma,
+            dma,
             dma((count,)),
             dma((count,)),
             dma,
         ],
         4 * slots * width,
         2 * rows * slots * width * 2,
+        VMEM_WHOLE,
     )(dest_row, target_logits, joined_cotangent)
     cot_got = lax.all_to_all(cot_send, "dp", split_axis=0, concat_axis=0, tiled=True)
 
@@ -324,7 +364,7 @@
     partial_rows, soft_labels, log_partition = call(
         functools.partial(grad_kernel, groups, capacity),
         "gain_partials",
-        [vmem, vmem, hbm, hbm],
+        [vmem, vmem, hbm, anywhere],
         (shape((groups, layers * width // groups), f32), shape((slots, kept), bf16), shape((slots, 1), f32)),
         (vmem, vmem, vmem),
         [
@@ -343,7 +383,7 @@
     joined_input = call(
         functools.partial(place_kernel, groups, capacity),
         "place_joined",
-        [hbm],
+        [anywhere],
         shape((slots, width), bf16),
         hbm,
         [pltpu.VMEM((count, rows, packed), bf16), pltpu.VMEM((count, slots, GROUP), bf16), dma((count,)), dma((count,))],

time: 179 us -> 164 us (0.916); the launches traced: 176 us -> 163 us
  waiting for transfers between devices: 124 us -> 116 us
  local copies, waits for them, and re-layouts: 11.1 us -> 7.89 us
    ppermute x4 -> x6, waiting for transfers between devices: 63.1 us -> 5.99 us  [reduce_rows(): lax.ppermute(sent, axis, [(i, i ^ m * stride) for i in range(size)])]
    all_to_all x1, waiting for transfers between devices: 0.01 us -> 48.6 us  [per_device(): lax.all_to_all(join_send, 'dp', split_axis=0, concat_axis=0, tiled=True)]
    unnamed x16 -> x10, local copies, waits for them, and re-layouts: 10.5 us -> 7.23 us
    ppermute x4 -> x6, starting transfers between devices: 8.72 us -> 8.4 us  [reduce_rows(): lax.ppermute(sent, axis, [(i, i ^ m * stride) for i in range(size)])]
  transfers between devices with their start and end apart: 6 -> 8, of which waited for: 4 -> 3; matrix products, arithmetic and copies ran while one was open for 0% -> 0% of each run, Pallas kernels for 9% -> 8%
where the time goes in v2:
time: 164 us; the launch traced here: 163 us
  waiting for transfers between devices  116 us (71%)
  starting transfers between devices  20 us (12%)
  Pallas kernels  17.8 us (11%)
  local copies, waits for them, and re-layouts  7.89 us (5%)
    all_to_all x1, waiting for transfers between devices, per_device(): lax.all_to_all(cot_send, 'dp', split_axis=0, concat_axis=0, tiled=True)  61.6 us
    all_to_all x1, waiting for transfers between devices, per_device(): lax.all_to_all(join_send, 'dp', split_axis=0, concat_axis=0, tiled=True)  48.6 us
    ppermute x6, starting transfers between devices, reduce_rows(): lax.ppermute(sent, axis, [(i, i ^ m * stride) for i in range(size)])  8.4 us
    unnamed x10, local copies, waits for them, and re-layouts  7.23 us
    all_to_all x1, starting transfers between devices, per_device(): lax.all_to_all(cot_send, 'dp', split_axis=0, concat_axis=0, tiled=True)  6.7 us
    ppermute x6, waiting for transfers between devices, reduce_rows(): lax.ppermute(sent, axis, [(i, i ^ m * stride) for i in range(size)])  5.99 us
    pallas_call x1, Pallas kernels, per_device(): call(functools.partial(join_kernel, groups, capacity), 'join_layers', [vm...  5.21 us
    all_to_all x1, starting transfers between devices, per_device(): lax.all_to_all(join_send, 'dp', split_axis=0, concat_axis=0, tiled=True)  4.91 us
  transfers between devices with their start and end apart: 8, of which 3 were waited for; matrix products, arithmetic and copies ran while one was open for 0% of the time, Pallas kernels for 8%

profile of v2, /device:TPU:13, one launch (start us, length us, event | category | flops | bytes accessed | tf_op | source)
XLA Modules:
  0.0 163.4 jit_solution(12925958005347154462)
XLA Ops:
  0.6 4.5 %pack_cotangent.1 = bf16[128,12544]{1,0:T(8,128)(2,1)} custom-call(s32[1,128]{1,0:T(1,128)} %bitcast.7, bf16[128,128]{1,0:T(8,128)(2,1)} %logit_hbm.1, bf16[192,8192]{1,0:T(8,128)(2,1)} %cot_hbm.1), custom_call_target="tpu_custom_call" | custom-call | flops 805306368 | bytes 6291456 | tf_op jit(solution)/shard_map/pack_cotangent/pallas_call | solution.py:323
  5.1 0.0 copy-start.3
  5.1 0.0 copy-start.4
  5.1 6.7 %all-to-all-start.1 = ((bf16[16,8,12544]{2,1,0:T(8,128)(2,1)}), bf16[16,8,12544]{2,1,0:T(8,128)(2,1)S(1)}, u32[]{:S(2)}, u32[]{:S(2)}) async-start(bf16[16,8,12544]{2,1,0:T(8,128)(2,1)} %bitcast.10), calls=%async_computation.1 | async-start | bytes 6422528 | tf_op jit(solution)/shard_map/all_to_all | solution.py:345
  11.8 0.0 copy-done.3
  11.8 0.0 copy-done.4
  11.8 0.0 copy-start
  11.8 2.8 %copy-done = bf16[128,24576]{1,0:T(8,128)(2,1)S(1)} copy-done((bf16[128,24576]{1,0:T(8,128)(2,1)S(1)}, bf16[128,24576]{1,0:T(8,128)(2,1)}, u32[]{:S(2)}) %copy-start) | copy-done | bytes 6291480
  14.6 5.2 %join_layers.1 = (bf16[128,12288]{1,0:T(8,128)(2,1)S(1)}, f32[128,128]{1,0:T(8,128)S(1)}) custom-call(s32[1,128]{1,0:T(1,128)S(1)} %bitcast.8, f32[3,8192]{1,0:T(4,128)S(1)} %copy-done.3, bf16[128,24576]{1,0:T(8,128)(2,1)S(1)} %copy-done), custom_call_target="tpu_custom_call" | custom-call | flops 536870912 | bytes 9437184 | tf_op jit(solution)/shard_map/join_layers/pallas_call | solution.py:347
  19.8 0.0 copy-start.2
  19.8 1.7 %copy-done.2 = bf16[128,12288]{1,0:T(8,128)(2,1)} copy-done((bf16[128,12288]{1,0:T(8,128)(2,1)}, bf16[128,12288]{1,0:T(8,128)(2,1)S(1)}, u32[]{:S(2)}) %copy-start.2) | copy-done | bytes 3145752
  21.5 61.6 %all-to-all-done.1 = bf16[16,8,12544]{2,1,0:T(8,128)(2,1)S(1)} async-done(((bf16[16,8,12544]{2,1,0:T(8,128)(2,1)}), bf16[16,8,12544]{2,1,0:T(8,128)(2,1)S(1)}, u32[]{:S(2)}, u32[]{:S(2)}) %all-to-all-start.1) | async-done | bytes 3211296 | tf_op jit(solution)/shard_map/all_to_all | solution.py:345
  83.1 4.9 %all-to-all-start = ((bf16[16,8,12288]{2,1,0:T(8,128)(2,1)}), bf16[16,8,12288]{2,1,0:T(8,128)(2,1)}, u32[]{:S(2)}, u32[]{:S(2)}) async-start(bf16[16,8,12288]{2,1,0:T(8,128)(2,1)} %bitcast.6), calls=%async_computation | async-start | bytes 6291456 | tf_op jit(solution)/shard_map/all_to_all | solution.py:362
  88.0 0.0 copy-start.1
  88.0 2.8 %copy-done.1 = bf16[128,24576]{1,0:T(8,128)(2,1)S(1)} copy-done((bf16[128,24576]{1,0:T(8,128)(2,1)S(1)}, bf16[128,24576]{1,0:T(8,128)(2,1)}, u32[]{:S(2)}) %copy-start.1) | copy-done | bytes 6291480
  90.8 4.5 %gain_partials.1 = (f32[16,1536]{1,0:T(8,128)S(1)}, bf16[192,128]{1,0:T(8,128)(2,1)}, f32[192,1]{1,0:T(8,128)S(1)}) custom-call(s32[1,128]{1,0:T(1,128)S(1)} %bitcast.9, f32[128,128]{1,0:T(8,128)S(1)} %get-tuple-element.10.inv_ref, bf16[128,24576]{1,0:T(8,128)(2,1)S(1)} %copy-done.1, bf16[128,12544]{1,0:T(8,128)(2,1)S(1)} %bitcast.5), custom_call_target="tpu_custom_call" | custom-call | flops 536870912 | bytes 9437184 | tf_op jit(solution)/shard_map/gain_partials/pallas_call | solution.py:364
  95.4 0.4 collective-permute-start
  95.8 0.3 collective-permute-start.2
  96.1 1.2 collective-permute-start.1
  97.3 0.0 collective-permute-done
  97.3 6.0 %collective-permute-done.2 = f32[4,1536]{1,0:T(4,128)S(1)} collective-permute-done((f32[4,1536]{1,0:T(4,128)S(1)}, f32[4,1536]{1,0:T(4,128)S(1)}, u32[]{:S(2)}, u32[]{:S(2)}) %collective-permute-start.2) | collective-permute-done | bytes 24608 | tf_op jit(solution)/shard_map/ppermute | solution.py:301
  103.3 0.0 collective-permute-done.1
  103.3 0.2 collective-permute-start.3
  103.5 6.3 %collective-permute-start.5 = (f32[1,1536]{1,0:T(1,128)S(1)}, f32[1,1536]{1,0:T(1,128)S(1)}, u32[]{:S(2)}, u32[]{:S(2)}) collective-permute-start(f32[1,1536]{1,0:T(1,128)S(1)} %get-tuple-element.18), channel_id=1, source_target_pairs={{0,12},{1,13},{2,14},{3,15},{4,8},{5,9},{6,10},{7,11},{8,4},{9,5},... | collective-permute-start | bytes 18440 | tf_op jit(solution)/shard_map/ppermute | solution.py:301
  109.8 0.0 collective-permute-start.4
  109.8 48.6 %all-to-all-done = bf16[16,8,12288]{2,1,0:T(8,128)(2,1)} async-done(((bf16[16,8,12288]{2,1,0:T(8,128)(2,1)}), bf16[16,8,12288]{2,1,0:T(8,128)(2,1)}, u32[]{:S(2)}, u32[]{:S(2)}) %all-to-all-start) | async-done | bytes 3145760 | tf_op jit(solution)/shard_map/all_to_all | solution.py:362
  158.4 3.6 %place_joined.1 = bf16[192,8192]{1,0:T(8,128)(2,1)} custom-call(bf16[128,12288]{1,0:T(8,128)(2,1)} %bitcast.2.got_hbm), custom_call_target="tpu_custom_call" | custom-call | flops 805306368 | bytes 6291456 | tf_op jit(solution)/shard_map/place_joined/pallas_call | solution.py:383
  162.0 0.7 reduce
  162.7 0.0 collective-permute-done.3
  162.7 0.0 collective-permute-done.5
  162.7 0.0 collective-permute-done.4
  162.8 0.6 reshape.19
  (4 shorter events, 0.1 us)
Async XLA Ops:
  5.1 6.7 %copy-start.3 = (f32[3,8192]{1,0:T(4,128)S(1)}, f32[3,8192]{1,0:T(4,128)}, u32[]{:S(2)}) copy-start(f32[3,8192]{1,0:T(4,128)} %gain_ref.1) | copy-start | bytes 294916
  5.1 6.7 %copy-start.4 = (s32[128,1]{0,1:T(1,128)S(1)}, s32[128,1]{0,1:T(1,128)}, u32[]{:S(2)}) copy-start(s32[128,1]{0,1:T(1,128)} %param.7) | copy-start | bytes 1540
  5.1 78.0 %all-to-all-start.1 = ((bf16[16,8,12544]{2,1,0:T(8,128)(2,1)}), bf16[16,8,12544]{2,1,0:T(8,128)(2,1)S(1)}, u32[]{:S(2)}, u32[]{:S(2)}) async-start(bf16[16,8,12544]{2,1,0:T(8,128)(2,1)} %bitcast.10), calls=%async_computation.1 | async-start | bytes 6422528 | tf_op jit(solution)/shard_map/all_to_all | solution.py:345
  11.8 2.8 %copy-start = (bf16[128,24576]{1,0:T(8,128)(2,1)S(1)}, bf16[128,24576]{1,0:T(8,128)(2,1)}, u32[]{:S(2)}) copy-start(bf16[128,24576]{1,0:T(8,128)(2,1)} %feat_hbm.3) | copy-start | bytes 18874372
  19.8 1.7 %copy-start.2 = (bf16[128,12288]{1,0:T(8,128)(2,1)}, bf16[128,12288]{1,0:T(8,128)(2,1)S(1)}, u32[]{:S(2)}) copy-start(bf16[128,12288]{1,0:T(8,128)(2,1)S(1)} %get-tuple-element.9) | copy-start | bytes 9437188
  83.1 75.3 %all-to-all-start = ((bf16[16,8,12288]{2,1,0:T(8,128)(2,1)}), bf16[16,8,12288]{2,1,0:T(8,128)(2,1)}, u32[]{:S(2)}, u32[]{:S(2)}) async-start(bf16[16,8,12288]{2,1,0:T(8,128)(2,1)} %bitcast.6), calls=%async_computation | async-start | bytes 6291456 | tf_op jit(solution)/shard_map/all_to_all | solution.py:362
  88.0 2.8 %copy-start.1 = (bf16[128,24576]{1,0:T(8,128)(2,1)S(1)}, bf16[128,24576]{1,0:T(8,128)(2,1)}, u32[]{:S(2)}) copy-start(bf16[128,24576]{1,0:T(8,128)(2,1)} %feat_hbm.3) | copy-start | bytes 18874372
  95.4 1.9 %collective-permute-start = (f32[4,1536]{1,0:T(4,128)S(1)}, f32[4,1536]{1,0:T(4,128)S(1)}, u32[]{:S(2)}, u32[]{:S(2)}) collective-permute-start(f32[4,1536]{1,0:T(4,128)S(1)} %get-tuple-element.14), channel_id=1, source_target_pairs={{0,1},{1,0},{2,3},{3,2},{4,5},{5,4},{6,7},{7,6},{8,9},{9,8},{10,11... | collective-permute-start | bytes 73736 | tf_op jit(solution)/shard_map/ppermute | solution.py:301
  95.8 7.5 %collective-permute-start.2 = (f32[4,1536]{1,0:T(4,128)S(1)}, f32[4,1536]{1,0:T(4,128)S(1)}, u32[]{:S(2)}, u32[]{:S(2)}) collective-permute-start(f32[4,1536]{1,0:T(4,128)S(1)} %get-tuple-element.15), channel_id=1, source_target_pairs={{0,3},{1,2},{2,1},{3,0},{4,7},{5,6},{6,5},{7,4},{8,11},{9,10},{10,... | collective-permute-start | bytes 73736 | tf_op jit(solution)/shard_map/ppermute | solution.py:301
  96.1 7.2 %collective-permute-start.1 = (f32[4,1536]{1,0:T(4,128)S(1)}, f32[4,1536]{1,0:T(4,128)S(1)}, u32[]{:S(2)}, u32[]{:S(2)}) collective-permute-start(f32[4,1536]{1,0:T(4,128)S(1)} %get-tuple-element.16), channel_id=1, source_target_pairs={{0,2},{1,3},{2,0},{3,1},{4,6},{5,7},{6,4},{7,5},{8,10},{9,11},{10,... | collective-permute-start | bytes 73736 | tf_op jit(solution)/shard_map/ppermute | solution.py:301
  103.3 59.4 %collective-permute-start.3 = (f32[1,1536]{1,0:T(1,128)S(1)}, f32[1,1536]{1,0:T(1,128)S(1)}, u32[]{:S(2)}, u32[]{:S(2)}) collective-permute-start(f32[1,1536]{1,0:T(1,128)S(1)} %get-tuple-element.17), channel_id=1, source_target_pairs={{0,4},{1,5},{2,6},{3,7},{4,0},{5,1},{6,2},{7,3},{8,12},{9,13},{10,... | collective-permute-start | bytes 18440 | tf_op jit(solution)/shard_map/ppermute | solution.py:301
  103.5 59.2 %collective-permute-start.5 = (f32[1,1536]{1,0:T(1,128)S(1)}, f32[1,1536]{1,0:T(1,128)S(1)}, u32[]{:S(2)}, u32[]{:S(2)}) collective-permute-start(f32[1,1536]{1,0:T(1,128)S(1)} %get-tuple-element.18), channel_id=1, source_target_pairs={{0,12},{1,13},{2,14},{3,15},{4,8},{5,9},{6,10},{7,11},{8,4},{9,5},... | collective-permute-start | bytes 18440 | tf_op jit(solution)/shard_map/ppermute | solution.py:301
  109.8 52.9 %collective-permute-start.4 = (f32[1,1536]{1,0:T(1,128)S(1)}, f32[1,1536]{1,0:T(1,128)S(1)}, u32[]{:S(2)}, u32[]{:S(2)}) collective-permute-start(f32[1,1536]{1,0:T(1,128)S(1)} %get-tuple-element.19), channel_id=1, source_target_pairs={{0,8},{1,9},{2,10},{3,11},{4,12},{5,13},{6,14},{7,15},{8,0},{9,1},... | collective-permute-start | bytes 18440 | tf_op jit(solution)/shard_map/ppermute | solution.py:301

commit v3 on v2

--- a/solution.py
+++ b/solution.py
@@ -11,6 +11,8 @@
 SUB = 8
 GROUP = 2048
 LANES = 128
+PLANE = 4
+CHUNKS = (2, 2)
 VMEM_LIMIT = 20 * 1024 * 1024
 VMEM_WHOLE = 56 * 1024 * 1024
 
@@ -155,19 +157,45 @@
     log_store.wait()
 
 
-def join_kernel(groups, capacity, dest_ref, gain_ref, feat_hbm, out_hbm, inv_ref, feat_v, out_v, in_sem, out_sem):
+def place_of():
+    me = lax.axis_index("dp")
+    return lax.div(me, PLANE), lax.rem(me, PLANE)
+
+
+def chunk_starts():
+    first = 0
+    for chunk, held in enumerate(CHUNKS):
+        yield chunk, first, held
+        first += held
+
+
+def join_kernel(groups, capacity, dest_ref, gain_ref, feat_hbm, *refs):
+    *outs, inv_ref, feat_v, out_v, in_sem, out_sem = refs
     layers, count, tokens, group = feat_v.shape
     width = count * group
     packed = out_v.shape[2]
+    part = out_v.shape[1] // PLANE
     loads = [
         [pltpu.make_async_copy(cols(feat_hbm, l * count + g, group), feat_v.at[l, g], in_sem.at[l, g]) for g in range(count)]
         for l in range(layers)
     ]
-    stores = [pltpu.make_async_copy(out_v.at[g], cols(out_hbm, g, packed), out_sem.at[g]) for g in range(count)]
+    stores = []
+    for chunk, first, held in chunk_starts():
+        for g in range(held):
+            stores.append(
+                [
+                    pltpu.make_async_copy(
+                        out_v.at[first + g, q * part : (q + 1) * part], cols(outs[chunk * PLANE + q], g, packed), out_sem.at[first + g, q]
+                    )
+                    for q in range(PLANE)
+                ]
+            )
     for row in loads:
         for load in row:
             load.start()
     target, rank, _, _ = ranks_of(dest_ref[...])
+    plane, within = place_of()
+    target = (lax.rem(target, PLANE) ^ within) * (groups // PLANE) + (lax.div(target, PLANE) ^ plane)
     matrices = pack_matrices(target, rank, groups, capacity)
     lane = iota((tokens, LANES), 1)
     inv_all = jnp.zeros((tokens, LANES), jnp.float32)
@@ -193,9 +221,11 @@
         for block in pack_group(joined.astype(jnp.bfloat16), matrices, capacity):
             out_v[g, :, base : base + block.shape[1]] = block
             base += block.shape[1]
-        stores[g].start()
-    for store in stores:
-        store.wait()
+        for store in stores[g]:
+            store.start()
+    for row in stores:
+        for store in row:
+            store.wait()
 
 
 def grad_kernel(
@@ -249,17 +279,28 @@
     soft_ref[...] = jnp.exp(logits - partition).astype(jnp.bfloat16)
 
 
-def place_kernel(groups, capacity, got_hbm, out_hbm, got_v, out_v, in_sem, out_sem):
+def place_kernel(groups, capacity, first, *refs):
+    planes = groups // PLANE
+    gots, (out_hbm, got_v, out_v, in_sem, out_sem) = refs[:planes], refs[-5:]
     count, slots, group = out_v.shape
     packed = got_v.shape[2]
-    loads = [pltpu.make_async_copy(cols(got_hbm, g, packed), got_v.at[g], in_sem.at[g]) for g in range(count)]
-    stores = [pltpu.make_async_copy(out_v.at[g], cols(out_hbm, g, group), out_sem.at[g]) for g in range(count)]
-    for load in loads:
-        load.start()
+    part = got_v.shape[1] // planes
+    loads = [
+        [pltpu.make_async_copy(cols(got, g, packed), got_v.at[g, j * part : (j + 1) * part], in_sem.at[g, j]) for j, got in enumerate(gots)]
+        for g in range(count)
+    ]
+    stores = [pltpu.make_async_copy(out_v.at[g], cols(out_hbm, first + g, group), out_sem.at[g]) for g in range(count)]
+    for row in loads:
+        for load in row:
+            load.start()
     slot = iota((slots, 1), 0)
-    matrices = unpack_matrices(slot // capacity, slot % capacity, groups, capacity)
+    plane, within = place_of()
+    source, rank = lax.div(slot, capacity), lax.rem(slot, capacity)
+    source = (lax.div(source, PLANE) ^ plane) * PLANE + (lax.rem(source, PLANE) ^ within)
+    matrices = unpack_matrices(source, rank, groups, capacity)
     for g in range(count):
-        loads[g].wait()
+        for load in loads[g]:
+            load.wait()
         blocks = unpack_group(got_v[g], matrices, capacity, group)
         wide = group // len(blocks)
         for b, block in enumerate(blocks):
@@ -274,7 +315,7 @@
 anywhere = pl.BlockSpec(memory_space=pl.ANY)
 
 
-def call(kernel, name, ins, out_shape, outs, scratch, moved, flops, limit=VMEM_LIMIT):
+def call(kernel, name, ins, out_shape, outs, scratch, moved, flops, limit=VMEM_LIMIT, aliases=None):
     return pl.pallas_call(
         kernel,
         out_shape=out_shape,
@@ -283,8 +324,14 @@
         scratch_shapes=scratch,
         compiler_params=pltpu.CompilerParams(vmem_limit_bytes=limit),
         cost_estimate=pl.CostEstimate(flops=flops, bytes_accessed=moved, transcendentals=0),
+        input_output_aliases=aliases or {},
         name=name,
     )
+
+
+def swap(blocks, axis, stride):
+    size = lax.axis_size(axis)
+    return [blocks[0]] + [lax.ppermute(block, axis, [(i, i ^ (m * stride)) for i in range(size)]) for m, block in enumerate(blocks) if m]
 
 
 def reduce_rows(rows, axis):
@@ -344,22 +391,28 @@
     )(dest_row, target_logits, joined_cotangent)
     cot_got = lax.all_to_all(cot_send, "dp", split_axis=0, concat_axis=0, tiled=True)
 
-    join_send, inverse = call(
+    planes = groups // PLANE
+    part = planes * SUB
+    *join_send, inverse = call(
         functools.partial(join_kernel, groups, capacity),
         "join_layers",
         [vmem, vmem, hbm],
-        (shape((rows, count * packed), bf16), shape((tokens, LANES), f32)),
-        (hbm, vmem),
+        tuple(shape((part, held * packed), bf16) for held in CHUNKS for _ in range(PLANE)) + (shape((tokens, LANES), f32),),
+        (hbm,) * (len(CHUNKS) * PLANE) + (vmem,),
         [
             pltpu.VMEM((layers, count, tokens, GROUP), bf16),
             pltpu.VMEM((count, rows, packed), bf16),
             dma((layers, count)),
-            dma((count,)),
+            dma((count, PLANE)),
         ],
         2 * layers * tokens * width + 2 * slots * width,
         2 * rows * tokens * width * 2,
     )(dest_row, joining_gains, features)
-    join_got = lax.all_to_all(join_send, "dp", split_axis=0, concat_axis=0, tiled=True)
+    join_got = []
+    for chunk, _, _ in chunk_starts():
+        plane_got = swap(join_send[chunk * PLANE : (chunk + 1) * PLANE], "dp", 1)
+        mixed = [jnp.concatenate([got[j * SUB : (j + 1) * SUB] for got in plane_got], axis=0) for j in range(planes)]
+        join_got.append(swap(mixed, "dp", PLANE))
 
     partial_rows, soft_labels, log_partition = call(
         functools.partial(grad_kernel, groups, capacity),
@@ -380,16 +433,27 @@
     )(dest_row, inverse, features, cot_got)
     gain_grad = reduce_rows(partial_rows, "dp").reshape(layers, width // groups)
 
-    joined_input = call(
-        functools.partial(place_kernel, groups, capacity),
-        "place_joined",
-        [anywhere],
-        shape((slots, width), bf16),
-        hbm,
-        [pltpu.VMEM((count, rows, packed), bf16), pltpu.VMEM((count, slots, GROUP), bf16), dma((count,)), dma((count,))],
-        4 * slots * width,
-        2 * rows * slots * width * 2,
-    )(join_got)
+    joined_input = ()
+    for chunk, first, held in chunk_starts():
+        joined_input = (
+            call(
+                functools.partial(place_kernel, groups, capacity, first),
+                "place_joined",
+                [anywhere] * (planes + len(joined_input)),
+                shape((slots, width), bf16),
+                hbm,
+                [
+                    pltpu.VMEM((held, rows, packed), bf16),
+                    pltpu.VMEM((held, slots, GROUP), bf16),
+                    dma((held, planes)),
+                    dma((held,)),
+                ],
+                4 * slots * held * GROUP,
+                2 * rows * slots * held * GROUP * 2,
+                aliases={planes: 0} if joined_input else None,
+            )(*join_got[chunk], *joined_input),
+        )
+    joined_input = joined_input[0]
     return (joined_input, soft_labels, log_partition[:, 0], gain_grad)
 
 

time: 164 us -> 157 us (0.957)
  waiting for transfers between devices: 116 us -> 82.3 us
  starting transfers between devices: 20 us -> 32 us
  other arithmetic: 0.73 us -> 7.96 us
  local copies, waits for them, and re-layouts: 7.89 us -> 12.4 us
  Pallas kernels: 17.8 us -> 21.1 us
    ppermute x0 -> x12, waiting for transfers between devices: none -> 78.3 us  [swap(): lax.ppermute(block, axis, [(i, i ^ m * stride) for i in range(size)])]
    all_to_all x1, waiting for transfers between devices: 61.6 us -> 3.97 us  [per_device(): lax.all_to_all(cot_send, 'dp', split_axis=0, concat_axis=0, tiled=True)]
    all_to_all x1 -> x0, waiting for transfers between devices: 48.6 us -> none  [per_device(): lax.all_to_all(join_send, 'dp', split_axis=0, concat_axis=0, tiled=True)]
    ppermute x0 -> x12, starting transfers between devices: none -> 19.9 us  [swap(): lax.ppermute(block, axis, [(i, i ^ m * stride) for i in range(size)])]
    concatenate x0 -> x8, other arithmetic: none -> 7.24 us  [per_device(): jnp.concatenate([got[j * SUB:(j + 1) * SUB] for got in plane_got], axis=0)]
    slice x0 -> x7, local copies, waits for them, and re-layouts: none -> 6.16 us  [per_device(): got[j * SUB:(j + 1) * SUB]]
    ppermute x6, waiting for transfers between devices: 5.99 us -> 0.02 us  [reduce_rows(): lax.ppermute(sent, axis, [(i, i ^ m * stride) for i in range(size)])]
    all_to_all x1 -> x0, starting transfers between devices: 4.91 us -> none  [per_device(): lax.all_to_all(join_send, 'dp', split_axis=0, concat_axis=0, tiled=True)]
  transfers between devices with their start and end apart: 8 -> 19, of which waited for: 3 -> 8; matrix products, arithmetic and copies ran while one was open for 0% -> 9% of each run, Pallas kernels for 8% -> 11%
where the time goes in v3:
time: 157 us
  waiting for transfers between devices  82.3 us (52%)
  starting transfers between devices  32 us (20%)
  Pallas kernels  21.1 us (13%)
  local copies, waits for them, and re-layouts  12.4 us (8%)
  other arithmetic  7.96 us (5%)
    ppermute x12, waiting for transfers between devices, swap(): lax.ppermute(block, axis, [(i, i ^ m * stride) for i in range(size)])  78.3 us
    ppermute x12, starting transfers between devices, swap(): lax.ppermute(block, axis, [(i, i ^ m * stride) for i in range(size)])  19.9 us
    concatenate x8, other arithmetic, per_device(): jnp.concatenate([got[j * SUB:(j + 1) * SUB] for got in plane_got], axis=0)  7.24 us
    all_to_all x1, starting transfers between devices, per_device(): lax.all_to_all(cot_send, 'dp', split_axis=0, concat_axis=0, tiled=True)  6.7 us
    pallas_call x1, Pallas kernels, per_device(): call(functools.partial(join_kernel, groups, capacity), 'join_layers', [vm...  6.42 us
    slice x7, local copies, waits for them, and re-layouts, per_device(): got[j * SUB:(j + 1) * SUB]  6.16 us
    pallas_call x2, Pallas kernels, per_device(): call(functools.partial(place_kernel, groups, capacity, first), 'place_joi...  5.73 us
    unnamed x26, local copies, waits for them, and re-layouts  5.61 us
  transfers between devices with their start and end apart: 19, of which 8 were waited for; matrix products, arithmetic and copies ran while one was open for 9% of the time, Pallas kernels for 11%

profile of v3, /device:TPU:13, one launch (start us, length us, event | category | flops | bytes accessed | tf_op | source)
XLA Modules:
  0.0 156.7 jit_solution(987971628058177140)
XLA Ops:
  0.6 4.4 %pack_cotangent.1 = bf16[128,12544]{1,0:T(8,128)(2,1)} custom-call(s32[1,128]{1,0:T(1,128)} %bitcast.4, bf16[128,128]{1,0:T(8,128)(2,1)} %logit_hbm.1, bf16[192,8192]{1,0:T(8,128)(2,1)} %cot_hbm.1), custom_call_target="tpu_custom_call" | custom-call | flops 805306368 | bytes 6291456 | tf_op jit(solution)/shard_map/pack_cotangent/pallas_call | solution.py:370
  5.1 6.7 %all-to-all-start = ((bf16[16,8,12544]{2,1,0:T(8,128)(2,1)}), bf16[16,8,12544]{2,1,0:T(8,128)(2,1)S(1)}, u32[]{:S(2)}, u32[]{:S(2)}) async-start(bf16[16,8,12544]{2,1,0:T(8,128)(2,1)} %bitcast.7), calls=%async_computation | async-start | bytes 6422528 | tf_op jit(solution)/shard_map/all_to_all | solution.py:392
  11.8 2.8 %copy-done = bf16[128,24576]{1,0:T(8,128)(2,1)S(1)} copy-done((bf16[128,24576]{1,0:T(8,128)(2,1)S(1)}, bf16[128,24576]{1,0:T(8,128)(2,1)}, u32[]{:S(2)}) %copy-start) | copy-done | bytes 6291480
  14.6 6.4 %join_layers.1 = (bf16[32,6144]{1,0:T(8,128)(2,1)S(1)}, bf16[32,6144]{1,0:T(8,128)(2,1)}, bf16[32,6144]{1,0:T(8,128)(2,1)}, bf16[32,6144]{1,0:T(8,128)(2,1)S(1)}...) custom-call(s32[1,128]{1,0:T(1,128)S(1)} %bitcast.5, ...), custom_call_target="tpu_custom_call" | custom-call | flops 536870912 | bytes 9437184 | tf_op jit(solution)/shard_map/join_layers/pallas_call | solution.py:396
  21.0 0.4 collective-permute-start
  21.4 0.3 collective-permute-start.1
  21.7 1.5 collective-permute-start.2
  23.2 0.1 collective-permute-start.6
  23.3 0.3 collective-permute-start.7
  23.6 0.8 fusion
  24.4 1.8 %collective-permute-start.8 = (bf16[32,6144]{1,0:T(8,128)(2,1)}, bf16[32,6144]{1,0:T(8,128)(2,1)S(1)}, u32[]{:S(2)}, u32[]{:S(2)}) collective-permute-start(bf16[32,6144]{1,0:T(8,128)(2,1)} %copy-done.6), channel_id=1, source_target_pairs={{0,3},{1,2},{2,1},{3,0},{4,7},{5,6},{6,5},{7,4},{8,11},{9,10},{10,... | collective-permute-start | bytes 1179656 | tf_op jit(solution)/shard_map/ppermute | solution.py:334
  26.3 1.1 fusion.5
  27.4 11.4 %collective-permute-done.1 = bf16[32,6144]{1,0:T(8,128)(2,1)} collective-permute-done((bf16[32,6144]{1,0:T(8,128)(2,1)}, bf16[32,6144]{1,0:T(8,128)(2,1)}, u32[]{:S(2)}, u32[]{:S(2)}) %collective-permute-start.1) | collective-permute-done | bytes 393248 | tf_op jit(solution)/shard_map/ppermute | solution.py:334
  38.8 1.1 fusion.6
  39.9 12.5 %collective-permute-done.2 = bf16[32,6144]{1,0:T(8,128)(2,1)} collective-permute-done((bf16[32,6144]{1,0:T(8,128)(2,1)}, bf16[32,6144]{1,0:T(8,128)(2,1)}, u32[]{:S(2)}, u32[]{:S(2)}) %collective-permute-start.2) | collective-permute-done | bytes 393248 | tf_op jit(solution)/shard_map/ppermute | solution.py:334
  52.3 1.1 fusion.7
  53.4 1.7 %pad_maximum_fusion.1 = bf16[32,6144]{1,0:T(8,128)(2,1)} fusion(bf16[8,6144]{1,0:T(8,128)(2,1)S(1)} %get-tuple-element.58, bf16[8,6144]{1,0:T(8,128)(2,1)S(1)} %get-tuple-element.54, bf16[8,6144]{1,0:T(8,128)(2,1)S(1)} %get-tuple-element.50, bf16[8,6144]{1,0:T(8,128)(2,1)} %get-tuple-element.67), kind=kLoop, calls=%fused_computation.1 | loop fusion | flops 1572864 | bytes 786432 | tf_op jit(solution)/shard_map/concatenate | solution.py:414
  55.1 8.2 %collective-permute-start.3 = (bf16[32,6144]{1,0:T(8,128)(2,1)}, bf16[32,6144]{1,0:T(8,128)(2,1)}, u32[]{:S(2)}, u32[]{:S(2)}) collective-permute-start(bf16[32,6144]{1,0:T(8,128)(2,1)} %pad_maximum_fusion.1), channel_id=1, source_target_pairs={{0,4},{1,5},{2,6},{3,7},{4,0},{5,1},{6,2},{7,3},{8,12},{9,13},{10,... | collective-permute-start | bytes 1179656 | tf_op jit(solution)/shard_map/ppermute | solution.py:334
  63.4 0.8 pad_maximum_fusion.2
  64.1 0.6 collective-permute-start.4
  64.7 1.1 fusion.1
  65.8 2.7 %collective-permute-done.7 = bf16[32,6144]{1,0:T(8,128)(2,1)} collective-permute-done((bf16[32,6144]{1,0:T(8,128)(2,1)}, bf16[32,6144]{1,0:T(8,128)(2,1)}, u32[]{:S(2)}, u32[]{:S(2)}) %collective-permute-start.7) | collective-permute-done | bytes 393248 | tf_op jit(solution)/shard_map/ppermute | solution.py:334
  68.5 1.1 fusion.2
  69.6 7.8 %collective-permute-done.8 = bf16[32,6144]{1,0:T(8,128)(2,1)S(1)} collective-permute-done((bf16[32,6144]{1,0:T(8,128)(2,1)}, bf16[32,6144]{1,0:T(8,128)(2,1)S(1)}, u32[]{:S(2)}, u32[]{:S(2)}) %collective-permute-start.8) | collective-permute-done | bytes 393248 | tf_op jit(solution)/shard_map/ppermute | solution.py:334
  77.5 0.8 pad_maximum_fusion.5
  78.3 4.4 %collective-permute-start.9 = (bf16[32,6144]{1,0:T(8,128)(2,1)}, bf16[32,6144]{1,0:T(8,128)(2,1)}, u32[]{:S(2)}, u32[]{:S(2)}) collective-permute-start(bf16[32,6144]{1,0:T(8,128)(2,1)} %pad_maximum_fusion.5), channel_id=1, source_target_pairs={{0,4},{1,5},{2,6},{3,7},{4,0},{5,1},{6,2},{7,3},{8,12},{9,13},{10,... | collective-permute-start | bytes 1179656 | tf_op jit(solution)/shard_map/ppermute | solution.py:334
  82.6 0.8 pad_maximum_fusion.6
  83.4 2.0 %collective-permute-start.10 = (bf16[32,6144]{1,0:T(8,128)(2,1)}, bf16[32,6144]{1,0:T(8,128)(2,1)}, u32[]{:S(2)}, u32[]{:S(2)}) collective-permute-start(bf16[32,6144]{1,0:T(8,128)(2,1)} %pad_maximum_fusion.6), channel_id=1, source_target_pairs={{0,8},{1,9},{2,10},{3,11},{4,12},{5,13},{6,14},{7,15},{8,0},{9,1},... | collective-permute-start | bytes 1179656 | tf_op jit(solution)/shard_map/ppermute | solution.py:334
  85.4 0.8 pad_maximum_fusion.7
  86.3 0.8 pad_maximum_fusion.3
  87.0 0.8 pad_maximum_fusion.refs_0_
  87.8 0.8 pad_maximum_fusion.4.refs_0_
  88.6 4.0 %all-to-all-done = bf16[16,8,12544]{2,1,0:T(8,128)(2,1)S(1)} async-done(((bf16[16,8,12544]{2,1,0:T(8,128)(2,1)}), bf16[16,8,12544]{2,1,0:T(8,128)(2,1)S(1)}, u32[]{:S(2)}, u32[]{:S(2)}) %all-to-all-start) | async-done | bytes 3211296 | tf_op jit(solution)/shard_map/all_to_all | solution.py:392
  92.6 2.8 %copy-done.1 = bf16[128,24576]{1,0:T(8,128)(2,1)S(1)} copy-done((bf16[128,24576]{1,0:T(8,128)(2,1)S(1)}, bf16[128,24576]{1,0:T(8,128)(2,1)}, u32[]{:S(2)}) %copy-start.1) | copy-done | bytes 6291480
  95.4 4.5 %gain_partials.1 = (f32[16,1536]{1,0:T(8,128)S(1)}, bf16[192,128]{1,0:T(8,128)(2,1)}, f32[192,1]{1,0:T(8,128)S(1)}) custom-call(s32[1,128]{1,0:T(1,128)S(1)} %bitcast.6, f32[128,128]{1,0:T(8,128)S(1)} %get-tuple-element.24.inv_ref, bf16[128,24576]{1,0:T(8,128)(2,1)S(1)} %copy-done.1, bf16[128,12544]{1,0:T(8,128)(2,1)S(1)} %bitcast.3), custom_call_target="tpu_custom_call" | custom-call | flops 536870912 | bytes 9437184 | tf_op jit(solution)/shard_map/gain_partials/pallas_call | solution.py:417
  100.0 0.1 collective-permute-start.12
  100.1 23.2 %collective-permute-done.10.refs_2_ = bf16[32,6144]{1,0:T(8,128)(2,1)} collective-permute-done((bf16[32,6144]{1,0:T(8,128)(2,1)}, bf16[32,6144]{1,0:T(8,128)(2,1)}, u32[]{:S(2)}, u32[]{:S(2)}) %collective-permute-start.10) | collective-permute-done | bytes 393248 | tf_op jit(solution)/shard_map/ppermute | solution.py:334
  123.3 1.6 collective-permute-start.14
  124.9 9.0 %collective-permute-done.11.refs_3_ = bf16[32,6144]{1,0:T(8,128)(2,1)} collective-permute-done((bf16[32,6144]{1,0:T(8,128)(2,1)}, bf16[32,6144]{1,0:T(8,128)(2,1)}, u32[]{:S(2)}, u32[]{:S(2)}) %collective-permute-start.11) | collective-permute-done | bytes 393248 | tf_op jit(solution)/shard_map/ppermute | solution.py:334
  133.8 0.2 collective-permute-start.13
  134.1 2.9 %place_joined.2.refs_4_ = bf16[192,8192]{1,0:T(8,128)(2,1)} custom-call(bf16[32,6144]{1,0:T(8,128)(2,1)S(1)} %copy-done.2, bf16[32,6144]{1,0:T(8,128)(2,1)} %collective-permute-done.9.refs_1_, bf16[32,6144]{1,0:T(8,128)(2,1)} %collective-permute-done.10.refs_2_, bf16[32,6144]{1,0:T(8,128)(2,1)} %collective-permute-done.11.refs_3_), custom_call_target="tpu_custom_call" | custom-call | flops 402653184 | bytes 3145728 | tf_op jit(solution)/shard_map/place_joined/pallas_call | solution.py:439
  137.0 0.3 collective-permute-start.5
  137.4 1.3 collective-permute-start.17
  138.7 2.2 %collective-permute-start.16 = (f32[1,1536]{1,0:T(1,128)S(1)}, f32[1,1536]{1,0:T(1,128)S(1)}, u32[]{:S(2)}, u32[]{:S(2)}) collective-permute-start(f32[1,1536]{1,0:T(1,128)S(1)} %get-tuple-element.65), channel_id=1, source_target_pairs={{0,8},{1,9},{2,10},{3,11},{4,12},{5,13},{6,14},{7,15},{8,0},{9,1},... | collective-permute-start | bytes 18440 | tf_op jit(solution)/shard_map/ppermute | solution.py:348
  140.9 11.6 %collective-permute-done.5.refs_3_ = bf16[32,6144]{1,0:T(8,128)(2,1)S(1)} collective-permute-done((bf16[32,6144]{1,0:T(8,128)(2,1)S(1)}, bf16[32,6144]{1,0:T(8,128)(2,1)S(1)}, u32[]{:S(2)}, u32[]{:S(2)}) %collective-permute-start.5) | collective-permute-done | bytes 393248 | tf_op jit(solution)/shard_map/ppermute | solution.py:334
  152.6 2.8 %place_joined.3 = bf16[192,8192]{1,0:T(8,128)(2,1)} custom-call(bf16[32,6144]{1,0:T(8,128)(2,1)S(1)} %copy-done.3, bf16[32,6144]{1,0:T(8,128)(2,1)} %collective-permute-done.3.refs_1_, bf16[32,6144]{1,0:T(8,128)(2,1)} %collective-permute-done.4.refs_2_, bf16[32,6144]{1,0:T(8,128)(2,1)S(1)} %collective-permute-done.5.refs_3_, ...), custom_call_target="tpu_custom_call", output_to_operand_aliasing={{}: (4, {})} | custom-call | flops 402653184 | bytes 3145728 | tf_op jit(solution)/shard_map/place_joined/pallas_call | solution.py:439
  155.4 0.7 reduce
  156.1 0.6 reshape.17
  (42 shorter events, 0.3 us)
Async XLA Ops:
  5.1 6.7 %copy-start.4 = (f32[3,8192]{1,0:T(4,128)S(1)}, f32[3,8192]{1,0:T(4,128)}, u32[]{:S(2)}) copy-start(f32[3,8192]{1,0:T(4,128)} %gain_ref.1) | copy-start | bytes 294916
  5.1 6.7 %copy-start.5 = (s32[128,1]{0,1:T(1,128)S(1)}, s32[128,1]{0,1:T(1,128)}, u32[]{:S(2)}) copy-start(s32[128,1]{0,1:T(1,128)} %param.7) | copy-start | bytes 1540
  5.1 87.5 %all-to-all-start = ((bf16[16,8,12544]{2,1,0:T(8,128)(2,1)}), bf16[16,8,12544]{2,1,0:T(8,128)(2,1)S(1)}, u32[]{:S(2)}, u32[]{:S(2)}) async-start(bf16[16,8,12544]{2,1,0:T(8,128)(2,1)} %bitcast.7), calls=%async_computation | async-start | bytes 6422528 | tf_op jit(solution)/shard_map/all_to_all | solution.py:392
  11.8 2.8 %copy-start = (bf16[128,24576]{1,0:T(8,128)(2,1)S(1)}, bf16[128,24576]{1,0:T(8,128)(2,1)}, u32[]{:S(2)}) copy-start(bf16[128,24576]{1,0:T(8,128)(2,1)} %feat_hbm.3) | copy-start | bytes 18874372
  21.0 3.4 %copy-start.6 = (bf16[32,6144]{1,0:T(8,128)(2,1)}, bf16[32,6144]{1,0:T(8,128)(2,1)S(1)}, u32[]{:S(2)}) copy-start(bf16[32,6144]{1,0:T(8,128)(2,1)S(1)} %get-tuple-element.23) | copy-start | bytes 1179652
  21.0 3.4 %collective-permute-start = (bf16[32,6144]{1,0:T(8,128)(2,1)}, bf16[32,6144]{1,0:T(8,128)(2,1)}, u32[]{:S(2)}, u32[]{:S(2)}) collective-permute-start(bf16[32,6144]{1,0:T(8,128)(2,1)} %get-tuple-element.17), channel_id=1, source_target_pairs={{0,1},{1,0},{2,3},{3,2},{4,5},{5,4},{6,7},{7,6},{8,9},{9,8},{10,11... | collective-permute-start | bytes 1179656 | tf_op jit(solution)/shard_map/ppermute | solution.py:334
  21.4 17.3 %collective-permute-start.1 = (bf16[32,6144]{1,0:T(8,128)(2,1)}, bf16[32,6144]{1,0:T(8,128)(2,1)}, u32[]{:S(2)}, u32[]{:S(2)}) collective-permute-start(bf16[32,6144]{1,0:T(8,128)(2,1)} %get-tuple-element.18), channel_id=1, source_target_pairs={{0,2},{1,3},{2,0},{3,1},{4,6},{5,7},{6,4},{7,5},{8,10},{9,11},{10,... | collective-permute-start | bytes 1179656 | tf_op jit(solution)/shard_map/ppermute | solution.py:334
  21.7 30.6 %collective-permute-start.2 = (bf16[32,6144]{1,0:T(8,128)(2,1)}, bf16[32,6144]{1,0:T(8,128)(2,1)}, u32[]{:S(2)}, u32[]{:S(2)}) collective-permute-start(bf16[32,6144]{1,0:T(8,128)(2,1)} %get-tuple-element.19), channel_id=1, source_target_pairs={{0,3},{1,2},{2,1},{3,0},{4,7},{5,6},{6,5},{7,4},{8,11},{9,10},{10,... | collective-permute-start | bytes 1179656 | tf_op jit(solution)/shard_map/ppermute | solution.py:334
  23.2 41.5 %collective-permute-start.6 = (bf16[32,6144]{1,0:T(8,128)(2,1)}, bf16[32,6144]{1,0:T(8,128)(2,1)}, u32[]{:S(2)}, u32[]{:S(2)}) collective-permute-start(bf16[32,6144]{1,0:T(8,128)(2,1)} %get-tuple-element.21), channel_id=1, source_target_pairs={{0,1},{1,0},{2,3},{3,2},{4,5},{5,4},{6,7},{7,6},{8,9},{9,8},{10,11... | collective-permute-start | bytes 1179656 | tf_op jit(solution)/shard_map/ppermute | solution.py:334
  23.3 45.2 %collective-permute-start.7 = (bf16[32,6144]{1,0:T(8,128)(2,1)}, bf16[32,6144]{1,0:T(8,128)(2,1)}, u32[]{:S(2)}, u32[]{:S(2)}) collective-permute-start(bf16[32,6144]{1,0:T(8,128)(2,1)} %get-tuple-element.22), channel_id=1, source_target_pairs={{0,2},{1,3},{2,0},{3,1},{4,6},{5,7},{6,4},{7,5},{8,10},{9,11},{10,... | collective-permute-start | bytes 1179656 | tf_op jit(solution)/shard_map/ppermute | solution.py:334
  24.4 38.9 %copy-start.11 = (bf16[8,6144]{1,0:T(8,128)(2,1)S(1)}, bf16[8,6144]{1,0:T(8,128)(2,1)}, u32[]{:S(2)}) copy-start(bf16[8,6144]{1,0:T(8,128)(2,1)} %get-tuple-element.68) | copy-start | bytes 294916
  24.4 53.0 %copy-start.10 = (bf16[8,6144]{1,0:T(8,128)(2,1)S(1)}, bf16[8,6144]{1,0:T(8,128)(2,1)}, u32[]{:S(2)}) copy-start(bf16[8,6144]{1,0:T(8,128)(2,1)} %get-tuple-element.30) | copy-start | bytes 294916
  24.4 53.0 %collective-permute-start.8 = (bf16[32,6144]{1,0:T(8,128)(2,1)}, bf16[32,6144]{1,0:T(8,128)(2,1)S(1)}, u32[]{:S(2)}, u32[]{:S(2)}) collective-permute-start(bf16[32,6144]{1,0:T(8,128)(2,1)} %copy-done.6), channel_id=1, source_target_pairs={{0,3},{1,2},{2,1},{3,0},{4,7},{5,6},{6,5},{7,4},{8,11},{9,10},{10,... | collective-permute-start | bytes 1179656 | tf_op jit(solution)/shard_map/ppermute | solution.py:334
  27.4 55.3 %copy-start.9 = (bf16[8,6144]{1,0:T(8,128)(2,1)S(1)}, bf16[8,6144]{1,0:T(8,128)(2,1)}, u32[]{:S(2)}) copy-start(bf16[8,6144]{1,0:T(8,128)(2,1)} %get-tuple-element.29) | copy-start | bytes 294916
  39.8 45.6 %copy-start.8 = (bf16[8,6144]{1,0:T(8,128)(2,1)S(1)}, bf16[8,6144]{1,0:T(8,128)(2,1)}, u32[]{:S(2)}) copy-start(bf16[8,6144]{1,0:T(8,128)(2,1)} %get-tuple-element.28) | copy-start | bytes 294916
  53.4 32.9 %copy-start.7 = (bf16[8,6144]{1,0:T(8,128)(2,1)S(1)}, bf16[8,6144]{1,0:T(8,128)(2,1)}, u32[]{:S(2)}) copy-start(bf16[8,6144]{1,0:T(8,128)(2,1)} %get-tuple-element.69) | copy-start | bytes 294916
  55.1 83.6 %collective-permute-start.3 = (bf16[32,6144]{1,0:T(8,128)(2,1)}, bf16[32,6144]{1,0:T(8,128)(2,1)}, u32[]{:S(2)}, u32[]{:S(2)}) collective-permute-start(bf16[32,6144]{1,0:T(8,128)(2,1)} %pad_maximum_fusion.1), channel_id=1, source_target_pairs={{0,4},{1,5},{2,6},{3,7},{4,0},{5,1},{6,2},{7,3},{8,12},{9,13},{10,... | collective-permute-start | bytes 1179656 | tf_op jit(solution)/shard_map/ppermute | solution.py:334
  64.1 76.8 %collective-permute-start.4 = (bf16[32,6144]{1,0:T(8,128)(2,1)}, bf16[32,6144]{1,0:T(8,128)(2,1)}, u32[]{:S(2)}, u32[]{:S(2)}) collective-permute-start(bf16[32,6144]{1,0:T(8,128)(2,1)} %pad_maximum_fusion.2), channel_id=1, source_target_pairs={{0,8},{1,9},{2,10},{3,11},{4,12},{5,13},{6,14},{7,15},{8,0},{9,1},... | collective-permute-start | bytes 1179656 | tf_op jit(solution)/shard_map/ppermute | solution.py:334
  78.3 21.7 %collective-permute-start.9 = (bf16[32,6144]{1,0:T(8,128)(2,1)}, bf16[32,6144]{1,0:T(8,128)(2,1)}, u32[]{:S(2)}, u32[]{:S(2)}) collective-permute-start(bf16[32,6144]{1,0:T(8,128)(2,1)} %pad_maximum_fusion.5), channel_id=1, source_target_pairs={{0,4},{1,5},{2,6},{3,7},{4,0},{5,1},{6,2},{7,3},{8,12},{9,13},{10,... | collective-permute-start | bytes 1179656 | tf_op jit(solution)/shard_map/ppermute | solution.py:334
  83.4 39.9 %collective-permute-start.10 = (bf16[32,6144]{1,0:T(8,128)(2,1)}, bf16[32,6144]{1,0:T(8,128)(2,1)}, u32[]{:S(2)}, u32[]{:S(2)}) collective-permute-start(bf16[32,6144]{1,0:T(8,128)(2,1)} %pad_maximum_fusion.6), channel_id=1, source_target_pairs={{0,8},{1,9},{2,10},{3,11},{4,12},{5,13},{6,14},{7,15},{8,0},{9,1},... | collective-permute-start | bytes 1179656 | tf_op jit(solution)/shard_map/ppermute | solution.py:334
  86.3 47.6 %collective-permute-start.11 = (bf16[32,6144]{1,0:T(8,128)(2,1)}, bf16[32,6144]{1,0:T(8,128)(2,1)}, u32[]{:S(2)}, u32[]{:S(2)}) collective-permute-start(bf16[32,6144]{1,0:T(8,128)(2,1)} %pad_maximum_fusion.7), channel_id=1, source_target_pairs={{0,12},{1,13},{2,14},{3,15},{4,8},{5,9},{6,10},{7,11},{8,4},{9,5},... | collective-permute-start | bytes 1179656 | tf_op jit(solution)/shard_map/ppermute | solution.py:334
  92.6 2.8 %copy-start.1 = (bf16[128,24576]{1,0:T(8,128)(2,1)S(1)}, bf16[128,24576]{1,0:T(8,128)(2,1)}, u32[]{:S(2)}) copy-start(bf16[128,24576]{1,0:T(8,128)(2,1)} %feat_hbm.3) | copy-start | bytes 18874372
  95.4 38.7 %copy-start.2 = (bf16[32,6144]{1,0:T(8,128)(2,1)S(1)}, bf16[32,6144]{1,0:T(8,128)(2,1)}, u32[]{:S(2)}) copy-start(bf16[32,6144]{1,0:T(8,128)(2,1)} %pad_maximum_fusion.4.refs_0_) | copy-start | bytes 1179652
  99.9 37.1 %copy-start.12 = (bf16[32,6144]{1,0:T(8,128)(2,1)S(1)}, bf16[32,6144]{1,0:T(8,128)(2,1)}, u32[]{:S(2)}) copy-start(bf16[32,6144]{1,0:T(8,128)(2,1)} %pad_maximum_fusion.3) | copy-start | bytes 1179652
  99.9 52.6 %copy-start.3 = (bf16[32,6144]{1,0:T(8,128)(2,1)S(1)}, bf16[32,6144]{1,0:T(8,128)(2,1)}, u32[]{:S(2)}) copy-start(bf16[32,6144]{1,0:T(8,128)(2,1)} %pad_maximum_fusion.refs_0_) | copy-start | bytes 1179652
  100.0 37.0 %collective-permute-start.12 = (f32[4,1536]{1,0:T(4,128)S(1)}, f32[4,1536]{1,0:T(4,128)S(1)}, u32[]{:S(2)}, u32[]{:S(2)}) collective-permute-start(f32[4,1536]{1,0:T(4,128)S(1)} %get-tuple-element.60), channel_id=1, source_target_pairs={{0,1},{1,0},{2,3},{3,2},{4,5},{5,4},{6,7},{7,6},{8,9},{9,8},{10,11... | collective-permute-start | bytes 73736 | tf_op jit(solution)/shard_map/ppermute | solution.py:348
  123.3 14.0 %collective-permute-start.14 = (f32[4,1536]{1,0:T(4,128)S(1)}, f32[4,1536]{1,0:T(4,128)S(1)}, u32[]{:S(2)}, u32[]{:S(2)}) collective-permute-start(f32[4,1536]{1,0:T(4,128)S(1)} %get-tuple-element.61), channel_id=1, source_target_pairs={{0,3},{1,2},{2,1},{3,0},{4,7},{5,6},{6,5},{7,4},{8,11},{9,10},{10,... | collective-permute-start | bytes 73736 | tf_op jit(solution)/shard_map/ppermute | solution.py:348
  133.8 3.4 %collective-permute-start.13 = (f32[4,1536]{1,0:T(4,128)S(1)}, f32[4,1536]{1,0:T(4,128)S(1)}, u32[]{:S(2)}, u32[]{:S(2)}) collective-permute-start(f32[4,1536]{1,0:T(4,128)S(1)} %get-tuple-element.62), channel_id=1, source_target_pairs={{0,2},{1,3},{2,0},{3,1},{4,6},{5,7},{6,4},{7,5},{8,10},{9,11},{10,... | collective-permute-start | bytes 73736 | tf_op jit(solution)/shard_map/ppermute | solution.py:348
  137.0 15.5 %collective-permute-start.5 = (bf16[32,6144]{1,0:T(8,128)(2,1)S(1)}, bf16[32,6144]{1,0:T(8,128)(2,1)S(1)}, u32[]{:S(2)}, u32[]{:S(2)}) collective-permute-start(bf16[32,6144]{1,0:T(8,128)(2,1)S(1)} %copy-done.12), channel_id=1, source_target_pairs={{0,12},{1,13},{2,14},{3,15},{4,8},{5,9},{6,10},{7,11},{8,4},{9,5},... | collective-permute-start | bytes 1179656 | tf_op jit(solution)/shard_map/ppermute | solution.py:334
  137.3 18.7 %collective-permute-start.15 = (f32[1,1536]{1,0:T(1,128)S(1)}, f32[1,1536]{1,0:T(1,128)S(1)}, u32[]{:S(2)}, u32[]{:S(2)}) collective-permute-start(f32[1,1536]{1,0:T(1,128)S(1)} %get-tuple-element.63), channel_id=1, source_target_pairs={{0,4},{1,5},{2,6},{3,7},{4,0},{5,1},{6,2},{7,3},{8,12},{9,13},{10,... | collective-permute-start | bytes 18440 | tf_op jit(solution)/shard_map/ppermute | solution.py:348
  137.4 18.7 %collective-permute-start.17 = (f32[1,1536]{1,0:T(1,128)S(1)}, f32[1,1536]{1,0:T(1,128)S(1)}, u32[]{:S(2)}, u32[]{:S(2)}) collective-permute-start(f32[1,1536]{1,0:T(1,128)S(1)} %get-tuple-element.64), channel_id=1, source_target_pairs={{0,12},{1,13},{2,14},{3,15},{4,8},{5,9},{6,10},{7,11},{8,4},{9,5},... | collective-permute-start | bytes 18440 | tf_op jit(solution)/shard_map/ppermute | solution.py:348
  138.7 17.3 %collective-permute-start.16 = (f32[1,1536]{1,0:T(1,128)S(1)}, f32[1,1536]{1,0:T(1,128)S(1)}, u32[]{:S(2)}, u32[]{:S(2)}) collective-permute-start(f32[1,1536]{1,0:T(1,128)S(1)} %get-tuple-element.65), channel_id=1, source_target_pairs={{0,8},{1,9},{2,10},{3,11},{4,12},{5,13},{6,14},{7,15},{8,0},{9,1},... | collective-permute-start | bytes 18440 | tf_op jit(solution)/shard_map/ppermute | solution.py:348

commit v4 on v2

--- a/solution.py
+++ b/solution.py
@@ -11,6 +11,8 @@
 SUB = 8
 GROUP = 2048
 LANES = 128
+QUARTERS = 4
+CORES = 2
 VMEM_LIMIT = 20 * 1024 * 1024
 VMEM_WHOLE = 56 * 1024 * 1024
 
@@ -120,8 +122,9 @@
 
 
 def cot_kernel(
-    groups, capacity, dest_hbm, logit_hbm, cot_hbm, out_hbm, dest_v, logit_v, cot_v, out_v, log_v, dest_sem, logit_sem, in_sem, out_sem, log_sem
+    groups, capacity, dest_hbm, logit_hbm, cot_hbm, *refs
 ):
+    out_hbm, dest_v, logit_v, cot_v, out_v, log_v, dest_sem, logit_sem, in_sem, out_sem, log_sem = refs
     count, slots, group = cot_v.shape
     packed = out_v.shape[2]
     loads = [pltpu.make_async_copy(cols(cot_hbm, g, group), cot_v.at[g], in_sem.at[g]) for g in range(count)]
@@ -142,32 +145,41 @@
     log_store = pltpu.make_async_copy(log_v, out_hbm.at[:, count * packed : count * packed + log_v.shape[1]], log_sem)
     log_store.start()
     slot = iota((1, slots), 1)
-    matrices = pack_matrices(slot // capacity, slot % capacity, groups, capacity)
+    matrices = pack_matrices(lax.div(slot, capacity), lax.rem(slot, capacity), groups, capacity)
     for g in range(count):
         loads[g].wait()
         base = 0
-        for block in pack_group(cot_v[g], matrices, capacity):
-            out_v[g, :, base : base + block.shape[1]] = block
-            base += block.shape[1]
+        for packed_block in pack_group(cot_v[g], matrices, capacity):
+            out_v[g, :, base : base + packed_block.shape[1]] = packed_block
+            base += packed_block.shape[1]
         stores[g].start()
-    for store in stores:
+    for store in stores + [log_store]:
         store.wait()
-    log_store.wait()
-
-
-def join_kernel(groups, capacity, dest_ref, gain_ref, feat_hbm, out_hbm, inv_ref, feat_v, out_v, in_sem, out_sem):
+
+
+def join_kernel(groups, capacity, dest_ref, gain_ref, feat_hbm, *refs):
+    *outs, inv_ref, feat_v, out_v, in_sem, out_sem = refs
     layers, count, tokens, group = feat_v.shape
     width = count * group
     packed = out_v.shape[2]
+    part = out_v.shape[1] // CORES
     loads = [
         [pltpu.make_async_copy(cols(feat_hbm, l * count + g, group), feat_v.at[l, g], in_sem.at[l, g]) for g in range(count)]
         for l in range(layers)
     ]
-    stores = [pltpu.make_async_copy(out_v.at[g], cols(out_hbm, g, packed), out_sem.at[g]) for g in range(count)]
+    stores = [
+        [
+            pltpu.make_async_copy(out_v.at[g, q * part : (q + 1) * part], cols(outs[q], g, packed), out_sem.at[g, q])
+            for q in range(CORES)
+        ]
+        for g in range(count)
+    ]
     for row in loads:
         for load in row:
             load.start()
     target, rank, _, _ = ranks_of(dest_ref[...])
+    target = target ^ lax.axis_index("dp")
+    target = lax.rem(target, CORES) * (groups // CORES) + lax.div(target, CORES)
     matrices = pack_matrices(target, rank, groups, capacity)
     lane = iota((tokens, LANES), 1)
     inv_all = jnp.zeros((tokens, LANES), jnp.float32)
@@ -193,9 +205,47 @@
         for block in pack_group(joined.astype(jnp.bfloat16), matrices, capacity):
             out_v[g, :, base : base + block.shape[1]] = block
             base += block.shape[1]
-        stores[g].start()
-    for store in stores:
-        store.wait()
+        for store in stores[g]:
+            store.start()
+    for row in stores:
+        for store in row:
+            store.wait()
+
+
+def sort_kernel(chips, held, *refs):
+    gots, outs, (got_v, out_v, in_sem, out_sem) = refs[:CORES], refs[CORES:-4], refs[-4:]
+    count, rows, packed = got_v.shape
+    own, part = chips * SUB, CORES * SUB
+    loads = [
+        [pltpu.make_async_copy(cols(got, g, packed), got_v.at[g, q * own : (q + 1) * own], in_sem.at[g, q]) for q, got in enumerate(gots)]
+        for g in range(count)
+    ]
+    stores = [
+        [
+            pltpu.make_async_copy(
+                out_v.at[g, j * part : (j + 1) * part],
+                outs[array].at[pl.ds(row, part), g * packed : (g + 1) * packed],
+                out_sem.at[g, j],
+            )
+            for j, (array, row) in enumerate(held)
+        ]
+        for g in range(count)
+    ]
+    for row in loads:
+        for load in row:
+            load.start()
+    at, come = iota((rows, rows), 0), iota((rows, rows), 1)
+    chip, core, rank = lax.div(at, part), lax.rem(lax.div(at, SUB), CORES), lax.rem(at, SUB)
+    matrix = hot(come == core * own + chip * SUB + rank)
+    for g in range(count):
+        for load in loads[g]:
+            load.wait()
+        out_v[g] = select(matrix, got_v[g])
+        for store in stores[g]:
+            store.start()
+    for row in stores:
+        for store in row:
+            store.wait()
 
 
 def grad_kernel(
@@ -203,7 +253,7 @@
 ):
     layers, count, tokens, group = feat_v.shape
     packed = got_v.shape[2]
-    own = grad_ref.shape[1] // layers
+    own = grad_ref.shape[2]
     order = exchange_order(groups)
     log_load = pltpu.make_async_copy(got_hbm.at[:, count * packed : count * packed + log_v.shape[1]], log_v, log_sem)
     log_load.start()
@@ -231,13 +281,12 @@
                 part = jnp.sum(x * inv_ref[:, l : l + 1] * cot, axis=0, keepdims=True)
                 for u in range(wide // step):
                     at = g * group + b * wide + u * step
-                    lo = l * own + at % own
-                    row = order[at // own]
-                    grad_ref[row : row + 1, lo : lo + step] = part[:, u * step : (u + 1) * step]
+                    lo = at % own
+                    grad_ref[order[at // own], l : l + 1, lo : lo + step] = part[:, u * step : (u + 1) * step]
     log_load.wait()
     slots = soft_ref.shape[0]
     slot = iota((slots, 1), 0)
-    target, rank = slot // capacity, slot % capacity
+    target, rank = lax.div(slot, capacity), lax.rem(slot, capacity)
     shape = (slots, groups * SUB)
     logits = jnp.zeros((slots, LANES), jnp.float32)
     for m in range(log_v.shape[1] // LANES):
@@ -245,26 +294,47 @@
         logits = logits + jnp.dot(place, log_v[:, m * LANES : (m + 1) * LANES], preferred_element_type=jnp.float32)
     top = jnp.max(logits, axis=1, keepdims=True)
     partition = top + jnp.log(jnp.sum(jnp.exp(logits - top), axis=1, keepdims=True))
-    part_ref[...] = partition
+    part_ref[...] = jnp.broadcast_to(partition, logits.shape).T[:1]
     soft_ref[...] = jnp.exp(logits - partition).astype(jnp.bfloat16)
 
 
-def place_kernel(groups, capacity, got_hbm, out_hbm, got_v, out_v, in_sem, out_sem):
-    count, slots, group = out_v.shape
-    packed = got_v.shape[2]
-    loads = [pltpu.make_async_copy(cols(got_hbm, g, packed), got_v.at[g], in_sem.at[g]) for g in range(count)]
-    stores = [pltpu.make_async_copy(out_v.at[g], cols(out_hbm, g, group), out_sem.at[g]) for g in range(count)]
-    for load in loads:
-        load.start()
-    slot = iota((slots, 1), 0)
-    matrices = unpack_matrices(slot // capacity, slot % capacity, groups, capacity)
-    for g in range(count):
-        loads[g].wait()
-        blocks = unpack_group(got_v[g], matrices, capacity, group)
-        wide = group // len(blocks)
-        for b, block in enumerate(blocks):
-            out_v[g, :, b * wide : (b + 1) * wide] = block.astype(jnp.bfloat16)
-        stores[g].start()
+def place_kernel(groups, capacity, away, found, *refs):
+    chips = groups // QUARTERS // CORES
+    gots, (out_hbm, got_v, out_v, in_sem, out_sem) = refs[:-5], refs[-5:]
+    _, count, held, group = out_v.shape
+    packed = got_v.shape[3]
+    part = CORES * SUB
+    me = lax.axis_index("dp")
+    quarter, within = lax.div(me, groups // QUARTERS), lax.rem(me, groups // QUARTERS)
+    loads, stores = [], []
+    for a, j in enumerate(away):
+        rows = pl.ds(pl.multiple_of((quarter ^ j) * held, held), held)
+        for g in range(count):
+            loads.append(
+                [
+                    pltpu.make_async_copy(
+                        gots[array].at[pl.ds(row, part), g * packed : (g + 1) * packed],
+                        got_v.at[a, g, i * part : (i + 1) * part],
+                        in_sem.at[a, g, i],
+                    )
+                    for i, (array, row) in enumerate(found[a * chips : (a + 1) * chips])
+                ]
+            )
+            stores.append(pltpu.make_async_copy(out_v.at[a, g], out_hbm.at[rows, g * group : (g + 1) * group], out_sem.at[a, g]))
+    for row in loads:
+        for load in row:
+            load.start()
+    slot = iota((held, 1), 0)
+    matrices = unpack_matrices(lax.div(slot, capacity) ^ within, lax.rem(slot, capacity), groups // QUARTERS, capacity)
+    for a in range(len(away)):
+        for g in range(count):
+            for load in loads[a * count + g]:
+                load.wait()
+            blocks = unpack_group(got_v[a, g], matrices, capacity, group)
+            wide = group // len(blocks)
+            for b, block in enumerate(blocks):
+                out_v[a, g, :, b * wide : (b + 1) * wide] = block.astype(jnp.bfloat16)
+            stores[a * count + g].start()
     for store in stores:
         store.wait()
 
@@ -274,7 +344,7 @@
 anywhere = pl.BlockSpec(memory_space=pl.ANY)
 
 
-def call(kernel, name, ins, out_shape, outs, scratch, moved, flops, limit=VMEM_LIMIT):
+def call(kernel, name, ins, out_shape, outs, scratch, moved, flops, limit=VMEM_LIMIT, aliases=None):
     return pl.pallas_call(
         kernel,
         out_shape=out_shape,
@@ -283,8 +353,13 @@
         scratch_shapes=scratch,
         compiler_params=pltpu.CompilerParams(vmem_limit_bytes=limit),
         cost_estimate=pl.CostEstimate(flops=flops, bytes_accessed=moved, transcendentals=0),
+        input_output_aliases=aliases or {},
         name=name,
     )
+
+
+def across(block, axis, bits):
+    return lax.ppermute(block, axis, [(i, i ^ bits) for i in range(lax.axis_size(axis))])
 
 
 def reduce_rows(rows, axis):
@@ -319,6 +394,9 @@
     bf16, f32, dma = jnp.bfloat16, jnp.float32, pltpu.SemaphoreType.DMA
     shape = jax.ShapeDtypeStruct
     dest_row = destination.reshape(1, tokens)
+
+    chips = groups // CORES
+    near = chips // QUARTERS
 
     cot_send = call(
         functools.partial(cot_kernel, groups, capacity),
@@ -342,30 +420,58 @@
         2 * rows * slots * width * 2,
         VMEM_WHOLE,
     )(dest_row, target_logits, joined_cotangent)
+
     cot_got = lax.all_to_all(cot_send, "dp", split_axis=0, concat_axis=0, tiled=True)
 
-    join_send, inverse = call(
+    *join_send, inverse = call(
         functools.partial(join_kernel, groups, capacity),
         "join_layers",
         [vmem, vmem, hbm],
-        (shape((rows, count * packed), bf16), shape((tokens, LANES), f32)),
-        (hbm, vmem),
+        (shape((chips * SUB, count * packed), bf16),) * CORES + (shape((tokens, LANES), f32),),
+        (hbm,) * CORES + (vmem,),
         [
             pltpu.VMEM((layers, count, tokens, GROUP), bf16),
             pltpu.VMEM((count, rows, packed), bf16),
             dma((layers, count)),
-            dma((count,)),
+            dma((count, CORES)),
         ],
         2 * layers * tokens * width + 2 * slots * width,
         2 * rows * tokens * width * 2,
     )(dest_row, joining_gains, features)
-    join_got = lax.all_to_all(join_send, "dp", split_axis=0, concat_axis=0, tiled=True)
+    part = CORES * SUB
+    relayed = near == 2
+    held = [(0, 0), (1, 0), (2, 0), (1, part)] if relayed else []
+    held += [(k - 1 if relayed else k, 0) for k in range(len(held), chips)]
+    tall = [sum(part for array, _ in held if array == i) for i in range(1 + held[-1][0])]
+    join_sorted = call(
+        functools.partial(sort_kernel, chips, held),
+        "sort_chips",
+        [anywhere] * CORES,
+        tuple(shape((size, count * packed), bf16) for size in tall),
+        (hbm,) * len(tall),
+        [
+            pltpu.VMEM((count, rows, packed), bf16),
+            pltpu.VMEM((count, rows, packed), bf16),
+            dma((count, CORES)),
+            dma((count, chips)),
+        ],
+        4 * slots * width,
+        2 * rows * rows * width,
+    )(join_send[0], across(join_send[1], "dp", 1))
+    if relayed:
+        first = across(join_sorted[1], "dp", CORES)
+        second = across(jnp.concatenate([join_sorted[2], first[part:]], axis=0), "dp", 2 * CORES)
+        join_got = [(join_sorted[0], 0), (first, 0), (second, 0), (second, part)]
+    else:
+        join_got = [(join_sorted[0], 0)]
+    for k in range(len(join_got), chips):
+        join_got.append((across(join_sorted[held[k][0]], "dp", k * CORES), 0))
 
     partial_rows, soft_labels, log_partition = call(
         functools.partial(grad_kernel, groups, capacity),
         "gain_partials",
         [vmem, vmem, hbm, anywhere],
-        (shape((groups, layers * width // groups), f32), shape((slots, kept), bf16), shape((slots, 1), f32)),
+        (shape((groups, layers, width // groups), f32), shape((slots, kept), bf16), shape((1, slots), f32)),
         (vmem, vmem, vmem),
         [
             pltpu.VMEM((layers, count, tokens, GROUP), bf16),
@@ -378,19 +484,36 @@
         2 * layers * tokens * width + 2 * slots * width,
         2 * rows * tokens * width * 2,
     )(dest_row, inverse, features, cot_got)
-    gain_grad = reduce_rows(partial_rows, "dp").reshape(layers, width // groups)
-
-    joined_input = call(
-        functools.partial(place_kernel, groups, capacity),
-        "place_joined",
-        [anywhere],
-        shape((slots, width), bf16),
-        hbm,
-        [pltpu.VMEM((count, rows, packed), bf16), pltpu.VMEM((count, slots, GROUP), bf16), dma((count,)), dma((count,))],
-        4 * slots * width,
-        2 * rows * slots * width * 2,
-    )(join_got)
-    return (joined_input, soft_labels, log_partition[:, 0], gain_grad)
+    gain_grad = reduce_rows(partial_rows, "dp")[0]
+
+    joined_input = ()
+    for away in ((0, 1), (2,), (3,)):
+        parts = [join_got[j * near + i] for j in away for i in range(near)]
+        arrays = []
+        for array, _ in parts:
+            if not any(array is seen for seen in arrays):
+                arrays.append(array)
+        found = [([array is seen for seen in arrays].index(True), row) for array, row in parts]
+        joined_input = (
+            call(
+                functools.partial(place_kernel, groups, capacity, away, found),
+                "place_joined",
+                [anywhere] * (len(arrays) + len(joined_input)),
+                shape((slots, width), bf16),
+                hbm,
+                [
+                    pltpu.VMEM((len(away), count, rows // QUARTERS, packed), bf16),
+                    pltpu.VMEM((len(away), count, slots // QUARTERS, GROUP), bf16),
+                    dma((len(away), count, near)),
+                    dma((len(away), count)),
+                ],
+                slots * width * len(away),
+                rows * slots * width * len(away),
+                aliases={len(arrays): 0} if joined_input else None,
+            )(*arrays, *joined_input),
+        )
+    joined_input = joined_input[0]
+    return (joined_input, soft_labels, log_partition[0], gain_grad)
 
 
 def solution(mesh):

time: 164 us -> 156 us (0.951)
  waiting for transfers between devices: 116 us -> 91.7 us
  Pallas kernels: 17.8 us -> 26.6 us
  starting transfers between devices: 20 us -> 26 us
    ppermute x0 -> x7, waiting for transfers between devices: none -> 76.8 us  [across(): lax.ppermute(block, axis, [(i, i ^ bits) for i in range(lax.axis_size(axi...]
    all_to_all x1 -> x0, waiting for transfers between devices: 48.6 us -> none  [per_device(): lax.all_to_all(join_send, 'dp', split_axis=0, concat_axis=0, tiled=True)]
    all_to_all x1, waiting for transfers between devices: 61.6 us -> 14.9 us  [per_device(): lax.all_to_all(cot_send, 'dp', split_axis=0, concat_axis=0, tiled=True)]
    ppermute x0 -> x7, starting transfers between devices: none -> 9.86 us  [across(): lax.ppermute(block, axis, [(i, i ^ bits) for i in range(lax.axis_size(axi...]
    pallas_call x1 -> x4, Pallas kernels: 3.61 us -> 12.3 us  [the longest x3 8.1 us: per_device(): call(functools.partial(place_kernel, groups, capacity, away, found), 'pla...]
    ppermute x6, waiting for transfers between devices: 5.99 us -> 0.02 us  [reduce_rows(): lax.ppermute(sent, axis, [(i, i ^ m * stride) for i in range(size)])]
    all_to_all x1 -> x0, starting transfers between devices: 4.91 us -> none  [per_device(): lax.all_to_all(join_send, 'dp', split_axis=0, concat_axis=0, tiled=True)]
    unnamed x10 -> x20, local copies, waits for them, and re-layouts: 7.23 us -> 7.22 us
  transfers between devices with their start and end apart: 8 -> 14, of which waited for: 3 -> 6; matrix products, arithmetic and copies ran while one was open for 0% -> 1% of each run, Pallas kernels for 8% -> 14%
where the time goes in v4:
time: 156 us; the launch traced here: 154 us
  waiting for transfers between devices  91.7 us (59%)
  Pallas kernels  26.6 us (17%)
  starting transfers between devices  26 us (17%)
  local copies, waits for them, and re-layouts  7.29 us (5%)
  other arithmetic  1.57 us (1%)
    ppermute x7, waiting for transfers between devices, across(): lax.ppermute(block, axis, [(i, i ^ bits) for i in range(lax.axis_size(axi...  76.8 us
    all_to_all x1, waiting for transfers between devices, per_device(): lax.all_to_all(cot_send, 'dp', split_axis=0, concat_axis=0, tiled=True)  14.9 us
    ppermute x7, starting transfers between devices, across(): lax.ppermute(block, axis, [(i, i ^ bits) for i in range(lax.axis_size(axi...  9.86 us
    ppermute x6, starting transfers between devices, reduce_rows(): lax.ppermute(sent, axis, [(i, i ^ m * stride) for i in range(size)])  9.45 us
    pallas_call x3, Pallas kernels, per_device(): call(functools.partial(place_kernel, groups, capacity, away, found), 'pla...  8.1 us
    unnamed x20, local copies, waits for them, and re-layouts  7.22 us
    all_to_all x1, starting transfers between devices, per_device(): lax.all_to_all(cot_send, 'dp', split_axis=0, concat_axis=0, tiled=True)  6.7 us
    pallas_call x1, Pallas kernels, per_device(): call(functools.partial(join_kernel, groups, capacity), 'join_layers', [vm...  5.38 us
  transfers between devices with their start and end apart: 14, of which 6 were waited for; matrix products, arithmetic and copies ran while one was open for 1% of the time, Pallas kernels for 14%

profile of v4, /device:TPU:13, one launch (start us, length us, event | category | flops | bytes accessed | tf_op | source)
XLA Modules:
  0.0 154.0 jit_solution(11427740742503338661)
XLA Ops:
  0.6 4.4 %pack_cotangent.1 = bf16[128,12544]{1,0:T(8,128)(2,1)} custom-call(s32[1,128]{1,0:T(1,128)} %bitcast.7, bf16[128,128]{1,0:T(8,128)(2,1)} %logit_hbm.1, bf16[192,8192]{1,0:T(8,128)(2,1)} %cot_hbm.1), custom_call_target="tpu_custom_call" | custom-call | flops 805306368 | bytes 6291456 | tf_op jit(solution)/shard_map/pack_cotangent/pallas_call | solution.py:401
  5.1 0.0 copy-start.6
  5.1 0.0 copy-start.7
  5.1 6.7 %all-to-all-start = ((bf16[16,8,12544]{2,1,0:T(8,128)(2,1)}), bf16[16,8,12544]{2,1,0:T(8,128)(2,1)S(1)}, u32[]{:S(2)}, u32[]{:S(2)}) async-start(bf16[16,8,12544]{2,1,0:T(8,128)(2,1)} %bitcast.10), calls=%async_computation | async-start | bytes 6422528 | tf_op jit(solution)/shard_map/all_to_all | solution.py:424
  11.8 0.0 copy-done.6
  11.8 0.0 copy-done.7
  11.8 0.0 copy-start
  11.8 2.8 %copy-done = bf16[128,24576]{1,0:T(8,128)(2,1)S(1)} copy-done((bf16[128,24576]{1,0:T(8,128)(2,1)S(1)}, bf16[128,24576]{1,0:T(8,128)(2,1)}, u32[]{:S(2)}) %copy-start) | copy-done | bytes 6291480
  14.6 5.4 %join_layers.1 = (bf16[64,12288]{1,0:T(8,128)(2,1)S(1)}, bf16[64,12288]{1,0:T(8,128)(2,1)S(1)}, f32[128,128]{1,0:T(8,128)S(1)}) custom-call(s32[1,128]{1,0:T(1,128)S(1)} %bitcast.8, f32[3,8192]{1,0:T(4,128)S(1)} %copy-done.6, bf16[128,24576]{1,0:T(8,128)(2,1)S(1)} %copy-done), custom_call_target="tpu_custom_call" | custom-call | flops 536870912 | bytes 9437184 | tf_op jit(solution)/shard_map/join_layers/pallas_call | solution.py:426
  20.0 0.4 collective-permute-start
  20.4 3.0 %collective-permute-done.refs_1_ = bf16[64,12288]{1,0:T(8,128)(2,1)S(1)} collective-permute-done((bf16[64,12288]{1,0:T(8,128)(2,1)S(1)}, bf16[64,12288]{1,0:T(8,128)(2,1)S(1)}, u32[]{:S(2)}, u32[]{:S(2)}) %collective-permute-start) | collective-permute-done | bytes 1572896 | tf_op jit(solution)/shard_map/ppermute | solution.py:362
  23.5 4.2 %sort_chips.1 = (bf16[16,12288]{1,0:T(8,128)(2,1)S(1)}, bf16[32,12288]{1,0:T(8,128)(2,1)S(1)}, bf16[16,12288]{1,0:T(8,128)(2,1)S(1)}, bf16[16,12288]{1,0:T(8,128...) custom-call(bf16[64,12288]{1,0:T(8,128)(2,1)S(1)} %get-tuple-element.17.refs_0_, ...), custom_call_target="tpu_custom_call" | custom-call | flops 268435456 | bytes 6291456 | tf_op jit(solution)/shard_map/sort_chips/pallas_call | solution.py:446
  27.7 0.0 copy-start.9
  27.7 0.8 copy-done.9
  28.4 0.3 collective-permute-start.5
  28.7 29.5 %collective-permute-done.5.refs_1_ = bf16[32,12288]{1,0:T(8,128)(2,1)S(1)} collective-permute-done((bf16[32,12288]{1,0:T(8,128)(2,1)S(1)}, bf16[32,12288]{1,0:T(8,128)(2,1)S(1)}, u32[]{:S(2)}, u32[]{:S(2)}) %collective-permute-start.5) | collective-permute-done | bytes 786464 | tf_op jit(solution)/shard_map/ppermute | solution.py:362
  58.2 0.0 copy-start.2
  58.2 0.9 copy-done.2
  59.1 0.9 pad_maximum_fusion
  60.0 4.4 %collective-permute-start.6 = (bf16[32,12288]{1,0:T(8,128)(2,1)}, bf16[32,12288]{1,0:T(8,128)(2,1)}, u32[]{:S(2)}, u32[]{:S(2)}) collective-permute-start(bf16[32,12288]{1,0:T(8,128)(2,1)} %pad_maximum_fusion), channel_id=1, source_target_pairs={{0,4},{1,5},{2,6},{3,7},{4,0},{5,1},{6,2},{7,3},{8,12},{9,13},{10,... | collective-permute-start | bytes 2359304 | tf_op jit(solution)/shard_map/ppermute | solution.py:362
  64.5 0.0 collective-permute-start.3
  64.5 1.3 collective-permute-start.4
  65.8 2.0 %collective-permute-start.1 = (bf16[16,12288]{1,0:T(8,128)(2,1)}, bf16[16,12288]{1,0:T(8,128)(2,1)}, u32[]{:S(2)}, u32[]{:S(2)}) collective-permute-start(bf16[16,12288]{1,0:T(8,128)(2,1)} %copy-done.9), channel_id=1, source_target_pairs={{0,12},{1,13},{2,14},{3,15},{4,8},{5,9},{6,10},{7,11},{8,4},{9,5},... | collective-permute-start | bytes 1179656 | tf_op jit(solution)/shard_map/ppermute | solution.py:362
  67.8 1.4 collective-permute-start.2
  69.2 14.9 %all-to-all-done = bf16[16,8,12544]{2,1,0:T(8,128)(2,1)S(1)} async-done(((bf16[16,8,12544]{2,1,0:T(8,128)(2,1)}), bf16[16,8,12544]{2,1,0:T(8,128)(2,1)S(1)}, u32[]{:S(2)}, u32[]{:S(2)}) %all-to-all-start) | async-done | bytes 3211296 | tf_op jit(solution)/shard_map/all_to_all | solution.py:424
  84.1 2.8 %copy-done.1 = bf16[128,24576]{1,0:T(8,128)(2,1)S(1)} copy-done((bf16[128,24576]{1,0:T(8,128)(2,1)S(1)}, bf16[128,24576]{1,0:T(8,128)(2,1)}, u32[]{:S(2)}) %copy-start.1) | copy-done | bytes 6291480
  86.9 4.5 %gain_partials.1 = (f32[16,3,512]{2,1,0:T(4,128)S(1)}, bf16[192,128]{1,0:T(8,128)(2,1)}, f32[1,192]{1,0:T(1,128)}) custom-call(s32[1,128]{1,0:T(1,128)S(1)} %bitcast.9, f32[128,128]{1,0:T(8,128)S(1)} %get-tuple-element.26.inv_ref, bf16[128,24576]{1,0:T(8,128)(2,1)S(1)} %copy-done.1, bf16[128,12544]{1,0:T(8,128)(2,1)S(1)} %bitcast.6), custom_call_target="tpu_custom_call" | custom-call | flops 536870912 | bytes 9437184 | tf_op jit(solution)/shard_map/gain_partials/pallas_call | solution.py:470
  91.4 31.8 %collective-permute-done.3.refs_0_ = bf16[16,12288]{1,0:T(8,128)(2,1)} collective-permute-done((bf16[16,12288]{1,0:T(8,128)(2,1)}, bf16[16,12288]{1,0:T(8,128)(2,1)}, u32[]{:S(2)}, u32[]{:S(2)}) %collective-permute-start.3) | collective-permute-done | bytes 393248 | tf_op jit(solution)/shard_map/ppermute | solution.py:362
  123.2 1.3 collective-permute-start.7
  124.6 7.1 %collective-permute-done.4.refs_1_ = bf16[16,12288]{1,0:T(8,128)(2,1)} collective-permute-done((bf16[16,12288]{1,0:T(8,128)(2,1)}, bf16[16,12288]{1,0:T(8,128)(2,1)}, u32[]{:S(2)}, u32[]{:S(2)}) %collective-permute-start.4) | collective-permute-done | bytes 393248 | tf_op jit(solution)/shard_map/ppermute | solution.py:362
  131.7 1.6 %collective-permute-start.9 = (f32[4,3,512]{2,1,0:T(4,128)S(1)}, f32[4,3,512]{2,1,0:T(4,128)S(1)}, u32[]{:S(2)}, u32[]{:S(2)}) collective-permute-start(f32[4,3,512]{2,1,0:T(4,128)S(1)} %get-tuple-element.31), channel_id=1, source_target_pairs={{0,3},{1,2},{2,1},{3,0},{4,7},{5,6},{6,5},{7,4},{8,11},{9,10},{10,... | collective-permute-start | bytes 73736 | tf_op jit(solution)/shard_map/ppermute | solution.py:376
  133.2 0.0 collective-permute-done.6.refs_2_
  133.2 1.1 collective-permute-start.8
  134.4 3.1 %place_joined.3.refs_2_ = bf16[192,8192]{1,0:T(8,128)(2,1)} custom-call(bf16[16,12288]{1,0:T(8,128)(2,1)S(1)} %copy-done.5, bf16[32,12288]{1,0:T(8,128)(2,1)S(1)} %copy-done.3, bf16[32,12288]{1,0:T(8,128)(2,1)} %collective-permute-done.6.refs_2_), custom_call_target="tpu_custom_call" | custom-call | flops 402653184 | bytes 3145728 | tf_op jit(solution)/shard_map/place_joined/pallas_call | solution.py:498
  137.5 2.5 %place_joined.4.refs_2_ = bf16[192,8192]{1,0:T(8,128)(2,1)} custom-call(bf16[16,12288]{1,0:T(8,128)(2,1)} %collective-permute-done.3.refs_0_, bf16[16,12288]{1,0:T(8,128)(2,1)} %collective-permute-done.4.refs_1_, bf16[192,8192]{1,0:T(8,128)(2,1)} %place_joined.3.refs_2_), custom_call_target="tpu_custom_call", output_to_operand_aliasing={{}: (2, {})} | custom-call | flops 201326592 | bytes 1572864 | tf_op jit(solution)/shard_map/place_joined/pallas_call | solution.py:498
  140.0 0.0 collective-permute-done.7
  140.0 0.0 collective-permute-done.9
  140.0 0.0 collective-permute-done.8
  140.1 3.3 %collective-permute-start.10 = (f32[1,3,512]{2,1,0:T(4,128)S(1)}, f32[1,3,512]{2,1,0:T(4,128)S(1)}, u32[]{:S(2)}, u32[]{:S(2)}) collective-permute-start(f32[1,3,512]{2,1,0:T(4,128)S(1)} %get-tuple-element.33), channel_id=1, source_target_pairs={{0,4},{1,5},{2,6},{3,7},{4,0},{5,1},{6,2},{7,3},{8,12},{9,13},{10,... | collective-permute-start | bytes 18440 | tf_op jit(solution)/shard_map/ppermute | solution.py:376
  143.3 0.2 collective-permute-start.12
  143.6 1.9 %collective-permute-start.11 = (f32[1,3,512]{2,1,0:T(4,128)S(1)}, f32[1,3,512]{2,1,0:T(4,128)S(1)}, u32[]{:S(2)}, u32[]{:S(2)}) collective-permute-start(f32[1,3,512]{2,1,0:T(4,128)S(1)} %get-tuple-element.35), channel_id=1, source_target_pairs={{0,8},{1,9},{2,10},{3,11},{4,12},{5,13},{6,14},{7,15},{8,0},{9,1},... | collective-permute-start | bytes 18440 | tf_op jit(solution)/shard_map/ppermute | solution.py:376
  145.5 0.0 collective-permute-done.1.refs_0_
  145.5 5.4 %collective-permute-done.2.refs_1_ = bf16[16,12288]{1,0:T(8,128)(2,1)} collective-permute-done((bf16[16,12288]{1,0:T(8,128)(2,1)}, bf16[16,12288]{1,0:T(8,128)(2,1)}, u32[]{:S(2)}, u32[]{:S(2)}) %collective-permute-start.2) | collective-permute-done | bytes 393248 | tf_op jit(solution)/shard_map/ppermute | solution.py:362
  150.9 2.5 %place_joined.5 = bf16[192,8192]{1,0:T(8,128)(2,1)} custom-call(bf16[16,12288]{1,0:T(8,128)(2,1)} %collective-permute-done.1.refs_0_, bf16[16,12288]{1,0:T(8,128)(2,1)} %collective-permute-done.2.refs_1_, bf16[192,8192]{1,0:T(8,128)(2,1)} %place_joined.4.refs_2_), custom_call_target="tpu_custom_call", output_to_operand_aliasing={{}: (2, {})} | custom-call | flops 201326592 | bytes 1572864 | tf_op jit(solution)/shard_map/place_joined/pallas_call | solution.py:498
  153.4 0.0 collective-permute-done.10
  153.4 0.0 collective-permute-done.12
  153.4 0.0 collective-permute-done.11
  153.4 0.6 add_bitcast_fusion
  (13 shorter events, 0.1 us)
Async XLA Ops:
  5.1 6.7 %copy-start.6 = (f32[3,8192]{1,0:T(4,128)S(1)}, f32[3,8192]{1,0:T(4,128)}, u32[]{:S(2)}) copy-start(f32[3,8192]{1,0:T(4,128)} %gain_ref.1) | copy-start | bytes 294916
  5.1 6.7 %copy-start.7 = (s32[128,1]{0,1:T(1,128)S(1)}, s32[128,1]{0,1:T(1,128)}, u32[]{:S(2)}) copy-start(s32[128,1]{0,1:T(1,128)} %param.7) | copy-start | bytes 1540
  5.1 79.0 %all-to-all-start = ((bf16[16,8,12544]{2,1,0:T(8,128)(2,1)}), bf16[16,8,12544]{2,1,0:T(8,128)(2,1)S(1)}, u32[]{:S(2)}, u32[]{:S(2)}) async-start(bf16[16,8,12544]{2,1,0:T(8,128)(2,1)} %bitcast.10), calls=%async_computation | async-start | bytes 6422528 | tf_op jit(solution)/shard_map/all_to_all | solution.py:424
  11.8 2.8 %copy-start = (bf16[128,24576]{1,0:T(8,128)(2,1)S(1)}, bf16[128,24576]{1,0:T(8,128)(2,1)}, u32[]{:S(2)}) copy-start(bf16[128,24576]{1,0:T(8,128)(2,1)} %feat_hbm.3) | copy-start | bytes 18874372
  20.0 3.5 %collective-permute-start = (bf16[64,12288]{1,0:T(8,128)(2,1)S(1)}, bf16[64,12288]{1,0:T(8,128)(2,1)S(1)}, u32[]{:S(2)}, u32[]{:S(2)}) collective-permute-start(bf16[64,12288]{1,0:T(8,128)(2,1)S(1)} %get-tuple-element.18), channel_id=1, source_target_pairs={{0,1},{1,0},{2,3},{3,2},{4,5},{5,4},{6,7},{7,6},{8,9},{9,8},{10,11... | collective-permute-start | bytes 4718600 | tf_op jit(solution)/shard_map/ppermute | solution.py:362
  27.7 0.8 copy-start.9
  28.4 29.8 %copy-start.4 = (bf16[16,12288]{1,0:T(8,128)(2,1)}, bf16[16,12288]{1,0:T(8,128)(2,1)S(1)}, u32[]{:S(2)}) copy-start(bf16[16,12288]{1,0:T(8,128)(2,1)S(1)} %get-tuple-element.23.refs_0_) | copy-start | bytes 1179652
  28.4 31.6 %copy-start.8 = (bf16[16,12288]{1,0:T(8,128)(2,1)}, bf16[16,12288]{1,0:T(8,128)(2,1)S(1)}, u32[]{:S(2)}) copy-start(bf16[16,12288]{1,0:T(8,128)(2,1)S(1)} %get-tuple-element.20) | copy-start | bytes 1179652
  28.4 29.7 %collective-permute-start.5 = (bf16[32,12288]{1,0:T(8,128)(2,1)S(1)}, bf16[32,12288]{1,0:T(8,128)(2,1)S(1)}, u32[]{:S(2)}, u32[]{:S(2)}) collective-permute-start(bf16[32,12288]{1,0:T(8,128)(2,1)S(1)} %get-tuple-element.24), channel_id=1, source_target_pairs={{0,2},{1,3},{2,0},{3,1},{4,6},{5,7},{6,4},{7,5},{8,10},{9,11},{10,... | collective-permute-start | bytes 2359304 | tf_op jit(solution)/shard_map/ppermute | solution.py:362
  58.2 0.9 copy-start.2
  60.0 73.2 %collective-permute-start.6 = (bf16[32,12288]{1,0:T(8,128)(2,1)}, bf16[32,12288]{1,0:T(8,128)(2,1)}, u32[]{:S(2)}, u32[]{:S(2)}) collective-permute-start(bf16[32,12288]{1,0:T(8,128)(2,1)} %pad_maximum_fusion), channel_id=1, source_target_pairs={{0,4},{1,5},{2,6},{3,7},{4,0},{5,1},{6,2},{7,3},{8,12},{9,13},{10,... | collective-permute-start | bytes 2359304 | tf_op jit(solution)/shard_map/ppermute | solution.py:362
  64.5 58.8 %collective-permute-start.3 = (bf16[16,12288]{1,0:T(8,128)(2,1)}, bf16[16,12288]{1,0:T(8,128)(2,1)}, u32[]{:S(2)}, u32[]{:S(2)}) collective-permute-start(bf16[16,12288]{1,0:T(8,128)(2,1)} %get-tuple-element.21), channel_id=1, source_target_pairs={{0,8},{1,9},{2,10},{3,11},{4,12},{5,13},{6,14},{7,15},{8,0},{9,1},... | collective-permute-start | bytes 1179656 | tf_op jit(solution)/shard_map/ppermute | solution.py:362
  64.5 67.2 %collective-permute-start.4 = (bf16[16,12288]{1,0:T(8,128)(2,1)}, bf16[16,12288]{1,0:T(8,128)(2,1)}, u32[]{:S(2)}, u32[]{:S(2)}) collective-permute-start(bf16[16,12288]{1,0:T(8,128)(2,1)} %get-tuple-element.22), channel_id=1, source_target_pairs={{0,10},{1,11},{2,8},{3,9},{4,14},{5,15},{6,12},{7,13},{8,2},{9,3},... | collective-permute-start | bytes 1179656 | tf_op jit(solution)/shard_map/ppermute | solution.py:362
  65.8 79.7 %collective-permute-start.1 = (bf16[16,12288]{1,0:T(8,128)(2,1)}, bf16[16,12288]{1,0:T(8,128)(2,1)}, u32[]{:S(2)}, u32[]{:S(2)}) collective-permute-start(bf16[16,12288]{1,0:T(8,128)(2,1)} %copy-done.9), channel_id=1, source_target_pairs={{0,12},{1,13},{2,14},{3,15},{4,8},{5,9},{6,10},{7,11},{8,4},{9,5},... | collective-permute-start | bytes 1179656 | tf_op jit(solution)/shard_map/ppermute | solution.py:362
  67.8 83.0 %collective-permute-start.2 = (bf16[16,12288]{1,0:T(8,128)(2,1)}, bf16[16,12288]{1,0:T(8,128)(2,1)}, u32[]{:S(2)}, u32[]{:S(2)}) collective-permute-start(bf16[16,12288]{1,0:T(8,128)(2,1)} %copy-done.8), channel_id=1, source_target_pairs={{0,14},{1,15},{2,12},{3,13},{4,10},{5,11},{6,8},{7,9},{8,6},{9,7},... | collective-permute-start | bytes 1179656 | tf_op jit(solution)/shard_map/ppermute | solution.py:362
  84.1 2.8 %copy-start.1 = (bf16[128,24576]{1,0:T(8,128)(2,1)S(1)}, bf16[128,24576]{1,0:T(8,128)(2,1)}, u32[]{:S(2)}) copy-start(bf16[128,24576]{1,0:T(8,128)(2,1)} %feat_hbm.3) | copy-start | bytes 18874372
  86.9 47.5 %copy-start.3 = (bf16[32,12288]{1,0:T(8,128)(2,1)S(1)}, bf16[32,12288]{1,0:T(8,128)(2,1)}, u32[]{:S(2)}) copy-start(bf16[32,12288]{1,0:T(8,128)(2,1)} %copy-done.2) | copy-start | bytes 2359300
  86.9 47.5 %copy-start.5 = (bf16[16,12288]{1,0:T(8,128)(2,1)S(1)}, bf16[16,12288]{1,0:T(8,128)(2,1)}, u32[]{:S(2)}) copy-start(bf16[16,12288]{1,0:T(8,128)(2,1)} %copy-done.4) | copy-start | bytes 1179652
  123.2 16.8 %collective-permute-start.7 = (f32[4,3,512]{2,1,0:T(4,128)S(1)}, f32[4,3,512]{2,1,0:T(4,128)S(1)}, u32[]{:S(2)}, u32[]{:S(2)}) collective-permute-start(f32[4,3,512]{2,1,0:T(4,128)S(1)} %get-tuple-element.30), channel_id=1, source_target_pairs={{0,1},{1,0},{2,3},{3,2},{4,5},{5,4},{6,7},{7,6},{8,9},{9,8},{10,11... | collective-permute-start | bytes 73736 | tf_op jit(solution)/shard_map/ppermute | solution.py:376
  131.7 8.3 %collective-permute-start.9 = (f32[4,3,512]{2,1,0:T(4,128)S(1)}, f32[4,3,512]{2,1,0:T(4,128)S(1)}, u32[]{:S(2)}, u32[]{:S(2)}) collective-permute-start(f32[4,3,512]{2,1,0:T(4,128)S(1)} %get-tuple-element.31), channel_id=1, source_target_pairs={{0,3},{1,2},{2,1},{3,0},{4,7},{5,6},{6,5},{7,4},{8,11},{9,10},{10,... | collective-permute-start | bytes 73736 | tf_op jit(solution)/shard_map/ppermute | solution.py:376
  133.2 6.8 %collective-permute-start.8 = (f32[4,3,512]{2,1,0:T(4,128)S(1)}, f32[4,3,512]{2,1,0:T(4,128)S(1)}, u32[]{:S(2)}, u32[]{:S(2)}) collective-permute-start(f32[4,3,512]{2,1,0:T(4,128)S(1)} %get-tuple-element.32), channel_id=1, source_target_pairs={{0,2},{1,3},{2,0},{3,1},{4,6},{5,7},{6,4},{7,5},{8,10},{9,11},{10,... | collective-permute-start | bytes 73736 | tf_op jit(solution)/shard_map/ppermute | solution.py:376
  140.1 13.3 %collective-permute-start.10 = (f32[1,3,512]{2,1,0:T(4,128)S(1)}, f32[1,3,512]{2,1,0:T(4,128)S(1)}, u32[]{:S(2)}, u32[]{:S(2)}) collective-permute-start(f32[1,3,512]{2,1,0:T(4,128)S(1)} %get-tuple-element.33), channel_id=1, source_target_pairs={{0,4},{1,5},{2,6},{3,7},{4,0},{5,1},{6,2},{7,3},{8,12},{9,13},{10,... | collective-permute-start | bytes 18440 | tf_op jit(solution)/shard_map/ppermute | solution.py:376
  143.3 10.1 %collective-permute-start.12 = (f32[1,3,512]{2,1,0:T(4,128)S(1)}, f32[1,3,512]{2,1,0:T(4,128)S(1)}, u32[]{:S(2)}, u32[]{:S(2)}) collective-permute-start(f32[1,3,512]{2,1,0:T(4,128)S(1)} %get-tuple-element.34), channel_id=1, source_target_pairs={{0,12},{1,13},{2,14},{3,15},{4,8},{5,9},{6,10},{7,11},{8,4},{9,5},... | collective-permute-start | bytes 18440 | tf_op jit(solution)/shard_map/ppermute | solution.py:376
  143.6 9.8 %collective-permute-start.11 = (f32[1,3,512]{2,1,0:T(4,128)S(1)}, f32[1,3,512]{2,1,0:T(4,128)S(1)}, u32[]{:S(2)}, u32[]{:S(2)}) collective-permute-start(f32[1,3,512]{2,1,0:T(4,128)S(1)} %get-tuple-element.35), channel_id=1, source_target_pairs={{0,8},{1,9},{2,10},{3,11},{4,12},{5,13},{6,14},{7,15},{8,0},{9,1},... | collective-permute-start | bytes 18440 | tf_op jit(solution)/shard_map/ppermute | solution.py:376

commit v5 on v4

--- a/solution.py
+++ b/solution.py
@@ -13,8 +13,7 @@
 LANES = 128
 QUARTERS = 4
 CORES = 2
-VMEM_LIMIT = 20 * 1024 * 1024
-VMEM_WHOLE = 56 * 1024 * 1024
+VMEM_LIMIT = 24 * 1024 * 1024
 
 
 def pieces_of(capacity):
@@ -121,44 +120,8 @@
     return ref.at[:, g * wide : (g + 1) * wide]
 
 
-def cot_kernel(
-    groups, capacity, dest_hbm, logit_hbm, cot_hbm, *refs
-):
-    out_hbm, dest_v, logit_v, cot_v, out_v, log_v, dest_sem, logit_sem, in_sem, out_sem, log_sem = refs
-    count, slots, group = cot_v.shape
-    packed = out_v.shape[2]
-    loads = [pltpu.make_async_copy(cols(cot_hbm, g, group), cot_v.at[g], in_sem.at[g]) for g in range(count)]
-    stores = [pltpu.make_async_copy(out_v.at[g], cols(out_hbm, g, packed), out_sem.at[g]) for g in range(count)]
-    dest_load = pltpu.make_async_copy(dest_hbm, dest_v, dest_sem)
-    logit_load = pltpu.make_async_copy(logit_hbm, logit_v, logit_sem)
-    dest_load.start()
-    logit_load.start()
-    for load in loads:
-        load.start()
-    dest_load.wait()
-    target, rank, _, _ = ranks_of(dest_v[...])
-    shape = (groups * SUB, target.shape[1])
-    logit_load.wait()
-    for m in range(log_v.shape[1] // LANES):
-        place = hot(iota(shape, 0) == spread(target, rank, m * SUB, SUB, 0))
-        log_v[:, m * LANES : (m + 1) * LANES] = select(place, logit_v[...])
-    log_store = pltpu.make_async_copy(log_v, out_hbm.at[:, count * packed : count * packed + log_v.shape[1]], log_sem)
-    log_store.start()
-    slot = iota((1, slots), 1)
-    matrices = pack_matrices(lax.div(slot, capacity), lax.rem(slot, capacity), groups, capacity)
-    for g in range(count):
-        loads[g].wait()
-        base = 0
-        for packed_block in pack_group(cot_v[g], matrices, capacity):
-            out_v[g, :, base : base + packed_block.shape[1]] = packed_block
-            base += packed_block.shape[1]
-        stores[g].start()
-    for store in stores + [log_store]:
-        store.wait()
-
-
-def join_kernel(groups, capacity, dest_ref, gain_ref, feat_hbm, *refs):
-    *outs, inv_ref, feat_v, out_v, in_sem, out_sem = refs
+def join_kernel(groups, capacity, dest_ref, logit_ref, gain_ref, feat_hbm, *refs):
+    *outs, share_hbm, inv_ref, share_inv_ref, feat_v, out_v, log_v, share_v, in_sem, out_sem, log_sem, share_sem = refs
     layers, count, tokens, group = feat_v.shape
     width = count * group
     packed = out_v.shape[2]
@@ -178,8 +141,24 @@
         for load in row:
             load.start()
     target, rank, _, _ = ranks_of(dest_ref[...])
-    target = target ^ lax.axis_index("dp")
+    me = lax.axis_index("dp")
+    own = share_hbm.shape[0]
+    given = jnp.where(lax.rem(target, CORES) == lax.rem(me, CORES), -1, lax.div(target, CORES) * capacity + rank)
+    shared = iota((own, tokens), 0) == given
+    shares = [
+        [pltpu.make_async_copy(share_v.at[l, g], cols(share_hbm, l * count + g, group), share_sem.at[l, g]) for g in range(count)]
+        for l in range(layers)
+    ]
+    target = target ^ me
     target = lax.rem(target, CORES) * (groups // CORES) + lax.div(target, CORES)
+    shape = (groups * SUB, tokens)
+    for m in range(log_v.shape[1] // LANES):
+        place = hot(iota(shape, 0) == spread(target, rank, m * SUB, SUB, 0))
+        log_v[:, m * LANES : (m + 1) * LANES] = select(place, logit_ref[...])
+    tail = slice(count * packed, count * packed + log_v.shape[1])
+    stores.append([pltpu.make_async_copy(log_v.at[q * part : (q + 1) * part], outs[q].at[:, tail], log_sem.at[q]) for q in range(CORES)])
+    for store in stores[-1]:
+        store.start()
     matrices = pack_matrices(target, rank, groups, capacity)
     lane = iota((tokens, LANES), 1)
     inv_all = jnp.zeros((tokens, LANES), jnp.float32)
@@ -196,6 +175,9 @@
         inverse.append(inv)
         inv_all = jnp.where(lane == l, inv, inv_all)
     inv_ref[...] = inv_all
+    share_inv_ref[...] = jnp.dot(
+        jnp.where(shared, 1.0, 0.0), inv_all, preferred_element_type=jnp.float32, precision=lax.Precision.HIGHEST
+    )
     for g in range(count):
         joined = None
         for l in range(layers):
@@ -207,40 +189,45 @@
             base += block.shape[1]
         for store in stores[g]:
             store.start()
-    for row in stores:
+    for l in range(layers):
+        for g in range(count):
+            share_v[l, g] = select(hot(shared), feat_v[l, g])
+            shares[l][g].start()
+    for row in stores + shares:
         for store in row:
             store.wait()
 
 
-def sort_kernel(chips, held, *refs):
+def sort_kernel(chips, held, widths, *refs):
     gots, outs, (got_v, out_v, in_sem, out_sem) = refs[:CORES], refs[CORES:-4], refs[-4:]
-    count, rows, packed = got_v.shape
+    rows = got_v.shape[1]
     own, part = chips * SUB, CORES * SUB
-    loads = [
-        [pltpu.make_async_copy(cols(got, g, packed), got_v.at[g, q * own : (q + 1) * own], in_sem.at[g, q]) for q, got in enumerate(gots)]
-        for g in range(count)
-    ]
-    stores = [
-        [
-            pltpu.make_async_copy(
-                out_v.at[g, j * part : (j + 1) * part],
-                outs[array].at[pl.ds(row, part), g * packed : (g + 1) * packed],
-                out_sem.at[g, j],
-            )
-            for j, (array, row) in enumerate(held)
-        ]
-        for g in range(count)
-    ]
+    loads, stores, base = [], [], 0
+    for g, wide in enumerate(widths):
+        span = slice(base, base + wide)
+        base += wide
+        loads.append(
+            [
+                pltpu.make_async_copy(got.at[:, span], got_v.at[g, q * own : (q + 1) * own, :wide], in_sem.at[g, q])
+                for q, got in enumerate(gots)
+            ]
+        )
+        stores.append(
+            [
+                pltpu.make_async_copy(out_v.at[g, j * part : (j + 1) * part, :wide], outs[array].at[pl.ds(row, part), span], out_sem.at[g, j])
+                for j, (array, row) in enumerate(held)
+            ]
+        )
     for row in loads:
         for load in row:
             load.start()
     at, come = iota((rows, rows), 0), iota((rows, rows), 1)
     chip, core, rank = lax.div(at, part), lax.rem(lax.div(at, SUB), CORES), lax.rem(at, SUB)
     matrix = hot(come == core * own + chip * SUB + rank)
-    for g in range(count):
+    for g, wide in enumerate(widths):
         for load in loads[g]:
             load.wait()
-        out_v[g] = select(matrix, got_v[g])
+        out_v[g, :, :wide] = select(matrix, got_v[g, :, :wide])
         for store in stores[g]:
             store.start()
     for row in stores:
@@ -249,61 +236,63 @@
 
 
 def grad_kernel(
-    groups, capacity, dest_ref, inv_ref, feat_hbm, got_hbm, grad_ref, soft_ref, part_ref, feat_v, got_v, log_v, in_sem, got_sem, log_sem
+    groups, capacity, dest_ref, inv_ref, feat_hbm, other_inv_ref, other_hbm, got_hbm, grad_ref, feat_v, got_v, in_sem, other_sem, got_sem
 ):
-    layers, count, tokens, group = feat_v.shape
-    packed = got_v.shape[2]
+    layers, count, both, group = feat_v.shape
+    tokens = inv_ref.shape[0]
+    slots = got_v.shape[1]
     own = grad_ref.shape[2]
     order = exchange_order(groups)
-    log_load = pltpu.make_async_copy(got_hbm.at[:, count * packed : count * packed + log_v.shape[1]], log_v, log_sem)
-    log_load.start()
-    gots = [pltpu.make_async_copy(cols(got_hbm, g, packed), got_v.at[g], got_sem.at[g]) for g in range(count)]
+    gots = [pltpu.make_async_copy(cols(got_hbm, g, group), got_v.at[g], got_sem.at[g]) for g in range(count)]
     loads = [
-        [pltpu.make_async_copy(cols(feat_hbm, l * count + g, group), feat_v.at[l, g], in_sem.at[l, g]) for g in range(count)]
+        [
+            (
+                pltpu.make_async_copy(cols(feat_hbm, l * count + g, group), feat_v.at[l, g, :tokens], in_sem.at[l, g]),
+                pltpu.make_async_copy(cols(other_hbm, l * count + g, group), feat_v.at[l, g, tokens:both], other_sem.at[l, g]),
+            )
+            for g in range(count)
+        ]
         for l in range(layers)
     ]
     for g in range(count):
         gots[g].start()
         for l in range(layers):
-            loads[l][g].start()
+            for load in loads[l][g]:
+                load.start()
     _, _, target, rank = ranks_of(dest_ref[...])
-    matrices = unpack_matrices(target, rank, groups, capacity)
+    mine = lax.rem(lax.axis_index("dp"), CORES)
+    row = jnp.where(lax.rem(target, CORES) == mine, target * capacity + rank, -1)
+    come = iota((both - tokens, 1), 0)
+    come = (lax.div(come, capacity) * CORES + 1 - mine) * capacity + lax.rem(come, capacity)
+    matrix = hot(iota((both, slots), 1) == jnp.concatenate([row, come], axis=0))
+    inverse = jnp.concatenate([inv_ref[...], other_inv_ref[...]], axis=0)
+    wide = group // 2
+    step = min(own, wide)
     for g in range(count):
         gots[g].wait()
         for l in range(layers):
-            loads[l][g].wait()
-        blocks = unpack_group(got_v[g], matrices, capacity, group)
-        wide = group // len(blocks)
-        for b, cot in enumerate(blocks):
-            step = min(own, wide)
+            for load in loads[l][g]:
+                load.wait()
+        for b in range(group // wide):
+            cot = jnp.dot(matrix, got_v[g, :, b * wide : (b + 1) * wide], preferred_element_type=jnp.float32)
             for l in range(layers):
                 x = feat_v[l, g, :, b * wide : (b + 1) * wide].astype(jnp.float32)
-                part = jnp.sum(x * inv_ref[:, l : l + 1] * cot, axis=0, keepdims=True)
+                part = jnp.sum(x * inverse[:, l : l + 1] * cot, axis=0, keepdims=True)
                 for u in range(wide // step):
                     at = g * group + b * wide + u * step
                     lo = at % own
                     grad_ref[order[at // own], l : l + 1, lo : lo + step] = part[:, u * step : (u + 1) * step]
-    log_load.wait()
-    slots = soft_ref.shape[0]
-    slot = iota((slots, 1), 0)
-    target, rank = lax.div(slot, capacity), lax.rem(slot, capacity)
-    shape = (slots, groups * SUB)
-    logits = jnp.zeros((slots, LANES), jnp.float32)
-    for m in range(log_v.shape[1] // LANES):
-        place = hot(iota(shape, 1) == spread(target, rank, m * SUB, SUB, 0))
-        logits = logits + jnp.dot(place, log_v[:, m * LANES : (m + 1) * LANES], preferred_element_type=jnp.float32)
-    top = jnp.max(logits, axis=1, keepdims=True)
-    partition = top + jnp.log(jnp.sum(jnp.exp(logits - top), axis=1, keepdims=True))
-    part_ref[...] = jnp.broadcast_to(partition, logits.shape).T[:1]
-    soft_ref[...] = jnp.exp(logits - partition).astype(jnp.bfloat16)
-
-
-def place_kernel(groups, capacity, away, found, *refs):
+
+
+def place_kernel(groups, capacity, away, found, logs, *refs):
     chips = groups // QUARTERS // CORES
-    gots, (out_hbm, got_v, out_v, in_sem, out_sem) = refs[:-5], refs[-5:]
+    part = CORES * SUB
+    if logs:
+        *gots, out_hbm, soft_ref, part_ref, got_v, out_v, in_sem, out_sem, log_v, log_sem = refs
+    else:
+        *gots, out_hbm, got_v, out_v, in_sem, out_sem = refs
     _, count, held, group = out_v.shape
     packed = got_v.shape[3]
-    part = CORES * SUB
     me = lax.axis_index("dp")
     quarter, within = lax.div(me, groups // QUARTERS), lax.rem(me, groups // QUARTERS)
     loads, stores = [], []
@@ -321,7 +310,11 @@
                 ]
             )
             stores.append(pltpu.make_async_copy(out_v.at[a, g], out_hbm.at[rows, g * group : (g + 1) * group], out_sem.at[a, g]))
-    for row in loads:
+    log_loads = []
+    for k, (array, row) in enumerate(logs):
+        span = slice(count * packed, count * packed + log_v.shape[1])
+        log_loads.append(pltpu.make_async_copy(gots[array].at[pl.ds(row, part), span], log_v.at[k * part : (k + 1) * part], log_sem.at[k]))
+    for row in loads + [log_loads]:
         for load in row:
             load.start()
     slot = iota((held, 1), 0)
@@ -335,6 +328,21 @@
             for b, block in enumerate(blocks):
                 out_v[a, g, :, b * wide : (b + 1) * wide] = block.astype(jnp.bfloat16)
             stores[a * count + g].start()
+    if logs:
+        for load in log_loads:
+            load.wait()
+        slots = soft_ref.shape[0]
+        slot = iota((slots, 1), 0)
+        source, rank = lax.div(slot, capacity) ^ me, lax.rem(slot, capacity)
+        shape = (slots, groups * SUB)
+        logits = jnp.zeros((slots, LANES), jnp.float32)
+        for m in range(log_v.shape[1] // LANES):
+            place = hot(iota(shape, 1) == spread(source, rank, m * SUB, SUB, 0))
+            logits = logits + jnp.dot(place, log_v[:, m * LANES : (m + 1) * LANES], preferred_element_type=jnp.float32)
+        top = jnp.max(logits, axis=1, keepdims=True)
+        partition = top + jnp.log(jnp.sum(jnp.exp(logits - top), axis=1, keepdims=True))
+        part_ref[...] = jnp.broadcast_to(partition, logits.shape).T[:1]
+        soft_ref[...] = jnp.exp(logits - partition).astype(jnp.bfloat16)
     for store in stores:
         store.wait()
 
@@ -397,63 +405,48 @@
 
     chips = groups // CORES
     near = chips // QUARTERS
-
-    cot_send = call(
-        functools.partial(cot_kernel, groups, capacity),
-        "pack_cotangent",
-        [hbm, hbm, hbm],
-        shape((rows, count * packed + log_wide), bf16),
-        hbm,
-        [
-            pltpu.VMEM((1, tokens), jnp.int32),
-            pltpu.VMEM((tokens, kept), bf16),
-            pltpu.VMEM((count, slots, GROUP), bf16),
-            pltpu.VMEM((count, rows, packed), bf16),
-            pltpu.VMEM((rows, log_wide), bf16),
-            dma,
-            dma,
-            dma((count,)),
-            dma((count,)),
-            dma,
-        ],
-        4 * slots * width,
-        2 * rows * slots * width * 2,
-        VMEM_WHOLE,
-    )(dest_row, target_logits, joined_cotangent)
-
-    cot_got = lax.all_to_all(cot_send, "dp", split_axis=0, concat_axis=0, tiled=True)
-
-    *join_send, inverse = call(
+    wide = count * packed + log_wide
+
+    by_core = [[chip * CORES + core for chip in range(chips)] for core in range(CORES)]
+    cot_chip = lax.all_to_all(joined_cotangent, "dp", split_axis=0, concat_axis=0, axis_index_groups=by_core, tiled=True)
+
+    *join_send, share, inverse, share_inverse = call(
         functools.partial(join_kernel, groups, capacity),
         "join_layers",
-        [vmem, vmem, hbm],
-        (shape((chips * SUB, count * packed), bf16),) * CORES + (shape((tokens, LANES), f32),),
-        (hbm,) * CORES + (vmem,),
+        [vmem, vmem, vmem, hbm],
+        (shape((chips * SUB, wide), bf16),) * CORES
+        + (shape((slots // CORES, layers * width), bf16), shape((tokens, LANES), f32), shape((slots // CORES, LANES), f32)),
+        (hbm,) * CORES + (hbm, vmem, vmem),
         [
             pltpu.VMEM((layers, count, tokens, GROUP), bf16),
             pltpu.VMEM((count, rows, packed), bf16),
+            pltpu.VMEM((rows, log_wide), bf16),
+            pltpu.VMEM((layers, count, slots // CORES, GROUP), bf16),
             dma((layers, count)),
             dma((count, CORES)),
+            dma((CORES,)),
+            dma((layers, count)),
         ],
         2 * layers * tokens * width + 2 * slots * width,
         2 * rows * tokens * width * 2,
-    )(dest_row, joining_gains, features)
+    )(dest_row, target_logits, joining_gains, features)
     part = CORES * SUB
     relayed = near == 2
     held = [(0, 0), (1, 0), (2, 0), (1, part)] if relayed else []
     held += [(k - 1 if relayed else k, 0) for k in range(len(held), chips)]
     tall = [sum(part for array, _ in held if array == i) for i in range(1 + held[-1][0])]
+    widths = (packed,) * count + (log_wide,)
     join_sorted = call(
-        functools.partial(sort_kernel, chips, held),
+        functools.partial(sort_kernel, chips, held, widths),
         "sort_chips",
         [anywhere] * CORES,
-        tuple(shape((size, count * packed), bf16) for size in tall),
+        tuple(shape((size, wide), bf16) for size in tall),
         (hbm,) * len(tall),
         [
-            pltpu.VMEM((count, rows, packed), bf16),
-            pltpu.VMEM((count, rows, packed), bf16),
-            dma((count, CORES)),
-            dma((count, chips)),
+            pltpu.VMEM((len(widths), rows, packed), bf16),
+            pltpu.VMEM((len(widths), rows, packed), bf16),
+            dma((len(widths), CORES)),
+            dma((len(widths), chips)),
         ],
         4 * slots * width,
         2 * rows * rows * width,
@@ -467,52 +460,53 @@
     for k in range(len(join_got), chips):
         join_got.append((across(join_sorted[held[k][0]], "dp", k * CORES), 0))
 
-    partial_rows, soft_labels, log_partition = call(
+    partial_rows = call(
         functools.partial(grad_kernel, groups, capacity),
         "gain_partials",
-        [vmem, vmem, hbm, anywhere],
-        (shape((groups, layers, width // groups), f32), shape((slots, kept), bf16), shape((1, slots), f32)),
-        (vmem, vmem, vmem),
+        [vmem, vmem, hbm, vmem, anywhere, anywhere],
+        shape((groups, layers, width // groups), f32),
+        vmem,
         [
-            pltpu.VMEM((layers, count, tokens, GROUP), bf16),
-            pltpu.VMEM((count, rows, packed), bf16),
-            pltpu.VMEM((rows, log_wide), bf16),
+            pltpu.VMEM((layers, count, tokens + slots // CORES, GROUP), bf16),
+            pltpu.VMEM((count, slots, GROUP), bf16),
+            dma((layers, count)),
             dma((layers, count)),
             dma((count,)),
-            dma,
         ],
         2 * layers * tokens * width + 2 * slots * width,
         2 * rows * tokens * width * 2,
-    )(dest_row, inverse, features, cot_got)
+    )(dest_row, inverse, features, across(share_inverse, "dp", 1), across(share, "dp", 1), cot_chip)
     gain_grad = reduce_rows(partial_rows, "dp")[0]
 
     joined_input = ()
     for away in ((0, 1), (2,), (3,)):
-        parts = [join_got[j * near + i] for j in away for i in range(near)]
+        last = away == (3,)
         arrays = []
-        for array, _ in parts:
+        for array, _ in join_got if last else [join_got[j * near + i] for j in away for i in range(near)]:
             if not any(array is seen for seen in arrays):
                 arrays.append(array)
-        found = [([array is seen for seen in arrays].index(True), row) for array, row in parts]
-        joined_input = (
-            call(
-                functools.partial(place_kernel, groups, capacity, away, found),
-                "place_joined",
-                [anywhere] * (len(arrays) + len(joined_input)),
-                shape((slots, width), bf16),
-                hbm,
-                [
-                    pltpu.VMEM((len(away), count, rows // QUARTERS, packed), bf16),
-                    pltpu.VMEM((len(away), count, slots // QUARTERS, GROUP), bf16),
-                    dma((len(away), count, near)),
-                    dma((len(away), count)),
-                ],
-                slots * width * len(away),
-                rows * slots * width * len(away),
-                aliases={len(arrays): 0} if joined_input else None,
-            )(*arrays, *joined_input),
-        )
-    joined_input = joined_input[0]
+        at = [[(n, row) for n, seen in enumerate(arrays) if seen is array] for array, row in join_got]
+        found = [at[j * near + i][0] for j in away for i in range(near)]
+        logs = [one[0] for one in at] if last else []
+        out = call(
+            functools.partial(place_kernel, groups, capacity, away, found, logs),
+            "place_joined",
+            [anywhere] * (len(arrays) + len(joined_input)),
+            (shape((slots, width), bf16),) + ((shape((slots, kept), bf16), shape((1, slots), f32)) if last else ()),
+            (hbm,) + ((vmem, vmem) if last else ()),
+            [
+                pltpu.VMEM((len(away), count, rows // QUARTERS, packed), bf16),
+                pltpu.VMEM((len(away), count, slots // QUARTERS, GROUP), bf16),
+                dma((len(away), count, near)),
+                dma((len(away), count)),
+            ]
+            + ([pltpu.VMEM((rows, log_wide), bf16), dma((chips,))] if last else []),
+            slots * width * len(away),
+            rows * slots * width * len(away),
+            aliases={len(arrays): 0} if joined_input else None,
+        )(*arrays, *joined_input)
+        joined_input = out[:1]
+    joined_input, soft_labels, log_partition = out
     return (joined_input, soft_labels, log_partition[0], gain_grad)
 
 

time: 156 us -> 151 us (0.968)
  waiting for transfers between devices: 91.7 us -> 86.4 us
  starting transfers between devices: 26 us -> 24.2 us
    all_to_all x1, waiting for transfers between devices: 14.9 us -> 0.01 us  [per_device(): lax.all_to_all(joined_cotangent, 'dp', split_axis=0, concat_axis=0, axis_...]
    ppermute x7 -> x9, waiting for transfers between devices: 76.8 us -> 86.4 us  [across(): lax.ppermute(block, axis, [(i, i ^ bits) for i in range(lax.axis_size(axi...]
    pallas_call x5 -> x4, Pallas kernels: 16.7 us -> 13.3 us  [the longest x3 8.81 us: per_device(): call(functools.partial(place_kernel, groups, capacity, away, found, logs)...]
    pallas_call x1, Pallas kernels: 5.38 us -> 8.68 us  [per_device(): call(functools.partial(join_kernel, groups, capacity), 'join_layers', [vm...]
    pallas_call x1, Pallas kernels: 4.53 us -> 6.12 us  [per_device(): call(functools.partial(grad_kernel, groups, capacity), 'gain_partials', [...]
    ppermute x7 -> x9, starting transfers between devices: 9.86 us -> 8.89 us  [across(): lax.ppermute(block, axis, [(i, i ^ bits) for i in range(lax.axis_size(axi...]
    unnamed x20 -> x22, local copies, waits for them, and re-layouts: 7.22 us -> 7.31 us
  transfers between devices with their start and end apart: 14 -> 16, of which waited for: 6 -> 6; matrix products, arithmetic and copies ran while one was open for 1% -> 1% of each run, Pallas kernels for 14% -> 19%
where the time goes in v5:
time: 151 us; the launch traced here: 149 us
  waiting for transfers between devices  86.4 us (57%)
  Pallas kernels  28.1 us (19%)
  starting transfers between devices  24.2 us (16%)
  local copies, waits for them, and re-layouts  7.38 us (5%)
  other arithmetic  1.59 us (1%)
    ppermute x9, waiting for transfers between devices, across(): lax.ppermute(block, axis, [(i, i ^ bits) for i in range(lax.axis_size(axi...  86.4 us
    ppermute x6, starting transfers between devices, reduce_rows(): lax.ppermute(sent, axis, [(i, i ^ m * stride) for i in range(size)])  9.55 us
    ppermute x9, starting transfers between devices, across(): lax.ppermute(block, axis, [(i, i ^ bits) for i in range(lax.axis_size(axi...  8.89 us
    pallas_call x3, Pallas kernels, per_device(): call(functools.partial(place_kernel, groups, capacity, away, found, logs)...  8.81 us
    pallas_call x1, Pallas kernels, per_device(): call(functools.partial(join_kernel, groups, capacity), 'join_layers', [vm...  8.68 us
    unnamed x22, local copies, waits for them, and re-layouts  7.31 us
    pallas_call x1, Pallas kernels, per_device(): call(functools.partial(grad_kernel, groups, capacity), 'gain_partials', [...  6.12 us
    all_to_all x1, starting transfers between devices, per_device(): lax.all_to_all(joined_cotangent, 'dp', split_axis=0, concat_axis=0, axis_...  5.81 us
  transfers between devices with their start and end apart: 16, of which 6 were waited for; matrix products, arithmetic and copies ran while one was open for 1% of the time, Pallas kernels for 19%

profile of v5, /device:TPU:13, one launch (start us, length us, event | category | flops | bytes accessed | tf_op | source)
XLA Modules:
  0.0 148.6 jit_solution(14591931671564169605)
XLA Ops:
  0.6 0.0 copy-start.4
  0.6 0.0 copy-start.7
  0.7 5.8 %all-to-all-start = ((bf16[8,24,8192]{2,1,0:T(8,128)(2,1)}), bf16[8,24,8192]{2,1,0:T(8,128)(2,1)S(1)}, u32[]{:S(2)}, u32[]{:S(2)}) async-start(bf16[8,24,8192]{2,1,0:T(8,128)(2,1)} %bitcast.9), calls=%async_computation | async-start | bytes 6291456 | tf_op jit(solution)/shard_map/all_to_all | solution.py:411
  6.5 0.0 copy-start
  6.5 2.8 %copy-done = bf16[128,24576]{1,0:T(8,128)(2,1)S(1)} copy-done((bf16[128,24576]{1,0:T(8,128)(2,1)S(1)}, bf16[128,24576]{1,0:T(8,128)(2,1)}, u32[]{:S(2)}) %copy-start) | copy-done | bytes 6291480
  9.3 8.7 %join_layers.1 = (bf16[64,12544]{1,0:T(8,128)(2,1)S(1)}, bf16[64,12544]{1,0:T(8,128)(2,1)S(1)}, bf16[96,24576]{1,0:T(8,128)(2,1)}, f32[128,128]{1,0:T(8,128)S(1)}, f32[96,128]{1,0:T(8,128)}) custom-call(s32[1,128]{1,0:T(1,128)S(1)} %bitcast.7, bf16[128,128]{1,0:T(8,128)(2,1)S(1)} %copy-done.7, f32[3,8192]{1,0:T(4,128)S(1)} %copy-done.4, ...), custom_call_target="tpu_custom_call" | custom-call | flops 536870912 | bytes 9437184 | tf_op jit(solution)/shard_map/join_layers/pallas_call | solution.py:413
  18.0 1.3 collective-permute-start.8
  19.3 0.1 collective-permute-start
  19.4 9.6 %collective-permute-done.refs_1_ = bf16[64,12544]{1,0:T(8,128)(2,1)S(1)} collective-permute-done((bf16[64,12544]{1,0:T(8,128)(2,1)S(1)}, bf16[64,12544]{1,0:T(8,128)(2,1)S(1)}, u32[]{:S(2)}, u32[]{:S(2)}) %collective-permute-start) | collective-permute-done | bytes 1605664 | tf_op jit(solution)/shard_map/ppermute | solution.py:370
  29.0 4.5 %sort_chips.1 = (bf16[16,12544]{1,0:T(8,128)(2,1)S(1)}, bf16[32,12544]{1,0:T(8,128)(2,1)S(1)}, bf16[16,12544]{1,0:T(8,128)(2,1)S(1)}, bf16[16,12544]{1,0:T(8,128...) custom-call(bf16[64,12544]{1,0:T(8,128)(2,1)S(1)} %get-tuple-element.19.refs_0_, ...), custom_call_target="tpu_custom_call" | custom-call | flops 268435456 | bytes 6291456 | tf_op jit(solution)/shard_map/sort_chips/pallas_call | solution.py:439
  33.5 0.4 collective-permute-start.1
  33.9 33.2 %collective-permute-done.1.refs_1_ = bf16[32,12544]{1,0:T(8,128)(2,1)S(1)} collective-permute-done((bf16[32,12544]{1,0:T(8,128)(2,1)S(1)}, bf16[32,12544]{1,0:T(8,128)(2,1)S(1)}, u32[]{:S(2)}, u32[]{:S(2)}) %collective-permute-start.1) | collective-permute-done | bytes 802848 | tf_op jit(solution)/shard_map/ppermute | solution.py:370
  67.1 0.0 copy-start.2
  67.1 0.9 copy-done.2
  68.0 1.0 pad_maximum_fusion
  68.9 0.0 collective-permute-start.2
  69.0 2.1 %collective-permute-start.3 = (bf16[16,12544]{1,0:T(8,128)(2,1)}, bf16[16,12544]{1,0:T(8,128)(2,1)}, u32[]{:S(2)}, u32[]{:S(2)}) collective-permute-start(bf16[16,12544]{1,0:T(8,128)(2,1)} %get-tuple-element.24), channel_id=1, source_target_pairs={{0,8},{1,9},{2,10},{3,11},{4,12},{5,13},{6,14},{7,15},{8,0},{9,1},... | collective-permute-start | bytes 1204232 | tf_op jit(solution)/shard_map/ppermute | solution.py:370
  71.0 2.8 %collective-permute-start.4 = (bf16[16,12544]{1,0:T(8,128)(2,1)}, bf16[16,12544]{1,0:T(8,128)(2,1)}, u32[]{:S(2)}, u32[]{:S(2)}) collective-permute-start(bf16[16,12544]{1,0:T(8,128)(2,1)} %get-tuple-element.25), channel_id=1, source_target_pairs={{0,10},{1,11},{2,8},{3,9},{4,14},{5,15},{6,12},{7,13},{8,2},{9,3},... | collective-permute-start | bytes 1204232 | tf_op jit(solution)/shard_map/ppermute | solution.py:370
  73.8 1.8 %collective-permute-start.7 = (f32[96,128]{1,0:T(8,128)}, f32[96,128]{1,0:T(8,128)}, u32[]{:S(2)}, u32[]{:S(2)}) collective-permute-start(f32[96,128]{1,0:T(8,128)} %get-tuple-element.32), channel_id=1, source_target_pairs={{0,1},{1,0},{2,3},{3,2},{4,5},{5,4},{6,7},{7,6},{8,9},{9,8},{10,11... | collective-permute-start | bytes 147464 | tf_op jit(solution)/shard_map/ppermute | solution.py:370
  75.6 1.2 collective-permute-done.7.other_inv_ref
  76.9 0.3 collective-permute-start.5
  77.1 0.0 collective-permute-done.8.other_hbm
  77.1 0.2 collective-permute-start.6
  77.3 0.0 all-to-all-done
  77.4 2.8 %copy-done.1 = bf16[128,24576]{1,0:T(8,128)(2,1)S(1)} copy-done((bf16[128,24576]{1,0:T(8,128)(2,1)S(1)}, bf16[128,24576]{1,0:T(8,128)(2,1)}, u32[]{:S(2)}) %copy-start.1) | copy-done | bytes 6291480
  80.1 0.8 copy-done.6
  81.0 6.1 %gain_partials.1 = f32[16,3,512]{2,1,0:T(4,128)S(1)} custom-call(s32[1,128]{1,0:T(1,128)S(1)} %bitcast.8, f32[128,128]{1,0:T(8,128)S(1)} %copy-done.6, bf16[128,24576]{1,0:T(8,128)(2,1)S(1)} %copy-done.1, f32[96,128]{1,0:T(8,128)} %collective-permute-done.7.other_inv_ref, bf16[96,24576]{1,0:T(8,128)(2,1)} %collective-permute-done.8.other_hbm, ...), custom_call_target="tpu_custom_call" | custom-call | flops 536870912 | bytes 9437184 | tf_op jit(solution)/shard_map/gain_partials/pallas_call | solution.py:463
  87.1 9.9 %collective-permute-done.3.refs_0_.refs_3_ = bf16[16,12544]{1,0:T(8,128)(2,1)} collective-permute-done((bf16[16,12544]{1,0:T(8,128)(2,1)}, bf16[16,12544]{1,0:T(8,128)(2,1)}, u32[]{:S(2)}, u32[]{:S(2)}) %collective-permute-start.3) | collective-permute-done | bytes 401440 | tf_op jit(solution)/shard_map/ppermute | solution.py:370
  97.1 2.5 %collective-permute-start.10 = (f32[4,3,512]{2,1,0:T(4,128)S(1)}, f32[4,3,512]{2,1,0:T(4,128)S(1)}, u32[]{:S(2)}, u32[]{:S(2)}) collective-permute-start(f32[4,3,512]{2,1,0:T(4,128)S(1)} %get-tuple-element.36), channel_id=1, source_target_pairs={{0,2},{1,3},{2,0},{3,1},{4,6},{5,7},{6,4},{7,5},{8,10},{9,11},{10,... | collective-permute-start | bytes 73736 | tf_op jit(solution)/shard_map/ppermute | solution.py:384
  99.6 26.8 %collective-permute-done.4.refs_1_.refs_4_ = bf16[16,12544]{1,0:T(8,128)(2,1)} collective-permute-done((bf16[16,12544]{1,0:T(8,128)(2,1)}, bf16[16,12544]{1,0:T(8,128)(2,1)}, u32[]{:S(2)}, u32[]{:S(2)}) %collective-permute-start.4) | collective-permute-done | bytes 401440 | tf_op jit(solution)/shard_map/ppermute | solution.py:370
  126.4 1.5 %collective-permute-start.11 = (f32[4,3,512]{2,1,0:T(4,128)S(1)}, f32[4,3,512]{2,1,0:T(4,128)S(1)}, u32[]{:S(2)}, u32[]{:S(2)}) collective-permute-start(f32[4,3,512]{2,1,0:T(4,128)S(1)} %get-tuple-element.35), channel_id=1, source_target_pairs={{0,3},{1,2},{2,1},{3,0},{4,7},{5,6},{6,5},{7,4},{8,11},{9,10},{10,... | collective-permute-start | bytes 73736 | tf_op jit(solution)/shard_map/ppermute | solution.py:384
  127.9 0.0 collective-permute-done.2.refs_2_
  127.9 0.0 collective-permute-start.9
  127.9 3.1 %place_joined.3.refs_2_ = bf16[192,8192]{1,0:T(8,128)(2,1)} custom-call(bf16[16,12544]{1,0:T(8,128)(2,1)S(1)} %get-tuple-element.21.refs_0_, bf16[32,12544]{1,0:T(8,128)(2,1)S(1)} %copy-done.3, bf16[32,12544]{1,0:T(8,128)(2,1)} %collective-permute-done.2.refs_2_), custom_call_target="tpu_custom_call" | custom-call | flops 402653184 | bytes 3145728 | tf_op jit(solution)/shard_map/place_joined/pallas_call | solution.py:491
  131.0 2.5 %place_joined.4.refs_7_ = bf16[192,8192]{1,0:T(8,128)(2,1)} custom-call(bf16[16,12544]{1,0:T(8,128)(2,1)} %collective-permute-done.3.refs_0_.refs_3_, bf16[16,12544]{1,0:T(8,128)(2,1)} %collective-permute-done.4.refs_1_.refs_4_, bf16[192,8192]{1,0:T(8,128)(2,1)} %place_joined.3.refs_2_), custom_call_target="tpu_custom_call", output_to_operand_aliasing={{}: (2, {})} | custom-call | flops 201326592 | bytes 1572864 | tf_op jit(solution)/shard_map/place_joined/pallas_call | solution.py:491
  133.5 0.0 collective-permute-done.10
  133.5 0.0 collective-permute-done.11
  133.5 0.0 collective-permute-done.9
  133.6 4.3 %collective-permute-start.12 = (f32[1,3,512]{2,1,0:T(4,128)S(1)}, f32[1,3,512]{2,1,0:T(4,128)S(1)}, u32[]{:S(2)}, u32[]{:S(2)}) collective-permute-start(f32[1,3,512]{2,1,0:T(4,128)S(1)} %get-tuple-element.37), channel_id=1, source_target_pairs={{0,4},{1,5},{2,6},{3,7},{4,0},{5,1},{6,2},{7,3},{8,12},{9,13},{10,... | collective-permute-start | bytes 18440 | tf_op jit(solution)/shard_map/ppermute | solution.py:384
  137.9 0.0 collective-permute-start.13
  137.9 1.3 collective-permute-start.14
  139.1 0.0 collective-permute-done.5.refs_5_
  139.1 5.7 %collective-permute-done.6.refs_6_ = bf16[16,12544]{1,0:T(8,128)(2,1)} collective-permute-done((bf16[16,12544]{1,0:T(8,128)(2,1)}, bf16[16,12544]{1,0:T(8,128)(2,1)}, u32[]{:S(2)}, u32[]{:S(2)}) %collective-permute-start.6) | collective-permute-done | bytes 401440 | tf_op jit(solution)/shard_map/ppermute | solution.py:370
  144.8 3.2 %place_joined.5 = (bf16[192,8192]{1,0:T(8,128)(2,1)}, bf16[192,128]{1,0:T(8,128)(2,1)}, f32[1,192]{1,0:T(1,128)}) custom-call(bf16[16,12544]{1,0:T(8,128)(2,1)S(1)} %get-tuple-element.21.refs_0_, bf16[32,12544]{1,0:T(8,128)(2,1)S(1)} %copy-done.3, bf16[32,12544]{1,0:T(8,128)(2,1)} %collective-permute-done.2.refs_2_, ...), custom_call_target="tpu_custom_call", output_to_operand_aliasing={{0}: (7, {})} | custom-call | flops 201326592 | bytes 1572864 | tf_op jit(solution)/shard_map/place_joined/pallas_call | solution.py:491
  148.0 0.0 collective-permute-done.12
  148.0 0.0 collective-permute-done.13
  148.0 0.0 collective-permute-done.14
  148.0 0.6 add_bitcast_fusion
  (18 shorter events, 0.1 us)
Async XLA Ops:
  0.6 5.8 %copy-start.4 = (f32[3,8192]{1,0:T(4,128)S(1)}, f32[3,8192]{1,0:T(4,128)}, u32[]{:S(2)}) copy-start(f32[3,8192]{1,0:T(4,128)} %gain_ref.1) | copy-start | bytes 294916
  0.6 5.8 %copy-start.7 = (bf16[128,128]{1,0:T(8,128)(2,1)S(1)}, bf16[128,128]{1,0:T(8,128)(2,1)}, u32[]{:S(2)}) copy-start(bf16[128,128]{1,0:T(8,128)(2,1)} %logit_ref.1) | copy-start | bytes 98308
  0.7 5.8 %copy-start.8 = (s32[128,1]{0,1:T(1,128)S(1)}, s32[128,1]{0,1:T(1,128)}, u32[]{:S(2)}) copy-start(s32[128,1]{0,1:T(1,128)} %param.7) | copy-start | bytes 1540
  0.7 76.7 %all-to-all-start = ((bf16[8,24,8192]{2,1,0:T(8,128)(2,1)}), bf16[8,24,8192]{2,1,0:T(8,128)(2,1)S(1)}, u32[]{:S(2)}, u32[]{:S(2)}) async-start(bf16[8,24,8192]{2,1,0:T(8,128)(2,1)} %bitcast.9), calls=%async_computation | async-start | bytes 6291456 | tf_op jit(solution)/shard_map/all_to_all | solution.py:411
  6.5 2.8 %copy-start = (bf16[128,24576]{1,0:T(8,128)(2,1)S(1)}, bf16[128,24576]{1,0:T(8,128)(2,1)}, u32[]{:S(2)}) copy-start(bf16[128,24576]{1,0:T(8,128)(2,1)} %feat_hbm.3) | copy-start | bytes 18874372
  18.0 51.0 %copy-start.5 = (f32[128,128]{1,0:T(8,128)}, f32[128,128]{1,0:T(8,128)S(1)}, u32[]{:S(2)}) copy-start(f32[128,128]{1,0:T(8,128)S(1)} %get-tuple-element.31.inv_ref) | copy-start | bytes 196612
  18.0 59.2 %collective-permute-start.8 = (bf16[96,24576]{1,0:T(8,128)(2,1)}, bf16[96,24576]{1,0:T(8,128)(2,1)}, u32[]{:S(2)}, u32[]{:S(2)}) collective-permute-start(bf16[96,24576]{1,0:T(8,128)(2,1)} %get-tuple-element.33), channel_id=1, source_target_pairs={{0,1},{1,0},{2,3},{3,2},{4,5},{5,4},{6,7},{7,6},{8,9},{9,8},{10,11... | collective-permute-start | bytes 14155784 | tf_op jit(solution)/shard_map/ppermute | solution.py:370
  19.3 9.7 %collective-permute-start = (bf16[64,12544]{1,0:T(8,128)(2,1)S(1)}, bf16[64,12544]{1,0:T(8,128)(2,1)S(1)}, u32[]{:S(2)}, u32[]{:S(2)}) collective-permute-start(bf16[64,12544]{1,0:T(8,128)(2,1)S(1)} %get-tuple-element.20), channel_id=1, source_target_pairs={{0,1},{1,0},{2,3},{3,2},{4,5},{5,4},{6,7},{7,6},{8,9},{9,8},{10,11... | collective-permute-start | bytes 4816904 | tf_op jit(solution)/shard_map/ppermute | solution.py:370
  33.5 35.4 %copy-start.9 = (bf16[16,12544]{1,0:T(8,128)(2,1)}, bf16[16,12544]{1,0:T(8,128)(2,1)S(1)}, u32[]{:S(2)}) copy-start(bf16[16,12544]{1,0:T(8,128)(2,1)S(1)} %get-tuple-element.27) | copy-start | bytes 1204228
  33.5 35.4 %copy-start.10 = (bf16[16,12544]{1,0:T(8,128)(2,1)}, bf16[16,12544]{1,0:T(8,128)(2,1)S(1)}, u32[]{:S(2)}) copy-start(bf16[16,12544]{1,0:T(8,128)(2,1)S(1)} %get-tuple-element.26) | copy-start | bytes 1204228
  33.5 33.5 %collective-permute-start.1 = (bf16[32,12544]{1,0:T(8,128)(2,1)S(1)}, bf16[32,12544]{1,0:T(8,128)(2,1)S(1)}, u32[]{:S(2)}, u32[]{:S(2)}) collective-permute-start(bf16[32,12544]{1,0:T(8,128)(2,1)S(1)} %get-tuple-element.22), channel_id=1, source_target_pairs={{0,2},{1,3},{2,0},{3,1},{4,6},{5,7},{6,4},{7,5},{8,10},{9,11},{10,... | collective-permute-start | bytes 2408456 | tf_op jit(solution)/shard_map/ppermute | solution.py:370
  67.1 0.9 copy-start.2
  68.9 58.9 %collective-permute-start.2 = (bf16[32,12544]{1,0:T(8,128)(2,1)}, bf16[32,12544]{1,0:T(8,128)(2,1)}, u32[]{:S(2)}, u32[]{:S(2)}) collective-permute-start(bf16[32,12544]{1,0:T(8,128)(2,1)} %pad_maximum_fusion), channel_id=1, source_target_pairs={{0,4},{1,5},{2,6},{3,7},{4,0},{5,1},{6,2},{7,3},{8,12},{9,13},{10,... | collective-permute-start | bytes 2408456 | tf_op jit(solution)/shard_map/ppermute | solution.py:370
  69.0 28.1 %collective-permute-start.3 = (bf16[16,12544]{1,0:T(8,128)(2,1)}, bf16[16,12544]{1,0:T(8,128)(2,1)}, u32[]{:S(2)}, u32[]{:S(2)}) collective-permute-start(bf16[16,12544]{1,0:T(8,128)(2,1)} %get-tuple-element.24), channel_id=1, source_target_pairs={{0,8},{1,9},{2,10},{3,11},{4,12},{5,13},{6,14},{7,15},{8,0},{9,1},... | collective-permute-start | bytes 1204232 | tf_op jit(solution)/shard_map/ppermute | solution.py:370
  71.0 55.3 %collective-permute-start.4 = (bf16[16,12544]{1,0:T(8,128)(2,1)}, bf16[16,12544]{1,0:T(8,128)(2,1)}, u32[]{:S(2)}, u32[]{:S(2)}) collective-permute-start(bf16[16,12544]{1,0:T(8,128)(2,1)} %get-tuple-element.25), channel_id=1, source_target_pairs={{0,10},{1,11},{2,8},{3,9},{4,14},{5,15},{6,12},{7,13},{8,2},{9,3},... | collective-permute-start | bytes 1204232 | tf_op jit(solution)/shard_map/ppermute | solution.py:370
  73.8 3.1 %collective-permute-start.7 = (f32[96,128]{1,0:T(8,128)}, f32[96,128]{1,0:T(8,128)}, u32[]{:S(2)}, u32[]{:S(2)}) collective-permute-start(f32[96,128]{1,0:T(8,128)} %get-tuple-element.32), channel_id=1, source_target_pairs={{0,1},{1,0},{2,3},{3,2},{4,5},{5,4},{6,7},{7,6},{8,9},{9,8},{10,11... | collective-permute-start | bytes 147464 | tf_op jit(solution)/shard_map/ppermute | solution.py:370
  76.9 62.3 %collective-permute-start.5 = (bf16[16,12544]{1,0:T(8,128)(2,1)}, bf16[16,12544]{1,0:T(8,128)(2,1)}, u32[]{:S(2)}, u32[]{:S(2)}) collective-permute-start(bf16[16,12544]{1,0:T(8,128)(2,1)} %copy-done.10), channel_id=1, source_target_pairs={{0,12},{1,13},{2,14},{3,15},{4,8},{5,9},{6,10},{7,11},{8,4},{9,5},... | collective-permute-start | bytes 1204232 | tf_op jit(solution)/shard_map/ppermute | solution.py:370
  77.1 67.7 %collective-permute-start.6 = (bf16[16,12544]{1,0:T(8,128)(2,1)}, bf16[16,12544]{1,0:T(8,128)(2,1)}, u32[]{:S(2)}, u32[]{:S(2)}) collective-permute-start(bf16[16,12544]{1,0:T(8,128)(2,1)} %copy-done.9), channel_id=1, source_target_pairs={{0,14},{1,15},{2,12},{3,13},{4,10},{5,11},{6,8},{7,9},{8,6},{9,7},... | collective-permute-start | bytes 1204232 | tf_op jit(solution)/shard_map/ppermute | solution.py:370
  77.3 2.8 %copy-start.1 = (bf16[128,24576]{1,0:T(8,128)(2,1)S(1)}, bf16[128,24576]{1,0:T(8,128)(2,1)}, u32[]{:S(2)}) copy-start(bf16[128,24576]{1,0:T(8,128)(2,1)} %feat_hbm.3) | copy-start | bytes 18874372
  80.1 0.8 copy-start.6
  81.0 46.9 %copy-start.3 = (bf16[32,12544]{1,0:T(8,128)(2,1)S(1)}, bf16[32,12544]{1,0:T(8,128)(2,1)}, u32[]{:S(2)}) copy-start(bf16[32,12544]{1,0:T(8,128)(2,1)} %copy-done.2) | copy-start | bytes 2408452
  97.1 36.5 %collective-permute-start.10 = (f32[4,3,512]{2,1,0:T(4,128)S(1)}, f32[4,3,512]{2,1,0:T(4,128)S(1)}, u32[]{:S(2)}, u32[]{:S(2)}) collective-permute-start(f32[4,3,512]{2,1,0:T(4,128)S(1)} %get-tuple-element.36), channel_id=1, source_target_pairs={{0,2},{1,3},{2,0},{3,1},{4,6},{5,7},{6,4},{7,5},{8,10},{9,11},{10,... | collective-permute-start | bytes 73736 | tf_op jit(solution)/shard_map/ppermute | solution.py:384
  126.4 7.2 %collective-permute-start.11 = (f32[4,3,512]{2,1,0:T(4,128)S(1)}, f32[4,3,512]{2,1,0:T(4,128)S(1)}, u32[]{:S(2)}, u32[]{:S(2)}) collective-permute-start(f32[4,3,512]{2,1,0:T(4,128)S(1)} %get-tuple-element.35), channel_id=1, source_target_pairs={{0,3},{1,2},{2,1},{3,0},{4,7},{5,6},{6,5},{7,4},{8,11},{9,10},{10,... | collective-permute-start | bytes 73736 | tf_op jit(solution)/shard_map/ppermute | solution.py:384
  127.9 5.7 %collective-permute-start.9 = (f32[4,3,512]{2,1,0:T(4,128)S(1)}, f32[4,3,512]{2,1,0:T(4,128)S(1)}, u32[]{:S(2)}, u32[]{:S(2)}) collective-permute-start(f32[4,3,512]{2,1,0:T(4,128)S(1)} %get-tuple-element.34), channel_id=1, source_target_pairs={{0,1},{1,0},{2,3},{3,2},{4,5},{5,4},{6,7},{7,6},{8,9},{9,8},{10,11... | collective-permute-start | bytes 73736 | tf_op jit(solution)/shard_map/ppermute | solution.py:384
  133.6 14.4 %collective-permute-start.12 = (f32[1,3,512]{2,1,0:T(4,128)S(1)}, f32[1,3,512]{2,1,0:T(4,128)S(1)}, u32[]{:S(2)}, u32[]{:S(2)}) collective-permute-start(f32[1,3,512]{2,1,0:T(4,128)S(1)} %get-tuple-element.37), channel_id=1, source_target_pairs={{0,4},{1,5},{2,6},{3,7},{4,0},{5,1},{6,2},{7,3},{8,12},{9,13},{10,... | collective-permute-start | bytes 18440 | tf_op jit(solution)/shard_map/ppermute | solution.py:384
  137.9 10.1 %collective-permute-start.13 = (f32[1,3,512]{2,1,0:T(4,128)S(1)}, f32[1,3,512]{2,1,0:T(4,128)S(1)}, u32[]{:S(2)}, u32[]{:S(2)}) collective-permute-start(f32[1,3,512]{2,1,0:T(4,128)S(1)} %get-tuple-element.39), channel_id=1, source_target_pairs={{0,8},{1,9},{2,10},{3,11},{4,12},{5,13},{6,14},{7,15},{8,0},{9,1},... | collective-permute-start | bytes 18440 | tf_op jit(solution)/shard_map/ppermute | solution.py:384
  137.9 10.1 %collective-permute-start.14 = (f32[1,3,512]{2,1,0:T(4,128)S(1)}, f32[1,3,512]{2,1,0:T(4,128)S(1)}, u32[]{:S(2)}, u32[]{:S(2)}) collective-permute-start(f32[1,3,512]{2,1,0:T(4,128)S(1)} %get-tuple-element.38), channel_id=1, source_target_pairs={{0,12},{1,13},{2,14},{3,15},{4,8},{5,9},{6,10},{7,11},{8,4},{9,5},... | collective-permute-start | bytes 18440 | tf_op jit(solution)/shard_map/ppermute | solution.py:384
